TPU v7x, 128 devices: a whole 4x4x4 slice. The times are simulated.
128 devices in a mesh: hid: 16 (over x, z), wid: 8 (over y, core).
Axes of the slice: x: 4, y: 4, z: 4, core: 2. Of those that a mesh axis runs over, the one named last changes fastest.
Arguments:
- tokens: bfloat16 [1024, 8192], P(None, 'wid'), may hold values from -6 to 6
- gate_weight: bfloat16 [8192, 28672], P('wid', 'hid'), may hold values from -0.0625 to 0.0625
- up_weight: bfloat16 [8192, 28672], P('wid', 'hid'), may hold values from -0.0625 to 0.0625
- down_weight: bfloat16 [28672, 8192], P('hid', 'wid'), may hold values from -0.03125 to 0.03125
- adapter_id: int32 [1024, 1], replicated, may hold values from 0 to 255; in each aligned block of 1024 rows (0 to 1023, 1024 to 2047, ...) at most 8 rows name the same one
- owner_slot: int32 [256], replicated, may hold values from 0 to 255, each once
- adapt_down: bfloat16 [256, 28672, 64], P(('hid', 'wid')), may hold values from -0.03125 to 0.03125
- adapt_up: bfloat16 [256, 64, 8192], P(('hid', 'wid')), may hold values from -0.75 to 0.75
Outputs:
- mixed: bfloat16 [1024, 8192], P('hid', 'wid')
Inputs may be any that keep to these rules, and one draw needn't show every extreme that they name: `adapter_id`: every adapter is named by at least one row and by at most 8 rows; some adapter is named by exactly 8 rows. `owner_slot`: each slot is given to exactly one adapter.
All inputs are finite; a program needn't handle non-finite values.
Results may differ from a plain program's by a relative error of at most 0.006.
Values may be sent and summed in bfloat16 or wider, within the bound.
No kernel may reach another device: no remote copies, remote signals or barrier semaphores. Data moves between devices by JAX's collectives and lax.ppermute only.
A program may use at most 128 MiB of HBM per device.

v0:
```python
import jax
import jax.numpy as jnp
from jax import lax
from jax.sharding import PartitionSpec as P


def per_device(
    tokens, gate_weight, up_weight, down_weight, adapter_id, owner_slot, adapt_down, adapt_up
):
    hid_size = lax.axis_size("hid")
    wid_size = lax.axis_size("wid")
    hid_index = lax.axis_index("hid")
    wid_index = lax.axis_index("wid")
    row_count = tokens.shape[0]
    ff_local = gate_weight.shape[1]
    d_local = down_weight.shape[1]
    adapter_count = owner_slot.shape[0]
    per_dev = adapt_down.shape[0]
    capacity = 2 * row_count // adapter_count
    gate = jnp.dot(tokens, gate_weight, preferred_element_type=jnp.float32)
    up_value = jnp.dot(tokens, up_weight, preferred_element_type=jnp.float32)
    gate, up_value = lax.psum((gate, up_value), "wid")
    hidden = (jax.nn.silu(gate) * up_value).astype(jnp.bfloat16)
    row_adapter = adapter_id[:, 0]
    adapter_range = jnp.arange(adapter_count, dtype=jnp.int32)
    row_slot = jnp.sum(
        jnp.where(row_adapter[:, None] == adapter_range[None, :], owner_slot[None, :], 0), axis=1
    )
    positions = jnp.arange(row_count, dtype=jnp.int32)
    earlier = (row_adapter[:, None] == row_adapter[None, :]) & (
        positions[None, :] < positions[:, None]
    )
    row_rank = jnp.sum(earlier.astype(jnp.int32), axis=1)
    row_owner = row_slot // per_dev
    row_local = row_slot % per_dev
    owner_hid = row_owner // wid_size
    owner_wid = row_owner % wid_size
    send_index = jnp.where(
        owner_wid == wid_index, (owner_hid * per_dev + row_local) * capacity + row_rank, -1
    )
    send_slots = jnp.arange(hid_size * per_dev * capacity, dtype=jnp.int32)
    selector = (send_slots[:, None] == send_index[None, :]).astype(jnp.bfloat16)
    packed = jnp.dot(selector, hidden, preferred_element_type=jnp.float32).astype(jnp.bfloat16)
    packed = packed.reshape(hid_size, per_dev, capacity, ff_local)
    arrived = lax.all_to_all(packed, "hid", split_axis=0, concat_axis=3, tiled=True)
    arrived = arrived.reshape(per_dev, capacity, ff_local * hid_size)
    low_rank = jnp.einsum(
        "jcf,jfr->jcr", arrived, adapt_down, preferred_element_type=jnp.float32
    ).astype(jnp.bfloat16)
    adapted = jnp.einsum(
        "jcr,jrd->jcd", low_rank, adapt_up, preferred_element_type=jnp.float32
    ).astype(jnp.bfloat16)
    returned = lax.all_to_all(adapted, "wid", split_axis=2, concat_axis=0, tiled=True)
    returned = returned.reshape(wid_size * per_dev * capacity, d_local)
    landing_index = jnp.where(
        owner_hid == hid_index, (owner_wid * per_dev + row_local) * capacity + row_rank, -1
    )
    landing_slots = jnp.arange(wid_size * per_dev * capacity, dtype=jnp.int32)
    landing = (landing_index[:, None] == landing_slots[None, :]).astype(jnp.bfloat16)
    adapter_rows = jnp.dot(landing, returned, preferred_element_type=jnp.float32)
    result = jnp.dot(hidden, down_weight, preferred_element_type=jnp.float32)
    mixed = lax.psum_scatter(result, "hid", scatter_dimension=0, tiled=True)
    mixed = mixed + lax.psum_scatter(
        adapter_rows.astype(jnp.bfloat16), "hid", scatter_dimension=0, tiled=True
    ).astype(jnp.float32)
    return mixed.astype(jnp.bfloat16)


def solution(mesh):
    return jax.shard_map(
        per_device,
        mesh=mesh,
        in_specs=(
            P(None, "wid"),
            P("wid", "hid"),
            P("wid", "hid"),
            P("hid", "wid"),
            P(),
            P(),
            P(("hid", "wid"), None, None),
            P(("hid", "wid"), None, None),
        ),
        out_specs=P("hid", "wid"),
        check_vma=False,
    )
```

profile of v0, /device:TPU:0, one launch (start us, length us, event | category | flops | bytes accessed | tf_op | source)
XLA Modules:
  0.0 425.1 jit_solution(7071007205781436928)
XLA Ops:
  6.5 0.0 copy-start
  6.5 0.0 all-reduce.3.cloned.1.call-start
  6.5 1.6 copy-done
  8.1 0.0 copy-start.5
  8.1 8.1 %fusion.8 = f32[1024,1792]{1,0:T(8,128)} fusion(bf16[1024,1024]{1,0:T(8,128)(2,1)S(1)} %copy-done, bf16[1024,1792]{1,0:T(8,128)(2,1)} %param.10), kind=kOutput, calls=%fused_computation.34 | convolution fusion | flops 3758096384 | bytes 13107200 | tf_op jit(solution)/shard_map/dot_general | solution.py:21
  16.3 0.0 copy-done.5
  16.3 5.9 %fusion.7 = f32[1024,1792]{1,0:T(8,128)} fusion(bf16[1024,1024]{1,0:T(8,128)(2,1)S(1)} %copy-done, bf16[1024,1792]{1,0:T(8,128)(2,1)S(1)} %copy-done.5), kind=kOutput, calls=%fused_computation.33 | convolution fusion | flops 3758096384 | bytes 13107200 | tf_op jit(solution)/shard_map/dot_general | solution.py:20
  22.2 0.0 copy-start.3
  22.2 0.0 copy-start.4
  22.2 0.0 all-reduce.3.cloned.1.call-update
  22.2 0.0 reduce-scatter.5.cloned.1.call-start
  22.3 0.6 copy-done.3
  22.9 0.0 copy-done.4
  22.9 0.4 select_reduce_fusion
  23.3 0.5 convert_reduce_fusion
  23.8 164.8 %all-reduce.3.cloned.1.call-done = (f32[1024,1792]{1,0:T(8,128)}, f32[1024,1792]{1,0:T(8,128)}) async-done(((f32[1024,1792]{1,0:T(8,128)}, f32[1024,1792]{1,0:T(8,128)}), (f32[1024,1792]{1,0:T(8,128)}, f32[1024,1792]{1,0:T(8,128)})) %all-reduce.3.cloned.1.call-update) | async-done | bytes 14680080 | tf_op jit(solution)/shard_map/psum | solution.py:22
  188.6 6.3 %multiply_convert_fusion = bf16[1024,1792]{1,0:T(8,128)(2,1)S(1)} fusion(f32[1024,1792]{1,0:T(8,128)} %get-tuple-element.5, f32[1024,1792]{1,0:T(8,128)} %get-tuple-element.6), kind=kLoop, calls=%fused_computation.1 | loop fusion | flops 11010048 | bytes 18350080 | tf_op jit(solution)/shard_map/convert_element_type | solution.py:23
  194.9 0.0 copy-start.2
  194.9 1.2 convolution_convert_fusion.1
  196.1 21.9 %all_to_all.30 = bf16[16,2,8,1792]{3,2,1,0:T(8,128)(2,1)S(1)} all-to-all(bf16[16,2,8,1792]{3,2,1,0:T(8,128)(2,1)S(1)} %bitcast.29), channel_id=1, replica_groups=mesh['hid'=16,'wid'=8] {'hid'}, dimensions={0} | all-to-all | bytes 1835008 | tf_op jit(solution)/shard_map/all_to_all | solution.py:45
  218.0 0.0 copy-done.2
  218.0 0.3 copy.17
  218.3 0.4 reshape.138
  218.7 6.1 %convolution_convert_fusion = bf16[2,8,8192]{2,1,0:T(8,128)(2,1)S(1)} fusion(bf16[2,64,8192]{2,1,0:T(8,128)(2,1)} %param.15, bf16[2,8,28672]{2,1,0:T(8,128)(2,1)S(1)} %reshape.138, bf16[2,28672,64]{1,2,0:T(8,128)(2,1)} %param.14), kind=kOutput, calls=%fused_computation | convolution fusion | flops 75629568 | bytes 10616832 | tf_op jit(solution)/shard_map/jcr,jrd->jcd/dot_general | solution.py:50
  224.8 6.8 %copy.18 = bf16[2,8,8192]{1,0,2:T(2,128)(2,1)} copy(bf16[2,8,8192]{2,1,0:T(8,128)(2,1)S(1)} %convolution_convert_fusion) | data formatting | bytes 524288 | tf_op jit(solution)/shard_map/convert_element_type | solution.py:52
  231.5 5.8 %reshape.140 = bf16[8,2,8192]{2,1,0:T(2,128)(2,1)S(1)} reshape(bf16[8192,2,8]{2,1,0:T(2,128)(2,1)} %bitcast.25) | data formatting | bytes 524288
  237.3 11.3 %all_to_all.31 = bf16[8,2,8192]{2,1,0:T(2,128)(2,1)S(1)} all-to-all(bf16[8,2,8192]{2,1,0:T(2,128)(2,1)S(1)} %reshape.140), channel_id=1, replica_groups=mesh['hid'=16,'wid'=8] {'wid'}, dimensions={0} | all-to-all | bytes 524288 | tf_op jit(solution)/shard_map/all_to_all | solution.py:53
  248.6 5.9 %reshape.141 = bf16[8192,2,8]{2,1,0:T(2,128)(2,1)} reshape(bf16[8,2,8192]{2,1,0:T(2,128)(2,1)S(1)} %all_to_all.31) | data formatting | bytes 524288
  254.5 8.9 %copy.22 = bf16[2,8,8,1024]{3,1,0,2:T(8,128)(2,1)S(1)} copy(bf16[2,8,8,1024]{1,0,3,2:T(2,128)(2,1)} %bitcast.26) | data formatting | bytes 524288 | tf_op jit(solution)/shard_map/all_to_all | solution.py:53
  263.4 2.2 convolution_convert_fusion.2
  265.6 0.0 reduce-scatter.5.cloned.1.call-update
  265.6 0.0 reduce-scatter.3.cloned.1.call-start
  265.7 0.0 copy-start.1
  265.7 9.2 %fusion.9 = f32[1024,1024]{1,0:T(8,128)} fusion(bf16[1024,1792]{1,0:T(8,128)(2,1)} %copy-done.2, bf16[1792,1024]{1,0:T(8,128)(2,1)} %param.11), kind=kOutput, calls=%fused_computation.35 | convolution fusion | flops 3758096384 | bytes 11534336 | tf_op jit(solution)/shard_map/dot_general | solution.py:61
  274.9 0.0 reduce-scatter.3.cloned.1.call-update
  274.9 61.3 %reduce-scatter.5.cloned.1.call-done = bf16[64,1024]{1,0:T(8,128)(2,1)} async-done(((bf16[1024,1024]{1,0:T(8,128)(2,1)}), bf16[64,1024]{1,0:T(8,128)(2,1)}) %reduce-scatter.5.cloned.1.call-update) | async-done | bytes 131088 | tf_op jit(solution)/shard_map/reduce_scatter | solution.py:63
  336.2 80.7 %reduce-scatter.3.cloned.1.call-done = f32[64,1024]{1,0:T(8,128)} async-done(((f32[1024,1024]{1,0:T(8,128)}), f32[64,1024]{1,0:T(8,128)}) %reduce-scatter.3.cloned.1.call-update) | async-done | bytes 262160 | tf_op jit(solution)/shard_map/reduce_scatter | solution.py:62
  416.9 1.7 add_convert_fusion
  418.6 0.0 copy-done.1
  (1 shorter events, 0.0 us)
Async XLA Ops:
  6.5 1.6 copy-start
  6.5 182.1 %all-reduce.3.cloned.1.call-start = ((), (), s32[]{:S(2)}) async-start(), calls=%async_computation.6 | async-start | bytes 29360128 | tf_op jit(solution)/shard_map/psum | solution.py:22
  8.1 8.2 %copy-start.5 = (bf16[1024,1792]{1,0:T(8,128)(2,1)S(1)}, bf16[1024,1792]{1,0:T(8,128)(2,1)}, u32[]{:S(2)}) copy-start(bf16[1024,1792]{1,0:T(8,128)(2,1)} %param.9) | copy-start | bytes 11010052
  22.2 0.7 copy-start.3
  22.2 0.7 copy-start.4
  22.2 314.0 %reduce-scatter.5.cloned.1.call-start = ((), (), s32[]{:S(2)}) async-start(), calls=%async_computation.5 | async-start | bytes 2228224 | tf_op jit(solution)/shard_map/reduce_scatter | solution.py:63
  194.9 23.1 %copy-start.2 = (bf16[1024,1792]{1,0:T(8,128)(2,1)}, bf16[1024,1792]{1,0:T(8,128)(2,1)S(1)}, u32[]{:S(2)}) copy-start(bf16[1024,1792]{1,0:T(8,128)(2,1)S(1)} %multiply_convert_fusion) | copy-start | bytes 11010052
  265.6 151.3 %reduce-scatter.3.cloned.1.call-start = ((), (), s32[]{:S(2)}) async-start(), calls=%async_computation.4 | async-start | bytes 4456448 | tf_op jit(solution)/shard_map/reduce_scatter | solution.py:62
  265.7 152.9 %copy-start.1 = (bf16[1024,1024]{1,0:T(8,128)(2,1)S(1)}, bf16[1024,1024]{1,0:T(8,128)(2,1)}, u32[]{:S(2)}) copy-start(bf16[1024,1024]{1,0:T(8,128)(2,1)} %param.8) | copy-start | bytes 6291460
Sparse Core Ops, SparseCore 0:
  22.4 166.1 all-reduce.2
  265.7 70.4 reduce-scatter.4
  339.9 76.9 reduce-scatter.2
where the time goes:
time: 426 us; the launch traced here: 425 us
  waiting for transfers between devices  307 us (72%)
  blocking collectives  33.2 us (8%)
  matrix products  32.7 us (8%)
  local copies, waits for them, and re-layouts  30.2 us (7%)
  between operations  13.2 us (3%)
  other arithmetic  8.87 us (2%)
    psum x1, waiting for transfers between devices, per_device(): gate, up_value = lax.psum((gate, up_value), 'wid')  165 us
    reduce_scatter x1, waiting for transfers between devices, per_device(): mixed = lax.psum_scatter(result, 'hid', scatter_dimension=0, tiled=True)  80.7 us
    reduce_scatter x1, waiting for transfers between devices, per_device(): lax.psum_scatter(adapter_rows.astype(jnp.bfloat16), 'hid', scatter_dimens...  61.3 us
    all_to_all x1, blocking collectives, per_device(): lax.all_to_all(packed, 'hid', split_axis=0, concat_axis=3, tiled=True)  21.9 us
    unnamed x14, local copies, waits for them, and re-layouts  13.9 us
    all_to_all x1, blocking collectives, per_device(): lax.all_to_all(adapted, 'wid', split_axis=2, concat_axis=0, tiled=True)  11.3 us
    dot_general x1, matrix products, per_device(): result = jnp.dot(hidden, down_weight, preferred_element_type=jnp.float32)  9.18 us
    all_to_all x1, local copies, waits for them, and re-layouts, per_device(): lax.all_to_all(adapted, 'wid', split_axis=2, concat_axis=0, tiled=True)  8.88 us
  transfers between devices with their start and end apart: 3, of which 3 were waited for; matrix products, arithmetic and copies ran while one was open for 2% of the time, Pallas kernels for 0%

commit v1 on v0

v1 whole, which is shorter than its diff:
```python
import jax
import jax.numpy as jnp
from jax import lax
from jax.sharding import Mesh, PartitionSpec as P

BF = jnp.bfloat16
F32 = jnp.float32
CHUNKS = (1024, 768)
ORDER = (0, 1, 3, 2)
STREAMS = (((0, 1, 2, 3), (2, 3, 0, 1)), ((1, 0, 3, 2), (3, 2, 1, 0)))


def gray(v):
    return v ^ (v >> 1)


def flip_a(v):
    return v ^ 1


def flip_b(v):
    return 3 - v


def hid_perm(dims):
    pairs = []
    for x in range(4):
        for z in range(4):
            for k in range(2):
                move = flip_b if dims[k] % 2 == 0 else flip_a
                to = (move(x), z) if dims[k] < 2 else (x, move(z))
                pairs.append(((x * 4 + z) * 2 + k, (to[0] * 4 + to[1]) * 2 + k))
    return pairs


def part(array, index, rows):
    return lax.dynamic_slice_in_dim(array, index * rows, rows, 0)


def join(bit, mine, other):
    return jnp.where(
        bit == 0, jnp.concatenate([mine, other], 0), jnp.concatenate([other, mine], 0)
    )


def per_device(
    tokens, gate_weight, up_weight, down_weight, adapter_id, owner_slot, adapt_down, adapt_up
):
    x, z, y, c = (lax.axis_index(n) for n in ("x", "z", "y", "c"))
    row_count = tokens.shape[0]
    ff_local = gate_weight.shape[1]
    d_local = down_weight.shape[1]
    adapter_count = owner_slot.shape[0]
    per_dev = adapt_down.shape[0]
    capacity = 2 * row_count // adapter_count
    wid_axes, hid_axes = ("y", "c"), ("x", "z")
    wid_index, hid_index = y * 2 + c, x * 4 + z
    block = row_count // 16

    gray_y = gray(y)
    low_y, high_y = gray_y & 1, gray_y >> 1
    keep1 = jnp.where(c == 0, low_y, high_y)
    keep2 = jnp.where(c == 0, high_y, low_y)
    swap_perm = [(i, i ^ 1) for i in range(8)]
    first = (flip_a, flip_b)
    perm1 = [(v * 2 + k, first[k](v) * 2 + k) for v in range(4) for k in range(2)]
    perm2 = [(v * 2 + k, first[1 - k](v) * 2 + k) for v in range(4) for k in range(2)]

    blocks = [(ORDER[i], ORDER[j]) for i in range(4) for j in range(4)]
    order = [bx * 4 + bz for bx, bz in blocks]
    permuted = jnp.concatenate([tokens[b * block : (b + 1) * block] for b in order], 0)
    row_id = (
        jnp.asarray(order, jnp.int32)[:, None] * block + jnp.arange(block, dtype=jnp.int32)
    ).reshape(-1)

    half = row_count // 2
    away = part(permuted, 1 - c, half)
    home = part(permuted, c, half)

    row_adapter = adapter_id[:, 0]
    adapter_range = jnp.arange(adapter_count, dtype=jnp.int32)
    row_slot = jnp.sum(
        jnp.where(row_adapter[:, None] == adapter_range[None, :], owner_slot[None, :], 0), axis=1
    )
    positions = jnp.arange(row_count, dtype=jnp.int32)
    earlier = (row_adapter[:, None] == row_adapter[None, :]) & (
        positions[None, :] < positions[:, None]
    )
    row_rank = jnp.sum(earlier.astype(jnp.int32), axis=1)

    def regroup(v):
        return jnp.concatenate([v[b * block : (b + 1) * block] for b in order], 0)

    row_slot, row_rank = regroup(row_slot), regroup(row_rank)
    row_owner = row_slot // per_dev
    row_local = row_slot % per_dev
    owner_hid = row_owner // 8
    owner_wid = row_owner % 8
    send_index = jnp.where(
        owner_wid == wid_index, (owner_hid * per_dev + row_local) * capacity + row_rank, -1
    )
    send_slots = jnp.arange(16 * per_dev * capacity, dtype=jnp.int32)
    selector = (send_slots[:, None] == send_index[None, :]).astype(BF)
    landing_index = jnp.where(
        owner_hid == hid_index, (owner_wid * per_dev + row_local) * capacity + row_rank, -1
    )
    landing_slots = jnp.arange(8 * per_dev * capacity, dtype=jnp.int32)
    landing = (landing_index[:, None] == landing_slots[None, :]).astype(BF)

    def dot(a, b):
        return jnp.dot(a, b, preferred_element_type=F32)

    low_rank = 0.0
    result = 0.0
    down_by_hid = adapt_down.reshape(per_dev, 16, ff_local, adapt_down.shape[2])
    offset = 0
    for width in CHUNKS:
        columns = slice(offset, offset + width)
        offset += width
        gw, uw = gate_weight[:, columns], up_weight[:, columns]
        far = [lax.ppermute(dot(away, w).astype(BF), wid_axes, swap_perm) for w in (gw, uw)]
        near = [dot(home, w) for w in (gw, uw)]
        sums = jnp.stack([n + f.astype(F32) for n, f in zip(near, far)], 1)
        for perm, keep, rows in ((perm1, keep1, half // 2), (perm2, keep2, half // 4)):
            arrived = lax.ppermute(part(sums, 1 - keep, rows).astype(BF), wid_axes, perm)
            sums = part(sums, keep, rows) + arrived.astype(F32)
        hidden = (jax.nn.silu(sums[:, 0]) * sums[:, 1]).astype(BF)
        hidden = join(keep2, hidden, lax.ppermute(hidden, wid_axes, perm2))
        hidden = join(keep1, hidden, lax.ppermute(hidden, wid_axes, perm1))
        hidden = join(c, hidden, lax.ppermute(hidden, wid_axes, swap_perm))
        packed = dot(selector, hidden).astype(BF).reshape(16, per_dev, capacity, width)
        arrived = lax.all_to_all(packed, hid_axes, split_axis=0, concat_axis=0, tiled=True)
        low_rank = low_rank + jnp.einsum(
            "hjcf,jhfr->jcr", arrived, down_by_hid[:, :, columns], preferred_element_type=F32
        )
        result = result + dot(hidden, down_weight[columns])
    adapted = jnp.einsum(
        "jcr,jrd->jcd", low_rank.astype(BF), adapt_up, preferred_element_type=F32
    ).astype(BF)
    slots = per_dev * capacity
    adapted = adapted.reshape(slots, 8, d_local).transpose(1, 0, 2)
    returned = lax.all_to_all(adapted, wid_axes, split_axis=0, concat_axis=0, tiled=True)
    result = result + dot(landing, returned.reshape(8 * slots, d_local))

    gray_x, gray_z = gray(x), gray(z)
    bits = (gray_x >> 1, gray_x & 1, gray_z >> 1, gray_z & 1)
    width = d_local // 2
    outs = []
    for stream, dims in enumerate(STREAMS):
        value = result[:, stream * width : (stream + 1) * width].reshape(16, block, width)
        left = [[0, 1, 2, 3], [0, 1, 2, 3]]
        for step in range(4):
            at = [left[k].index(dims[k][step]) for k in range(2)]
            bit = jnp.where(c == 0, bits[dims[0][step]], bits[dims[1][step]])
            count = value.shape[0]

            def pick(value, bit):
                both = []
                for k in range(2):
                    shaped = value.reshape(2 ** at[k], 2, -1, block, width)
                    taken = lax.dynamic_index_in_dim(shaped, bit, 1, keepdims=False)
                    both.append(taken.reshape(count // 2, block, width))
                return both[0] if at[0] == at[1] else jnp.where(c == 0, both[0], both[1])

            sent = pick(value, 1 - bit).astype(BF)
            arrived = lax.ppermute(sent, ("x", "z", "c"), hid_perm([dims[k][step] for k in range(2)]))
            value = pick(value, bit) + arrived.astype(F32)
            for k in range(2):
                left[k].remove(dims[k][step])
        outs.append(value[0])
    return jnp.concatenate(outs, 1).astype(BF)


def solution(mesh):
    fine = Mesh(mesh.devices.reshape(4, 4, 4, 2), ("x", "z", "y", "c"))
    hid, wid = ("x", "z"), ("y", "c")
    return jax.shard_map(
        per_device,
        mesh=fine,
        in_specs=(
            P(None, wid),
            P(wid, hid),
            P(wid, hid),
            P(hid, wid),
            P(),
            P(),
            P(hid + wid, None, None),
            P(hid + wid, None, None),
        ),
        out_specs=P(hid, wid),
        check_vma=False,
    )
```

time: 426 us -> 204 us (0.48)
  waiting for transfers between devices: 307 us -> 53 us
  starting transfers between devices: 0.09 us -> 44.9 us
  blocking collectives: 33.2 us -> 0 us
  matrix products: 32.7 us -> 57.2 us
  between operations: 13.2 us -> 0.49 us
  local copies, waits for them, and re-layouts: 30.2 us -> 35.4 us
    psum x1 -> x0, waiting for transfers between devices: 165 us -> none  [per_device(): gate, up_value = lax.psum((gate, up_value), 'wid')]
    reduce_scatter x2 -> x0, waiting for transfers between devices: 142 us -> none  [the longest x1 80.7 us: per_device(): mixed = lax.psum_scatter(result, 'hid', scatter_dimension=0, tiled=True)]
    ppermute x0 -> x22, waiting for transfers between devices: none -> 42.8 us  [the longest x8 16.3 us: per_device(): lax.ppermute(sent, ('x', 'z', 'c'), hid_perm([dims[k][step] for k in rang...]
    all_to_all x2 -> x0, blocking collectives: 33.2 us -> none  [the longest x1 21.9 us: per_device(): lax.all_to_all(packed, 'hid', split_axis=0, concat_axis=3, tiled=True)]
    ppermute x0 -> x22, starting transfers between devices: none -> 28.8 us  [the longest x8 13.7 us: per_device(): lax.ppermute(sent, ('x', 'z', 'c'), hid_perm([dims[k][step] for k in rang...]
    dot_general x6 -> x15, matrix products: 32.7 us -> 57.2 us  [the longest x13 47.1 us: dot(): return jnp.dot(a, b, preferred_element_type=F32)]
    all_to_all x0 -> x3, starting transfers between devices: none -> 16.1 us  [the longest x2 11.7 us: per_device(): lax.all_to_all(packed, hid_axes, split_axis=0, concat_axis=0, tiled=True)]
    unnamed x14 -> x41, local copies, waits for them, and re-layouts: 13.9 us -> 26.3 us
  transfers between devices with their start and end apart: 3 -> 25, of which waited for: 3 -> 14; matrix products, arithmetic and copies ran while one was open for 2% -> 32% of each run, Pallas kernels for 0% -> 0%
where the time goes in v1:
time: 204 us; the launch traced here: 202 us
  matrix products  57.2 us (28%)
  waiting for transfers between devices  53 us (26%)
  starting transfers between devices  44.9 us (22%)
  local copies, waits for them, and re-layouts  35.4 us (17%)
  other arithmetic  11.5 us (6%)
    dot_general x13, matrix products, dot(): return jnp.dot(a, b, preferred_element_type=F32)  47.1 us
    unnamed x41, local copies, waits for them, and re-layouts  26.3 us
    ppermute x8, waiting for transfers between devices, per_device(): lax.ppermute(sent, ('x', 'z', 'c'), hid_perm([dims[k][step] for k in rang...  16.3 us
    ppermute x8, starting transfers between devices, per_device(): lax.ppermute(sent, ('x', 'z', 'c'), hid_perm([dims[k][step] for k in rang...  13.7 us
    ppermute x4, waiting for transfers between devices, per_device(): lax.ppermute(part(sums, 1 - keep, rows).astype(BF), wid_axes, perm)  13.1 us
    all_to_all x2, starting transfers between devices, per_device(): lax.all_to_all(packed, hid_axes, split_axis=0, concat_axis=0, tiled=True)  11.7 us
    all_to_all x2, waiting for transfers between devices, per_device(): lax.all_to_all(packed, hid_axes, split_axis=0, concat_axis=0, tiled=True)  8.82 us
    ppermute x4, starting transfers between devices, per_device(): lax.ppermute(part(sums, 1 - keep, rows).astype(BF), wid_axes, perm)  8.2 us
  transfers between devices with their start and end apart: 25, of which 14 were waited for; matrix products, arithmetic and copies ran while one was open for 32% of the time, Pallas kernels for 0%

profile of v1, /device:TPU:0, one launch (start us, length us, event | category | flops | bytes accessed | tf_op | source)
XLA Modules:
  0.0 202.4 jit_solution(3988698958746652259)
XLA Ops:
  0.0 1.8 slice_dynamic-update-slice_fusion.3
  1.8 1.6 slice_dynamic-update-slice_fusion.11
  3.4 1.6 slice_dynamic-update-slice_fusion.10
  5.0 1.7 slice_dynamic-update-slice_fusion.2
  6.6 1.6 slice_dynamic-update-slice_fusion.9
  8.2 1.6 slice_dynamic-update-slice_fusion.8
  9.8 1.7 slice_dynamic-update-slice_fusion.1
  11.5 1.6 slice_dynamic-update-slice_fusion.7
  13.1 1.6 slice_dynamic-update-slice_fusion.6
  14.6 1.7 slice_dynamic-update-slice_fusion
  16.3 1.6 slice_dynamic-update-slice_fusion.5
  17.9 1.6 slice_dynamic-update-slice_fusion.4
  19.4 4.3 %fusion.31 = bf16[512,1024]{1,0:T(8,128)(2,1)} fusion(bf16[1024,1792]{1,0:T(8,128)(2,1)} %param.9, bf16[1024,1024]{1,0:T(8,128)(2,1)} %slice_dynamic-update-slice_fusion.4, s32[]{:T(128)S(6)} %select_n.259), kind=kOutput, calls=%fused_computation.43 | convolution fusion | flops 1074266112 | bytes 4194308 | tf_op jit(solution)/shard_map/dot_general | solution.py:111
  23.8 3.5 %fusion.34 = bf16[512,1024]{1,0:T(8,128)(2,1)} fusion(bf16[1024,1792]{1,0:T(8,128)(2,1)S(1)} %copy-done.12, bf16[1024,1024]{1,0:T(8,128)(2,1)} %slice_dynamic-update-slice_fusion.4, s32[]{:T(128)S(6)} %select_n.259), kind=kOutput, calls=%fused_computation.44 | convolution fusion | flops 1074266112 | bytes 4194308 | tf_op jit(solution)/shard_map/dot_general | solution.py:111
  27.8 3.6 %convolution_convert_fusion.2 = bf16[512,768]{1,0:T(8,128)(2,1)} fusion(bf16[1024,1792]{1,0:T(8,128)(2,1)} %param.9, bf16[1024,1024]{1,0:T(8,128)(2,1)} %slice_dynamic-update-slice_fusion.4, s32[]{:T(128)S(6)} %select_n.259), kind=kOutput, calls=%fused_computation.46 | convolution fusion | flops 805699584 | bytes 3407876 | tf_op jit(solution)/shard_map/dot_general | solution.py:111
  31.3 3.1 %convolution_convert_fusion.1 = bf16[512,768]{1,0:T(8,128)(2,1)} fusion(bf16[1024,1792]{1,0:T(8,128)(2,1)S(1)} %copy-done.12, bf16[1024,1024]{1,0:T(8,128)(2,1)} %slice_dynamic-update-slice_fusion.4, s32[]{:T(128)S(6)} %select_n.259), kind=kOutput, calls=%fused_computation.45 | convolution fusion | flops 805699584 | bytes 3407876 | tf_op jit(solution)/shard_map/dot_general | solution.py:111
  35.0 3.6 %add_bitcast_fusion.1 = f32[512,1,1024]{2,0,1:T(8,128)S(1)} fusion(bf16[512,1024]{1,0:T(8,128)(2,1)} %collective-permute-done, bf16[1024,1792]{1,0:T(8,128)(2,1)} %param.9, bf16[1024,1024]{1,0:T(8,128)(2,1)} %slice_dynamic-update-slice_fusion.4, s32[]{:T(128)S(6)} %select_n.258), kind=kOutput, calls=%fused_computation.25 | convolution fusion | flops 1074790400 | bytes 6291460 | tf_op jit(solution)/shard_map/dot_general | solution.py:111
  38.6 3.2 %add_bitcast_fusion = f32[512,1,1024]{2,0,1:T(8,128)S(1)} fusion(bf16[512,1024]{1,0:T(8,128)(2,1)S(1)} %collective-permute-done.1, bf16[1024,1792]{1,0:T(8,128)(2,1)S(1)} %copy-done.13, bf16[1024,1024]{1,0:T(8,128)(2,1)} %slice_dynamic-update-slice_fusion.4, s32[]{:T(128)S(6)} %select_n.258), kind=kOutput, calls=%fused_computation.24 | convolution fusion | flops 1074790400 | bytes 6291460 | tf_op jit(solution)/shard_map/dot_general | solution.py:111
  42.0 1.2 copy-done.2
  43.2 1.7 collective-permute-start.2
  44.8 2.9 %add_bitcast_fusion.3 = f32[512,1,768]{2,0,1:T(8,128)S(1)} fusion(bf16[512,768]{1,0:T(8,128)(2,1)} %collective-permute-done.7, bf16[1024,1792]{1,0:T(8,128)(2,1)} %param.9, bf16[1024,1024]{1,0:T(8,128)(2,1)} %slice_dynamic-update-slice_fusion.4, s32[]{:T(128)S(6)} %select_n.258), kind=kOutput, calls=%fused_computation.42 | convolution fusion | flops 806092800 | bytes 4980740 | tf_op jit(solution)/shard_map/dot_general | solution.py:111
  47.8 3.0 %add_bitcast_fusion.2 = f32[512,1,768]{2,0,1:T(8,128)S(1)} fusion(bf16[512,768]{1,0:T(8,128)(2,1)} %collective-permute-done.8, bf16[1024,1792]{1,0:T(8,128)(2,1)S(1)} %copy-done.13, bf16[1024,1024]{1,0:T(8,128)(2,1)} %slice_dynamic-update-slice_fusion.4, s32[]{:T(128)S(6)} %select_n.258), kind=kOutput, calls=%fused_computation.41 | convolution fusion | flops 806092800 | bytes 4980740 | tf_op jit(solution)/shard_map/dot_general | solution.py:111
  52.6 5.4 %collective-permute-done.2 = bf16[256,2,1024]{2,0,1:T(8,128)(2,1)} collective-permute-done((bf16[256,2,1024]{2,0,1:T(8,128)(2,1)S(1)}, bf16[256,2,1024]{2,0,1:T(8,128)(2,1)}, u32[]{:S(2)}, u32[]{:S(2)}) %collective-permute-start.2) | collective-permute-done | bytes 1048608 | tf_op jit(solution)/shard_map/ppermute | solution.py:125
  58.1 2.2 %fusion.8 = f32[256,2,1024]{2,0,1:T(8,128)S(1)} fusion(s32[]{:T(128)S(6)} %select_n.260, f32[512,1,1024]{2,0,1:T(8,128)} %copy-done.1, f32[512,1,1024]{2,0,1:T(8,128)} %copy-done.2, bf16[256,2,1024]{2,0,1:T(8,128)(2,1)} %collective-permute-done.2), kind=kLoop, calls=%fused_computation.20 | loop fusion | flops 1572864 | bytes 7340036 | tf_op jit(solution)/shard_map/add | solution.py:126
  60.2 1.4 copy-done.3
  61.7 3.2 %collective-permute-start.3 = (bf16[128,2,1024]{2,0,1:T(8,128)(2,1)S(1)}, bf16[128,2,1024]{2,0,1:T(8,128)(2,1)S(1)}, u32[]{:S(2)}, u32[]{:S(2)}) collective-permute-start(bf16[128,2,1024]{2,0,1:T(8,128)(2,1)S(1)} %dynamic-slice_convert_fusion), channel_id=1, source_target_pairs={{0,6},{1,3},{2,4},{3,1},{4,2},{5,7},{6,0},{7,5},{8,14},{9,11},{10,... | collective-permute-start | bytes 1572872 | tf_op jit(solution)/shard_map/ppermute | solution.py:125
  64.9 3.6 %collective-permute-done.9 = bf16[256,2,768]{2,0,1:T(8,128)(2,1)} collective-permute-done((bf16[256,2,768]{2,0,1:T(8,128)(2,1)}, bf16[256,2,768]{2,0,1:T(8,128)(2,1)}, u32[]{:S(2)}, u32[]{:S(2)}) %collective-permute-start.9) | collective-permute-done | bytes 786464 | tf_op jit(solution)/shard_map/ppermute | solution.py:125
  68.5 1.8 fusion.24
  71.1 3.0 %collective-permute-start.10 = (bf16[128,2,768]{2,0,1:T(8,128)(2,1)}, bf16[128,2,768]{2,0,1:T(8,128)(2,1)S(1)}, u32[]{:S(2)}, u32[]{:S(2)}) collective-permute-start(bf16[128,2,768]{2,0,1:T(8,128)(2,1)} %dynamic-slice_convert_fusion.1), channel_id=1, source_target_pairs={{0,6},{1,3},{2,4},{3,1},{4,2},{5,7},{6,0},{7,5},{8,14},{9,11},{10,... | collective-permute-start | bytes 1179656 | tf_op jit(solution)/shard_map/ppermute | solution.py:125
  74.5 1.3 collective-permute-start.4
  76.3 4.0 %collective-permute-done.10 = bf16[128,2,768]{2,0,1:T(8,128)(2,1)S(1)} collective-permute-done((bf16[128,2,768]{2,0,1:T(8,128)(2,1)}, bf16[128,2,768]{2,0,1:T(8,128)(2,1)S(1)}, u32[]{:S(2)}, u32[]{:S(2)}) %collective-permute-start.10) | collective-permute-done | bytes 393248 | tf_op jit(solution)/shard_map/ppermute | solution.py:125
  80.3 1.2 convert_add_fusion.1
  81.5 1.6 collective-permute-done.4
  83.3 2.1 %collective-permute-start.5 = (bf16[256,1024]{1,0:T(8,128)(2,1)S(1)}, bf16[256,1024]{1,0:T(8,128)(2,1)S(1)}, u32[]{:S(2)}, u32[]{:S(2)}) collective-permute-start(bf16[256,1024]{1,0:T(8,128)(2,1)S(1)} %maximum_select_fusion.4), channel_id=1, source_target_pairs={{0,2},{1,7},{2,0},{3,5},{4,6},{5,3},{6,4},{7,1},{8,10},{9,15},{10,... | collective-permute-start | bytes 1572872 | tf_op jit(solution)/shard_map/ppermute | solution.py:129
  85.5 1.3 collective-permute-start.11
  86.9 6.0 %collective-permute-done.11 = bf16[128,768]{1,0:T(8,128)(2,1)S(1)} collective-permute-done((bf16[128,768]{1,0:T(8,128)(2,1)S(1)}, bf16[128,768]{1,0:T(8,128)(2,1)S(1)}, u32[]{:S(2)}, u32[]{:S(2)}) %collective-permute-start.11) | collective-permute-done | bytes 196640 | tf_op jit(solution)/shard_map/ppermute | solution.py:128
  95.2 5.7 %collective-permute-done.12 = bf16[256,768]{1,0:T(8,128)(2,1)S(1)} collective-permute-done((bf16[256,768]{1,0:T(8,128)(2,1)S(1)}, bf16[256,768]{1,0:T(8,128)(2,1)S(1)}, u32[]{:S(2)}, u32[]{:S(2)}) %collective-permute-start.12) | collective-permute-done | bytes 393248 | tf_op jit(solution)/shard_map/ppermute | solution.py:129
  100.9 1.2 maximum_select_fusion.3
  102.3 3.4 %convolution_convert_fusion.3 = bf16[256,1024]{1,0:T(8,128)(2,1)} fusion(s32[1024]{0:T(1024)S(1)} %get-tuple-element.8, bf16[512,1024]{1,0:T(8,128)(2,1)} %collective-permute-done.6, bf16[512,1024]{1,0:T(8,128)(2,1)S(1)} %maximum_select_fusion.2, pred[]{:T(512)S(6)} %eq.51), kind=kOutput, calls=%fused_computation.53 | convolution fusion | flops 546832384 | bytes 2625537 | tf_op jit(solution)/shard_map/dot_general | solution.py:111
  105.7 7.9 %all-to-all-start = ((bf16[16,2,8,1024]{3,2,1,0:T(8,128)(2,1)}), bf16[16,2,8,1024]{3,2,1,0:T(8,128)(2,1)S(1)}, u32[]{:S(2)}, u32[]{:S(2)}) async-start(bf16[16,2,8,1024]{3,2,1,0:T(8,128)(2,1)} %bitcast.154), calls=%async_computation | async-start | bytes 1048576 | tf_op jit(solution)/shard_map/all_to_all | solution.py:132
  113.6 3.3 %convolution_convert_fusion.4 = bf16[256,768]{1,0:T(8,128)(2,1)} fusion(s32[1024]{0:T(1024)S(1)} %get-tuple-element.8, bf16[512,768]{1,0:T(8,128)(2,1)} %collective-permute-done.13, bf16[512,768]{1,0:T(8,128)(2,1)} %maximum_select_fusion.3, pred[]{:T(512)S(6)} %eq.51), kind=kOutput, calls=%fused_computation.54 | convolution fusion | flops 410189824 | bytes 1970177 | tf_op jit(solution)/shard_map/dot_general | solution.py:111
  116.9 8.8 %all-to-all-done = bf16[16,2,8,1024]{3,2,1,0:T(8,128)(2,1)S(1)} async-done(((bf16[16,2,8,1024]{3,2,1,0:T(8,128)(2,1)}), bf16[16,2,8,1024]{3,2,1,0:T(8,128)(2,1)S(1)}, u32[]{:S(2)}, u32[]{:S(2)}) %all-to-all-start) | async-done | bytes 524320 | tf_op jit(solution)/shard_map/all_to_all | solution.py:132
  125.8 3.8 %all-to-all-start.1 = ((bf16[16,2,8,768]{3,2,1,0:T(8,128)(2,1)}), bf16[16,2,8,768]{3,2,1,0:T(8,128)(2,1)S(1)}, u32[]{:S(2)}, u32[]{:S(2)}) async-start(bf16[16,2,8,768]{3,2,1,0:T(8,128)(2,1)} %bitcast.11), calls=%async_computation.1 | async-start | bytes 786432 | tf_op jit(solution)/shard_map/all_to_all | solution.py:132
  129.5 4.9 %copy.18 = bf16[16,8,16,1792]{3,2,1,0:T(8,128)(2,1)S(1)} copy(bf16[16,8,16,1792]{3,1,2,0:T(8,128)(2,1)} %bitcast.138) | data formatting | bytes 14680064
  134.4 2.6 %slice.228 = bf16[2,16,1024,64]{2,1,3,0:T(8,128)(2,1)} slice(bf16[2,16,1792,64]{2,1,3,0:T(8,128)(2,1)S(1)} %bitcast.128), slice={[0:2], [0:16], [0:1024], [0:64]} | slice | bytes 8388608 | tf_op jit(solution)/shard_map/slice | solution.py:134
  137.0 1.9 slice.229
  138.9 6.7 %fusion.50 = f32[2,8,64]{2,1,0:T(8,128)S(1)} fusion(bf16[16,2,8,1024]{3,2,1,0:T(8,128)(2,1)S(1)} %all-to-all-done, bf16[2,16,1024,64]{2,1,3,0:T(8,128)(2,1)} %slice.228), kind=kOutput, calls=%fused_computation.56 | convolution fusion | flops 33554432 | bytes 4722688 | tf_op jit(solution)/shard_map/hjcf,jhfr->jcr/dot_general | solution.py:133
  145.5 3.4 %convolution_convert_fusion = bf16[2,8,8192]{2,1,0:T(8,128)(2,1)S(1)} fusion(bf16[2,64,8192]{2,1,0:T(8,128)(2,1)S(1)} %copy-done, f32[2,8,64]{2,1,0:T(8,128)S(1)} %fusion.50, bf16[16,2,8,768]{3,2,1,0:T(8,128)(2,1)S(1)} %all-to-all-done.1, bf16[2,16,768,64]{2,1,3,0:T(8,128)(2,1)} %slice.229), kind=kOutput, calls=%fused_computation | convolution fusion | flops 42076160 | bytes 5902336 | tf_op jit(solution)/shard_map/jcr,jrd->jcd/dot_general | solution.py:137
  150.0 4.4 %all-to-all-start.2 = ((bf16[8,16,1024]{2,1,0:T(8,128)(2,1)}), bf16[8,16,1024]{2,1,0:T(8,128)(2,1)S(1)}, u32[]{:S(2)}, u32[]{:S(2)}) async-start(bf16[8,16,1024]{2,1,0:T(8,128)(2,1)} %bitcast.127), calls=%async_computation.2 | async-start | bytes 524288 | tf_op jit(solution)/shard_map/all_to_all | solution.py:142
  154.4 6.1 %fusion.25 = f32[1024,1024]{1,0:T(8,128)} fusion(bf16[1792,1024]{1,0:T(8,128)(2,1)} %param.11, bf16[512,768]{1,0:T(8,128)(2,1)} %collective-permute-done.13, bf16[512,768]{1,0:T(8,128)(2,1)} %maximum_select_fusion.3, pred[]{:T(512)S(6)} %eq.51), kind=kOutput, calls=%fused_computation.39 | convolution fusion | flops 1617690624 | bytes 7340033 | tf_op jit(solution)/shard_map/dot_general | solution.py:111
  160.5 1.4 all-to-all-done.2
  163.2 6.2 %add_add_fusion = f32[1024,1024]{1,0:T(8,128)S(1)} fusion(f32[1024,1024]{1,0:T(8,128)S(1)} %fusion.81, f32[1024,1024]{1,0:T(8,128)} %fusion.25, bf16[1792,1024]{1,0:T(8,128)(2,1)} %param.11, bf16[512,1024]{1,0:T(8,128)(2,1)} %collective-permute-done.6, bf16[512,1024]{1,0:T(8,128)(2,1)S(1)} %copy-done.9, pred[]{:T(512)S(6)} %eq.51), kind=kOutput, calls=%fused_computation.9 | convolution fusion | flops 2159017984 | bytes 16777216 | tf_op jit(solution)/shard_map/dot_general | solution.py:111
  170.1 1.7 collective-permute-start.18
  172.0 2.1 %collective-permute-start.14 = (bf16[8,64,512]{2,1,0:T(8,128)(2,1)S(1)}, bf16[8,64,512]{2,1,0:T(8,128)(2,1)S(1)}, u32[]{:S(2)}, u32[]{:S(2)}) collective-permute-start(bf16[8,64,512]{2,1,0:T(8,128)(2,1)S(1)} %fusion.63), channel_id=1, source_target_pairs={{0,96},{1,25},{8,104},{9,17},{16,112},{17,9},{24,120},{25,1},{32,6... | collective-permute-start | bytes 1572872 | tf_op jit(solution)/shard_map/ppermute | solution.py:166
  174.4 5.0 %collective-permute-done.18 = bf16[8,64,512]{2,1,0:T(8,128)(2,1)S(1)} collective-permute-done((bf16[8,64,512]{2,1,0:T(8,128)(2,1)S(1)}, bf16[8,64,512]{2,1,0:T(8,128)(2,1)S(1)}, u32[]{:S(2)}, u32[]{:S(2)}) %collective-permute-start.18) | collective-permute-done | bytes 524320 | tf_op jit(solution)/shard_map/ppermute | solution.py:166
  179.7 2.9 %collective-permute-start.19 = (bf16[4,64,512]{2,1,0:T(8,128)(2,1)S(1)}, bf16[4,64,512]{2,1,0:T(8,128)(2,1)S(1)}, u32[]{:S(2)}, u32[]{:S(2)}) collective-permute-start(bf16[4,64,512]{2,1,0:T(8,128)(2,1)S(1)} %fusion.75), channel_id=1, source_target_pairs={{0,96},{1,25},{8,104},{9,17},{16,112},{17,9},{24,120},{25,1},{32,6... | collective-permute-start | bytes 786440 | tf_op jit(solution)/shard_map/ppermute | solution.py:166
  183.3 4.0 %collective-permute-done.19 = bf16[4,64,512]{2,1,0:T(8,128)(2,1)S(1)} collective-permute-done((bf16[4,64,512]{2,1,0:T(8,128)(2,1)S(1)}, bf16[4,64,512]{2,1,0:T(8,128)(2,1)S(1)}, u32[]{:S(2)}, u32[]{:S(2)}) %collective-permute-start.19) | collective-permute-done | bytes 262176 | tf_op jit(solution)/shard_map/ppermute | solution.py:166
  187.5 1.7 collective-permute-start.20
  189.2 1.6 collective-permute-done.15
  191.0 2.6 %collective-permute-start.16 = (bf16[2,64,512]{2,1,0:T(8,128)(2,1)S(1)}, bf16[2,64,512]{2,1,0:T(8,128)(2,1)S(1)}, u32[]{:S(2)}, u32[]{:S(2)}) collective-permute-start(bf16[2,64,512]{2,1,0:T(8,128)(2,1)S(1)} %fusion.85), channel_id=1, source_target_pairs={{0,24},{1,97},{8,16},{9,105},{16,8},{17,113},{24,0},{25,121},{32,5... | collective-permute-start | bytes 393224 | tf_op jit(solution)/shard_map/ppermute | solution.py:166
  193.7 1.8 collective-permute-start.21
  195.6 1.7 collective-permute-done.16
  197.7 1.6 collective-permute-done.21
  199.3 2.4 %collective-permute-done.17 = bf16[1,64,512]{2,1,0:T(8,128)(2,1)S(1)} collective-permute-done((bf16[1,64,512]{2,1,0:T(8,128)(2,1)S(1)}, bf16[1,64,512]{2,1,0:T(8,128)(2,1)S(1)}, u32[]{:S(2)}, u32[]{:S(2)}) %collective-permute-start.17) | collective-permute-done | bytes 65568 | tf_op jit(solution)/shard_map/ppermute | solution.py:166
  (91 shorter events, 13.3 us)
Async XLA Ops:
  0.0 145.5 %copy-start = (bf16[2,64,8192]{2,1,0:T(8,128)(2,1)S(1)}, bf16[2,64,8192]{2,1,0:T(8,128)(2,1)}, u32[]{:S(2)}) copy-start(bf16[2,64,8192]{2,1,0:T(8,128)(2,1)} %param.15) | copy-start | bytes 6291460
  19.4 4.3 %copy-start.12 = (bf16[1024,1792]{1,0:T(8,128)(2,1)S(1)}, bf16[1024,1792]{1,0:T(8,128)(2,1)}, u32[]{:S(2)}) copy-start(bf16[1024,1792]{1,0:T(8,128)(2,1)} %param.10) | copy-start | bytes 11010052
  23.7 11.2 %collective-permute-start = (bf16[512,1024]{1,0:T(8,128)(2,1)}, bf16[512,1024]{1,0:T(8,128)(2,1)}, u32[]{:S(2)}, u32[]{:S(2)}) collective-permute-start(bf16[512,1024]{1,0:T(8,128)(2,1)} %fusion.31), channel_id=1, source_target_pairs={{0,1},{1,0},{2,3},{3,2},{4,5},{5,4},{6,7},{7,6},{8,9},{9,8},{10,11... | collective-permute-start | bytes 3145736 | tf_op jit(solution)/shard_map/ppermute | solution.py:121
  27.2 11.3 %collective-permute-start.1 = (bf16[512,1024]{1,0:T(8,128)(2,1)}, bf16[512,1024]{1,0:T(8,128)(2,1)S(1)}, u32[]{:S(2)}, u32[]{:S(2)}) collective-permute-start(bf16[512,1024]{1,0:T(8,128)(2,1)} %fusion.34), channel_id=1, source_target_pairs={{0,1},{1,0},{2,3},{3,2},{4,5},{5,4},{6,7},{7,6},{8,9},{9,8},{10,11... | collective-permute-start | bytes 3145736 | tf_op jit(solution)/shard_map/ppermute | solution.py:121
  31.3 13.5 %collective-permute-start.7 = (bf16[512,768]{1,0:T(8,128)(2,1)}, bf16[512,768]{1,0:T(8,128)(2,1)}, u32[]{:S(2)}, u32[]{:S(2)}) collective-permute-start(bf16[512,768]{1,0:T(8,128)(2,1)} %convolution_convert_fusion.2), channel_id=1, source_target_pairs={{0,1},{1,0},{2,3},{3,2},{4,5},{5,4},{6,7},{7,6},{8,9},{9,8},{10,11... | collective-permute-start | bytes 2359304 | tf_op jit(solution)/shard_map/ppermute | solution.py:121
  34.5 13.3 %collective-permute-start.8 = (bf16[512,768]{1,0:T(8,128)(2,1)}, bf16[512,768]{1,0:T(8,128)(2,1)}, u32[]{:S(2)}, u32[]{:S(2)}) collective-permute-start(bf16[512,768]{1,0:T(8,128)(2,1)} %convolution_convert_fusion.1), channel_id=1, source_target_pairs={{0,1},{1,0},{2,3},{3,2},{4,5},{5,4},{6,7},{7,6},{8,9},{9,8},{10,11... | collective-permute-start | bytes 2359304 | tf_op jit(solution)/shard_map/ppermute | solution.py:121
  35.0 3.6 %copy-start.13 = (bf16[1024,1792]{1,0:T(8,128)(2,1)S(1)}, bf16[1024,1792]{1,0:T(8,128)(2,1)}, u32[]{:S(2)}) copy-start(bf16[1024,1792]{1,0:T(8,128)(2,1)} %param.10) | copy-start | bytes 11010052
  38.5 3.3 %copy-start.1 = (f32[512,1,1024]{2,0,1:T(8,128)}, f32[512,1,1024]{2,0,1:T(8,128)S(1)}, u32[]{:S(2)}) copy-start(f32[512,1,1024]{2,0,1:T(8,128)S(1)} %add_bitcast_fusion.1) | copy-start | bytes 6291460
  41.8 1.3 copy-start.2
  43.2 14.9 %collective-permute-start.2 = (bf16[256,2,1024]{2,0,1:T(8,128)(2,1)S(1)}, bf16[256,2,1024]{2,0,1:T(8,128)(2,1)}, u32[]{:S(2)}, u32[]{:S(2)}) collective-permute-start(bf16[256,2,1024]{2,0,1:T(8,128)(2,1)S(1)} %fusion.6), channel_id=1, source_target_pairs={{0,2},{1,7},{2,0},{3,5},{4,6},{5,3},{6,4},{7,1},{8,10},{9,15},{10,... | collective-permute-start | bytes 3145736 | tf_op jit(solution)/shard_map/ppermute | solution.py:125
  47.7 3.0 %copy-start.5 = (f32[512,1,768]{2,0,1:T(8,128)}, f32[512,1,768]{2,0,1:T(8,128)S(1)}, u32[]{:S(2)}) copy-start(f32[512,1,768]{2,0,1:T(8,128)S(1)} %add_bitcast_fusion.3) | copy-start | bytes 4718596
  50.8 1.5 copy-start.6
  52.3 16.2 %collective-permute-start.9 = (bf16[256,2,768]{2,0,1:T(8,128)(2,1)}, bf16[256,2,768]{2,0,1:T(8,128)(2,1)}, u32[]{:S(2)}, u32[]{:S(2)}) collective-permute-start(bf16[256,2,768]{2,0,1:T(8,128)(2,1)} %fusion.22), channel_id=1, source_target_pairs={{0,2},{1,7},{2,0},{3,5},{4,6},{5,3},{6,4},{7,1},{8,10},{9,15},{10,... | collective-permute-start | bytes 2359304 | tf_op jit(solution)/shard_map/ppermute | solution.py:125
  60.2 1.4 copy-start.3
  61.7 12.5 %collective-permute-start.3 = (bf16[128,2,1024]{2,0,1:T(8,128)(2,1)S(1)}, bf16[128,2,1024]{2,0,1:T(8,128)(2,1)S(1)}, u32[]{:S(2)}, u32[]{:S(2)}) collective-permute-start(bf16[128,2,1024]{2,0,1:T(8,128)(2,1)S(1)} %dynamic-slice_convert_fusion), channel_id=1, source_target_pairs={{0,6},{1,3},{2,4},{3,1},{4,2},{5,7},{6,0},{7,5},{8,14},{9,11},{10,... | collective-permute-start | bytes 1572872 | tf_op jit(solution)/shard_map/ppermute | solution.py:125
  64.9 9.3 %copy-start.4 = (f32[256,2,1024]{2,0,1:T(8,128)S(1)}, f32[256,2,1024]{2,0,1:T(8,128)}, u32[]{:S(2)}) copy-start(f32[256,2,1024]{2,0,1:T(8,128)} %copy-done.3) | copy-start | bytes 6291460
  70.2 4.2 %copy-start.7 = (f32[256,2,768]{2,0,1:T(8,128)}, f32[256,2,768]{2,0,1:T(8,128)S(1)}, u32[]{:S(2)}) copy-start(f32[256,2,768]{2,0,1:T(8,128)S(1)} %fusion.24) | copy-start | bytes 4718596
  71.1 4.6 %copy-start.10 = (s32[1024,1]{0,1:T(1,128)S(1)}, s32[1024,1]{0,1:T(1,128)}, u32[]{:S(2)}) copy-start(s32[1024,1]{0,1:T(1,128)} %param.12) | copy-start | bytes 12292
  71.1 9.2 %collective-permute-start.10 = (bf16[128,2,768]{2,0,1:T(8,128)(2,1)}, bf16[128,2,768]{2,0,1:T(8,128)(2,1)S(1)}, u32[]{:S(2)}, u32[]{:S(2)}) collective-permute-start(bf16[128,2,768]{2,0,1:T(8,128)(2,1)} %dynamic-slice_convert_fusion.1), channel_id=1, source_target_pairs={{0,6},{1,3},{2,4},{3,1},{4,2},{5,7},{6,0},{7,5},{8,14},{9,11},{10,... | collective-permute-start | bytes 1179656 | tf_op jit(solution)/shard_map/ppermute | solution.py:125
  74.5 8.7 %collective-permute-start.4 = (bf16[128,1024]{1,0:T(8,128)(2,1)S(1)}, bf16[128,1024]{1,0:T(8,128)(2,1)S(1)}, u32[]{:S(2)}, u32[]{:S(2)}) collective-permute-start(bf16[128,1024]{1,0:T(8,128)(2,1)S(1)} %fusion.74), channel_id=1, source_target_pairs={{0,6},{1,3},{2,4},{3,1},{4,2},{5,7},{6,0},{7,5},{8,14},{9,11},{10,... | collective-permute-start | bytes 786440 | tf_op jit(solution)/shard_map/ppermute | solution.py:128
  83.3 11.4 %copy-start.11 = (s32[256]{0:T(256)S(1)}, s32[256]{0:T(256)}, u32[]{:S(2)}) copy-start(s32[256]{0:T(256)} %param.13) | copy-start | bytes 3076
  83.3 10.8 %collective-permute-start.5 = (bf16[256,1024]{1,0:T(8,128)(2,1)S(1)}, bf16[256,1024]{1,0:T(8,128)(2,1)S(1)}, u32[]{:S(2)}, u32[]{:S(2)}) collective-permute-start(bf16[256,1024]{1,0:T(8,128)(2,1)S(1)} %maximum_select_fusion.4), channel_id=1, source_target_pairs={{0,2},{1,7},{2,0},{3,5},{4,6},{5,3},{6,4},{7,1},{8,10},{9,15},{10,... | collective-permute-start | bytes 1572872 | tf_op jit(solution)/shard_map/ppermute | solution.py:129
  85.5 7.4 %collective-permute-start.11 = (bf16[128,768]{1,0:T(8,128)(2,1)S(1)}, bf16[128,768]{1,0:T(8,128)(2,1)S(1)}, u32[]{:S(2)}, u32[]{:S(2)}) collective-permute-start(bf16[128,768]{1,0:T(8,128)(2,1)S(1)} %fusion.83), channel_id=1, source_target_pairs={{0,6},{1,3},{2,4},{3,1},{4,2},{5,7},{6,0},{7,5},{8,14},{9,11},{10,... | collective-permute-start | bytes 589832 | tf_op jit(solution)/shard_map/ppermute | solution.py:128
  93.0 7.9 %collective-permute-start.12 = (bf16[256,768]{1,0:T(8,128)(2,1)S(1)}, bf16[256,768]{1,0:T(8,128)(2,1)S(1)}, u32[]{:S(2)}, u32[]{:S(2)}) collective-permute-start(bf16[256,768]{1,0:T(8,128)(2,1)S(1)} %maximum_select_fusion.5), channel_id=1, source_target_pairs={{0,2},{1,7},{2,0},{3,5},{4,6},{5,3},{6,4},{7,1},{8,10},{9,15},{10,... | collective-permute-start | bytes 1179656 | tf_op jit(solution)/shard_map/ppermute | solution.py:129
  94.6 11.1 %copy-start.8 = (bf16[512,1024]{1,0:T(8,128)(2,1)}, bf16[512,1024]{1,0:T(8,128)(2,1)S(1)}, u32[]{:S(2)}) copy-start(bf16[512,1024]{1,0:T(8,128)(2,1)S(1)} %maximum_select_fusion.2) | copy-start | bytes 3145732
  94.6 7.7 %collective-permute-start.6 = (bf16[512,1024]{1,0:T(8,128)(2,1)S(1)}, bf16[512,1024]{1,0:T(8,128)(2,1)}, u32[]{:S(2)}, u32[]{:S(2)}) collective-permute-start(bf16[512,1024]{1,0:T(8,128)(2,1)S(1)} %maximum_select_fusion.2), channel_id=1, source_target_pairs={{0,1},{1,0},{2,3},{3,2},{4,5},{5,4},{6,7},{7,6},{8,9},{9,8},{10,11... | collective-permute-start | bytes 3145736 | tf_op jit(solution)/shard_map/ppermute | solution.py:130
  102.1 11.5 %collective-permute-start.13 = (bf16[512,768]{1,0:T(8,128)(2,1)}, bf16[512,768]{1,0:T(8,128)(2,1)}, u32[]{:S(2)}, u32[]{:S(2)}) collective-permute-start(bf16[512,768]{1,0:T(8,128)(2,1)} %maximum_select_fusion.3), channel_id=1, source_target_pairs={{0,1},{1,0},{2,3},{3,2},{4,5},{5,4},{6,7},{7,6},{8,9},{9,8},{10,11... | collective-permute-start | bytes 2359304 | tf_op jit(solution)/shard_map/ppermute | solution.py:130
  105.7 20.1 %all-to-all-start = ((bf16[16,2,8,1024]{3,2,1,0:T(8,128)(2,1)}), bf16[16,2,8,1024]{3,2,1,0:T(8,128)(2,1)S(1)}, u32[]{:S(2)}, u32[]{:S(2)}) async-start(bf16[16,2,8,1024]{3,2,1,0:T(8,128)(2,1)} %bitcast.154), calls=%async_computation | async-start | bytes 1048576 | tf_op jit(solution)/shard_map/all_to_all | solution.py:132
  125.8 19.8 %all-to-all-start.1 = ((bf16[16,2,8,768]{3,2,1,0:T(8,128)(2,1)}), bf16[16,2,8,768]{3,2,1,0:T(8,128)(2,1)S(1)}, u32[]{:S(2)}, u32[]{:S(2)}) async-start(bf16[16,2,8,768]{3,2,1,0:T(8,128)(2,1)} %bitcast.11), calls=%async_computation.1 | async-start | bytes 786432 | tf_op jit(solution)/shard_map/all_to_all | solution.py:132
  150.0 12.0 %all-to-all-start.2 = ((bf16[8,16,1024]{2,1,0:T(8,128)(2,1)}), bf16[8,16,1024]{2,1,0:T(8,128)(2,1)S(1)}, u32[]{:S(2)}, u32[]{:S(2)}) async-start(bf16[8,16,1024]{2,1,0:T(8,128)(2,1)} %bitcast.127), calls=%async_computation.2 | async-start | bytes 524288 | tf_op jit(solution)/shard_map/all_to_all | solution.py:142
  161.9 1.2 copy-start.9
  170.1 9.3 %collective-permute-start.18 = (bf16[8,64,512]{2,1,0:T(8,128)(2,1)S(1)}, bf16[8,64,512]{2,1,0:T(8,128)(2,1)S(1)}, u32[]{:S(2)}, u32[]{:S(2)}) collective-permute-start(bf16[8,64,512]{2,1,0:T(8,128)(2,1)S(1)} %fusion.61), channel_id=1, source_target_pairs={{0,32},{1,9},{8,40},{9,1},{16,48},{17,25},{24,56},{25,17},{32,0},{... | collective-permute-start | bytes 1572872 | tf_op jit(solution)/shard_map/ppermute | solution.py:166
  172.0 10.7 %collective-permute-start.14 = (bf16[8,64,512]{2,1,0:T(8,128)(2,1)S(1)}, bf16[8,64,512]{2,1,0:T(8,128)(2,1)S(1)}, u32[]{:S(2)}, u32[]{:S(2)}) collective-permute-start(bf16[8,64,512]{2,1,0:T(8,128)(2,1)S(1)} %fusion.63), channel_id=1, source_target_pairs={{0,96},{1,25},{8,104},{9,17},{16,112},{17,9},{24,120},{25,1},{32,6... | collective-permute-start | bytes 1572872 | tf_op jit(solution)/shard_map/ppermute | solution.py:166
  179.7 7.7 %collective-permute-start.19 = (bf16[4,64,512]{2,1,0:T(8,128)(2,1)S(1)}, bf16[4,64,512]{2,1,0:T(8,128)(2,1)S(1)}, u32[]{:S(2)}, u32[]{:S(2)}) collective-permute-start(bf16[4,64,512]{2,1,0:T(8,128)(2,1)S(1)} %fusion.75), channel_id=1, source_target_pairs={{0,96},{1,25},{8,104},{9,17},{16,112},{17,9},{24,120},{25,1},{32,6... | collective-permute-start | bytes 786440 | tf_op jit(solution)/shard_map/ppermute | solution.py:166
  183.0 7.9 %collective-permute-start.15 = (bf16[4,64,512]{2,1,0:T(8,128)(2,1)S(1)}, bf16[4,64,512]{2,1,0:T(8,128)(2,1)S(1)}, u32[]{:S(2)}, u32[]{:S(2)}) collective-permute-start(bf16[4,64,512]{2,1,0:T(8,128)(2,1)S(1)} %fusion.77), channel_id=1, source_target_pairs={{0,32},{1,9},{8,40},{9,1},{16,48},{17,25},{24,56},{25,17},{32,0},{... | collective-permute-start | bytes 786440 | tf_op jit(solution)/shard_map/ppermute | solution.py:166
  187.5 6.2 %collective-permute-start.20 = (bf16[2,64,512]{2,1,0:T(8,128)(2,1)S(1)}, bf16[2,64,512]{2,1,0:T(8,128)(2,1)S(1)}, u32[]{:S(2)}, u32[]{:S(2)}) collective-permute-start(bf16[2,64,512]{2,1,0:T(8,128)(2,1)S(1)} %fusion.86), channel_id=1, source_target_pairs={{0,8},{1,33},{8,0},{9,41},{16,24},{17,49},{24,16},{25,57},{32,40},... | collective-permute-start | bytes 393224 | tf_op jit(solution)/shard_map/ppermute | solution.py:166
  191.0 6.3 %collective-permute-start.16 = (bf16[2,64,512]{2,1,0:T(8,128)(2,1)S(1)}, bf16[2,64,512]{2,1,0:T(8,128)(2,1)S(1)}, u32[]{:S(2)}, u32[]{:S(2)}) collective-permute-start(bf16[2,64,512]{2,1,0:T(8,128)(2,1)S(1)} %fusion.85), channel_id=1, source_target_pairs={{0,24},{1,97},{8,16},{9,105},{16,8},{17,113},{24,0},{25,121},{32,5... | collective-permute-start | bytes 393224 | tf_op jit(solution)/shard_map/ppermute | solution.py:166
  193.7 5.6 %collective-permute-start.21 = (bf16[1,64,512]{2,1,0:T(8,128)(2,1)S(1)}, bf16[1,64,512]{2,1,0:T(8,128)(2,1)S(1)}, u32[]{:S(2)}, u32[]{:S(2)}) collective-permute-start(bf16[1,64,512]{2,1,0:T(8,128)(2,1)S(1)} %dynamic-slice_convert_fusion.4), channel_id=1, source_target_pairs={{0,24},{1,97},{8,16},{9,105},{16,8},{17,113},{24,0},{25,121},{32,5... | collective-permute-start | bytes 196616 | tf_op jit(solution)/shard_map/ppermute | solution.py:166
  197.3 4.3 %collective-permute-start.17 = (bf16[1,64,512]{2,1,0:T(8,128)(2,1)S(1)}, bf16[1,64,512]{2,1,0:T(8,128)(2,1)S(1)}, u32[]{:S(2)}, u32[]{:S(2)}) collective-permute-start(bf16[1,64,512]{2,1,0:T(8,128)(2,1)S(1)} %dynamic-slice_convert_fusion.5), channel_id=1, source_target_pairs={{0,8},{1,33},{8,0},{9,41},{16,24},{17,49},{24,16},{25,57},{32,40},... | collective-permute-start | bytes 196616 | tf_op jit(solution)/shard_map/ppermute | solution.py:166

commit v2 on v0

v2 whole, which is shorter than its diff:
```python
import jax
import jax.numpy as jnp
from jax import lax
from jax.experimental import pallas as pl
from jax.experimental.pallas import tpu as pltpu
from jax.sharding import Mesh, PartitionSpec as P

BF = jnp.bfloat16
F32 = jnp.float32
TILE = 256
STEP_TYPES = (BF, BF, BF, F32)
VM_OWN, VM_LOW = 24, 24
STREAMS = (((0, 1, 2, 3), (2, 3, 0, 1)), ((1, 0, 3, 2), (3, 2, 1, 0)))


def flip_a(v):
    return v ^ 1


def flip_b(v):
    return 3 - v


def gray(v):
    return v ^ (v >> 1)


def hid_perm(dims):
    pairs = []
    for x in range(4):
        for z in range(4):
            for k in range(2):
                move = flip_b if dims[k] % 2 == 0 else flip_a
                to = (move(x), z) if dims[k] < 2 else (x, move(z))
                pairs.append(((x * 4 + z) * 2 + k, (to[0] * 4 + to[1]) * 2 + k))
    return pairs


def dot(a, b):
    return jnp.dot(a, b, preferred_element_type=F32)


def take(ref, table, start, count, rows):
    return jnp.concatenate(
        [ref[pl.ds(pl.multiple_of(table[start + p] * rows, rows), rows), :] for p in range(count)], 0
    )


def call(body, grid, ins, outs, mib, flops=0, moved=0, after=(), table=None, scratch=()):
    first = 0 if table is None else 1
    token_spec = pl.BlockSpec((8, 128), lambda *i: (0, 0))

    def kernel(*refs):
        used = refs[: first + len(ins)] + refs[first + len(ins) + len(after) :]
        used[first + len(ins) + len(outs)][...] = jnp.zeros((8, 128), F32)
        body(*used[: first + len(ins) + len(outs)], *used[first + len(ins) + len(outs) + 1 :])

    specs = [spec for _, spec in ins] + [pl.BlockSpec(memory_space=pl.ANY)] * len(after)
    args = [] if table is None else [table]
    args += [v for v, _ in ins] + list(after)
    return pl.pallas_call(
        kernel,
        out_shape=[jax.ShapeDtypeStruct(*o[0]) for o in outs]
        + [jax.ShapeDtypeStruct((8, 128), F32)],
        grid_spec=pltpu.PrefetchScalarGridSpec(
            num_scalar_prefetch=first,
            grid=(grid,),
            in_specs=specs,
            out_specs=[o[1] for o in outs] + [token_spec],
            scratch_shapes=list(scratch),
        ),
        compiler_params=pltpu.CompilerParams(
            vmem_limit_bytes=mib * 2**20, dimension_semantics=("arbitrary",)
        ),
        cost_estimate=pl.CostEstimate(flops=flops, bytes_accessed=moved, transcendentals=0),
    )(*args)


def block_of(*shape):
    return pl.BlockSpec(shape, lambda *_: (0,) * len(shape))


def whole(v):
    return v, pl.BlockSpec(v.shape, lambda *_: (0,) * v.ndim)


def own_sums(table, tokens, weight, after=()):
    rows, depth = tokens.shape
    width = weight.shape[1] // 2

    def body(table, tokens, weight, out):
        left = take(tokens, table, 1, 4, rows // 4)
        for start in range(0, width, TILE):
            at = slice(start, min(start + TILE, width))
            out[:, at] = dot(left, weight[:, at])

    return call(
        body, 1, [whole(tokens), (weight, pl.BlockSpec((depth, width), lambda j, t: (0, t[0])))],
        [(((rows, width), F32), block_of(rows, width))],
        VM_OWN, 2 * rows * depth * width, 2 * depth * width, after, table,
    )


def add_sums(table, tokens, weight, own, after=()):
    rows, depth = tokens.shape
    width = weight.shape[1]
    half = rows // 2

    def body(table, tokens, weight, own, sent, kept):
        left = take(tokens, table, 1, 4, rows // 4)
        for start in range(0, width, TILE):
            at = slice(start, min(start + TILE, width))
            total = dot(left, weight[:, at]) + own[:, at]
            kept[:, at] = total[:half]
            sent[:, at] = total[half:].astype(sent.dtype)

    return call(
        body, 1, [whole(tokens), whole(weight), whole(own)],
        [(((half, width), BF), block_of(half, width)), (((half, width), F32), block_of(half, width))],
        30, 2 * rows * depth * width, 2 * depth * width, after, table,
    )


def add_halves(kept, arrived, after=()):
    rows, width = kept.shape
    half = rows // 2

    def body(kept_in, arrived, sent, kept):
        total = kept_in[...] + arrived[...].astype(F32)
        kept[...] = total[:half]
        sent[...] = total[half:].astype(sent.dtype)

    return call(
        body, 1, [whole(kept), whole(arrived)],
        [(((half, width), BF), block_of(half, width)), (((half, width), F32), block_of(half, width))],
        16, 4 * rows * width, 9 * rows * width, after,
    )


def activate(gate, gate_arrived, up, up_arrived):
    def body(gate, gate_arrived, up, up_arrived, out):
        gates = gate[...] + gate_arrived[...].astype(F32)
        ups = up[...] + up_arrived[...].astype(F32)
        out[...] = (jax.nn.silu(gates) * ups).astype(BF)

    rows, width = gate.shape
    return call(
        body, 1, [whole(v) for v in (gate, gate_arrived, up, up_arrived)],
        [((gate.shape, BF), block_of(rows, width))],
        16, 20 * rows * width, 14 * rows * width,
    )


def pack(table, selectors, mine, theirs):
    slots, rows = selectors[0].shape
    width = mine.shape[1]

    def body(table, first, second, mine, theirs, out):
        for ref, selector, turn in ((mine, first, 0), (theirs, second, 1)):
            value = dot(selector[...], ref[...]).astype(out.dtype)
            for side in range(2):
                @pl.when((table[0] ^ turn) == side)
                def _():
                    out[:, side * width : (side + 1) * width] = value

    return call(
        body, 1, [whole(selectors[0]), whole(selectors[1]), whole(mine), whole(theirs)],
        [(((slots, 2 * width), BF), block_of(slots, 2 * width))],
        20, 4 * slots * rows * width, 4 * rows * width, (), table,
    )


def down(table, weight, mine, theirs, after):
    depth, width = weight.shape
    rows, half = mine.shape

    def body(table, weight, mine, theirs, out):
        side = table[0]
        left = mine[...]
        right = take(theirs, table, 5, 4, rows // 4)
        for start in range(0, width, TILE):
            at = slice(start, start + TILE)
            near = weight[pl.ds(pl.multiple_of(side * half, half), half), at]
            far = weight[pl.ds(pl.multiple_of((1 - side) * half, half), half), at]
            out[:, at] = dot(left, near) + dot(right, far)

    return call(
        body, 1, [whole(weight), whole(mine), whole(theirs)],
        [(((rows, width), F32), block_of(rows, width))],
        36, 2 * rows * depth * width, 2 * rows * depth + 2 * depth * width, after, table,
    )


def adapt(arrived, first, second, per_dev, pieces, after):
    groups, slots, width = arrived.shape
    ranks, columns = second.shape
    piece = columns // pieces

    def body(rows, first, second, out, held, low_ref):
        h = pl.program_id(0)

        @pl.when(h == 0)
        def _():
            low_ref[...] = jnp.zeros_like(low_ref)

        low_ref[...] += lax.dot_general(
            rows[0], first[...], (((1,), (1,)), ((), ())), preferred_element_type=F32
        )

        @pl.when(h == groups - 1)
        def _():
            low = low_ref[...]
            row = lax.broadcasted_iota(jnp.int32, low.shape, 0) // (slots // per_dev)
            column = lax.broadcasted_iota(jnp.int32, low.shape, 1) // (ranks // per_dev)
            own = jnp.where(row == column, low, 0.0).astype(BF)
            for j in range(pieces):
                out[j] = dot(own, second[:, j * piece : (j + 1) * piece]).astype(out.dtype)

    return call(
        lambda rows, first, second, out, low: body(rows, first, second, out, None, low), groups,
        [
            (arrived, pl.BlockSpec((1, slots, width), lambda h: (h, 0, 0))),
            (first, pl.BlockSpec((ranks, width), lambda h: (0, h))),
            whole(second),
        ],
        [(((pieces, slots, piece), BF), block_of(pieces, slots, piece))],
        VM_LOW, 2 * slots * ranks * width * groups, 2 * ranks * width * groups, after, None,
        [pltpu.VMEM((slots, ranks), F32)],
    )


def land(table, base, landing, returned):
    rows, columns = base.shape
    width, slots = columns // 2, returned.shape[0]
    count = 8
    block = rows // 2 // count
    half = pl.BlockSpec((rows // 2, width), lambda s, t: (0, 0))

    def body(table, base, landing, returned, *outs):
        for stream in range(2):
            at = slice(stream * width, (stream + 1) * width)
            for ref, start in ((outs[2 * stream], count), (outs[2 * stream + 1], 0)):
                first = stream * 2 * count + start
                left = take(landing, table, first, count, block)
                near = jnp.concatenate(
                    [
                        base[pl.ds(pl.multiple_of(table[first + p] * block, block), block), at]
                        for p in range(count)
                    ],
                    0,
                )
                ref[...] = (near + dot(left, returned[:, at])).astype(ref.dtype)

    shape = (rows // 2, width)
    outs = [((shape, BF), half), ((shape, F32), half)] * 2
    return call(
        body, 1, [whole(base), whole(landing), whole(returned)], outs,
        20, 2 * rows * slots * columns, 10 * rows * columns, (), table,
    )


def per_device(
    tokens, gate_weight, up_weight, down_weight, adapter_id, owner_slot, adapt_down, adapt_up
):
    x, z, y, c = (lax.axis_index(n) for n in ("x", "z", "y", "c"))
    row_count = tokens.shape[0]
    d_local = down_weight.shape[1]
    adapter_count = owner_slot.shape[0]
    per_dev, ff_count, rank = adapt_down.shape
    capacity = 2 * row_count // adapter_count
    slots = per_dev * capacity
    wid_axes, hid_axes = ("y", "c"), ("x", "z")
    wid_index, hid_index = y * 2 + c, x * 4 + z

    swap_perm = [(i, i ^ 1) for i in range(8)]
    first = (flip_a, flip_b)
    perm1 = [(v * 2 + k, first[k](v) * 2 + k) for v in range(4) for k in range(2)]
    perm2 = [(v * 2 + k, first[1 - k](v) * 2 + k) for v in range(4) for k in range(2)]

    gray_y = gray(y)
    low_y, high_y = gray_y & 1, gray_y >> 1
    four = jnp.arange(4, dtype=jnp.int32)
    ff_half = gate_weight.shape[1] // 2

    def at_place(core):
        one, two = four >> 1, four & 1
        low = jnp.where(core == 0, one, two) ^ low_y
        high = jnp.where(core == 0, two, one) ^ high_y
        return low * 2 + high

    def place_of(core, blocks):
        low, high = (blocks >> 1) ^ low_y, (blocks & 1) ^ high_y
        return jnp.where(core == 0, low * 2 + high, high * 2 + low)

    home_blocks, away_blocks = at_place(c), at_place(1 - c)
    table = jnp.concatenate([c[None], home_blocks, place_of(1 - c, home_blocks)])

    bits = jnp.stack([gray(x) >> 1, gray(x) & 1, gray(z) >> 1, gray(z) & 1])
    sixteen = jnp.arange(16, dtype=jnp.int32)
    land_tables = []
    for dims in STREAMS:
        found = []
        for d in range(4):
            shift = jnp.where(c == 0, 3 - dims[0].index(d), 3 - dims[1].index(d))
            found.append(((sixteen >> shift) & 1) ^ bits[d])
        at_x, at_z = gray(found[0] * 2 + found[1]), gray(found[2] * 2 + found[3])
        land_tables.append(place_of(c, at_x) * 4 + at_z)
    land_table = jnp.concatenate(land_tables)

    def selections(token):
        row_adapter = adapter_id[:, 0] + token[0, 0].astype(jnp.int32)
        adapter_range = jnp.arange(adapter_count, dtype=jnp.int32)
        row_slot = jnp.sum(
            jnp.where(row_adapter[:, None] == adapter_range[None, :], owner_slot[None, :], 0), axis=1
        )
        positions = jnp.arange(row_count, dtype=jnp.int32)
        earlier = (row_adapter[:, None] == row_adapter[None, :]) & (
            positions[None, :] < positions[:, None]
        )
        row_rank = jnp.sum(earlier.astype(jnp.int32), axis=1)
        row_owner = row_slot // per_dev
        owner_hid, owner_wid = row_owner // 8, row_owner % 8
        place = (row_slot % per_dev) * capacity + row_rank

        def own_order(v, blocks):
            chosen = blocks[:, None] == four[None, :]
            v = v.reshape(1, 4, row_count // 4)
            return jnp.sum(jnp.where(chosen[:, :, None], v, 0), axis=1).reshape(-1)

        send_index = jnp.where(owner_wid == wid_index, owner_hid * slots + place, -1)
        send_slots = jnp.arange(16 * slots, dtype=jnp.int32)[:, None]
        selectors = [
            (send_slots == own_order(send_index, blocks)[None, :]).astype(BF)
            for blocks in (home_blocks, away_blocks)
        ]
        land_index = jnp.where(owner_hid == hid_index, owner_wid * slots + place, -1)
        land_index = own_order(land_index, home_blocks)
        landing = (land_index[:, None] == jnp.arange(8 * slots, dtype=jnp.int32)[None, :]).astype(BF)
        return selectors, landing

    down_factor = adapt_down.transpose(0, 2, 1).reshape(per_dev * rank, ff_count)
    up_factor = adapt_up.reshape(per_dev * rank, adapt_up.shape[2])

    swap, one, two = (
        lambda v, perm=perm: lax.ppermute(v, wid_axes, perm) for perm in (swap_perm, perm1, perm2)
    )
    far_tokens = swap(tokens)
    far_gate, far_up = (
        swap(lax.dynamic_slice_in_dim(w, (1 - c) * ff_half, ff_half, 1))
        for w in (gate_weight, up_weight)
    )
    own, token = own_sums(table, tokens, gate_weight)
    sent_gate, kept_gate, token = add_sums(table, far_tokens, far_gate, own, [token])
    own, token = own_sums(table, tokens, up_weight, [token])
    sent_up, kept_up, token = add_sums(table, far_tokens, far_up, own, [token])
    selectors, landing = selections(token)
    order = [token, *selectors, landing]
    sent_gate, kept_gate, token = add_halves(kept_gate, one(sent_gate), order)
    sent_up, kept_up, token = add_halves(kept_up, one(sent_up), [token])
    hidden, _ = activate(kept_gate, two(sent_gate), kept_up, two(sent_up))
    hidden = jnp.concatenate([hidden, two(hidden)], 0)
    mine = jnp.concatenate([hidden, one(hidden)], 0)
    theirs = swap(mine)
    packed, token = pack(table, selectors, mine, theirs)
    packed = packed.reshape(16, slots, packed.shape[1])
    arrived = lax.all_to_all(packed, hid_axes, split_axis=0, concat_axis=0, tiled=True)
    base, token = down(table, down_weight, mine, theirs, [token])
    adapted, _ = adapt(arrived, down_factor, up_factor, per_dev, 8, [token])
    returned = lax.all_to_all(adapted, wid_axes, split_axis=0, concat_axis=0, tiled=True)
    ends = land(land_table, base, landing, returned.reshape(8 * slots, d_local))

    outs = []
    for stream, dims in enumerate(STREAMS):
        value = None
        for step in range(4):
            perm = hid_perm([dims[k][step] for k in range(2)])
            if step == 0:
                going, value = ends[2 * stream], ends[2 * stream + 1]
            else:
                half = value.shape[0] // 2
                going, value = value[half:].astype(STEP_TYPES[step]), value[:half]
            value = value + lax.ppermute(going, ("x", "z", "c"), perm).astype(F32)
        outs.append(value)
    return jnp.concatenate(outs, 1).astype(BF)


def solution(mesh):
    fine = Mesh(mesh.devices.reshape(4, 4, 4, 2), ("x", "z", "y", "c"))
    hid, wid = ("x", "z"), ("y", "c")
    return jax.shard_map(
        per_device,
        mesh=fine,
        in_specs=(
            P(None, wid),
            P(wid, hid),
            P(wid, hid),
            P(hid, wid),
            P(),
            P(),
            P(hid + wid, None, None),
            P(hid + wid, None, None),
        ),
        out_specs=P(hid, wid),
        check_vma=False,
    )
```

time: 426 us -> 172 us (0.40)
  waiting for transfers between devices: 307 us -> 81.8 us
  blocking collectives: 33.2 us -> 0 us
  matrix products: 32.7 us -> 0 us
  Pallas kernels: 0 us -> 31.8 us
  starting transfers between devices: 0.09 us -> 27.7 us
  between operations: 13.2 us -> 1.07 us
  other arithmetic: 8.87 us -> 3.07 us
    psum x1 -> x0, waiting for transfers between devices: 165 us -> none  [per_device(): gate, up_value = lax.psum((gate, up_value), 'wid')]
    reduce_scatter x2 -> x0, waiting for transfers between devices: 142 us -> none  [the longest x1 80.7 us: per_device(): mixed = lax.psum_scatter(result, 'hid', scatter_dimension=0, tiled=True)]
    ppermute x0 -> x18, waiting for transfers between devices: none -> 68.4 us  [the longest x10 44.8 us: per_device(): lax.ppermute(v, wid_axes, perm)]
    all_to_all x2 -> x0, blocking collectives: 33.2 us -> none  [the longest x1 21.9 us: per_device(): lax.all_to_all(packed, 'hid', split_axis=0, concat_axis=3, tiled=True)]
    dot_general x6 -> x0, matrix products: 32.7 us -> none  [the longest x1 9.18 us: per_device(): result = jnp.dot(hidden, down_weight, preferred_element_type=jnp.float32)]
    pallas_call x0 -> x11, Pallas kernels: none -> 31.8 us  [call(): pl.pallas_call(kernel, out_shape=[jax.ShapeDtypeStruct(*o[0]) for o in ou...]
    ppermute x0 -> x18, starting transfers between devices: none -> 16.2 us  [the longest x10 10.5 us: per_device(): lax.ppermute(v, wid_axes, perm)]
    all_to_all x0 -> x2, waiting for transfers between devices: none -> 13.4 us  [the longest x1 7.44 us: per_device(): lax.all_to_all(adapted, wid_axes, split_axis=0, concat_axis=0, tiled=True)]
  transfers between devices with their start and end apart: 3 -> 20, of which waited for: 3 -> 14; matrix products, arithmetic and copies ran while one was open for 2% -> 4% of each run, Pallas kernels for 0% -> 13%
where the time goes in v2:
time: 172 us; the launch traced here: 171 us
  waiting for transfers between devices  81.8 us (48%)
  Pallas kernels  31.8 us (18%)
  starting transfers between devices  27.7 us (16%)
  local copies, waits for them, and re-layouts  26 us (15%)
  other arithmetic  3.07 us (2%)
    ppermute x10, waiting for transfers between devices, per_device(): lax.ppermute(v, wid_axes, perm)  44.8 us
    pallas_call x11, Pallas kernels, call(): pl.pallas_call(kernel, out_shape=[jax.ShapeDtypeStruct(*o[0]) for o in ou...  31.8 us
    ppermute x8, waiting for transfers between devices, per_device(): value = value + lax.ppermute(going, ('x', 'z', 'c'), perm).astype(F32)  23.6 us
    unnamed x45, local copies, waits for them, and re-layouts  20.8 us
    ppermute x10, starting transfers between devices, per_device(): lax.ppermute(v, wid_axes, perm)  10.5 us
    all_to_all x1, starting transfers between devices, per_device(): lax.all_to_all(packed, hid_axes, split_axis=0, concat_axis=0, tiled=True)  7.88 us
    all_to_all x1, waiting for transfers between devices, per_device(): lax.all_to_all(adapted, wid_axes, split_axis=0, concat_axis=0, tiled=True)  7.44 us
    all_to_all x1, waiting for transfers between devices, per_device(): lax.all_to_all(packed, hid_axes, split_axis=0, concat_axis=0, tiled=True)  5.97 us
  transfers between devices with their start and end apart: 20, of which 14 were waited for; matrix products, arithmetic and copies ran while one was open for 4% of the time, Pallas kernels for 13%

profile of v2, /device:TPU:0, one launch (start us, length us, event | category | flops | bytes accessed | tf_op | source)
XLA Modules:
  0.0 171.5 jit_solution(10460084764916541063)
XLA Ops:
  0.0 3.0 %constant_dynamic-slice_fusion.1 = bf16[1024,896]{1,0:T(8,128)(2,1)} fusion(bf16[1024,1792]{1,0:T(8,128)(2,1)} %refs_2_.2, s32[]{:T(128)S(6)} %select_n.163), kind=kLoop, calls=%fused_computation.88 | loop fusion | bytes 3670020 | tf_op jit(solution)/shard_map/dynamic_slice | solution.py:349
  3.0 0.5 collective-permute-start.1
  3.6 1.4 constant_dynamic-slice_fusion
  5.1 2.0 %copy-done.11 = bf16[1024,1792]{1,0:T(8,128)(2,1)S(1)} copy-done((bf16[1024,1792]{1,0:T(8,128)(2,1)S(1)}, bf16[1024,1792]{1,0:T(8,128)(2,1)}, u32[]{:S(2)}) %copy-start.11) | copy-done | bytes 3670040
  7.1 1.6 copy-done.15
  8.7 2.9 %shard_map.82 = (f32[1024,896]{1,0:T(8,128)S(1)}, f32[8,128]{1,0:T(8,128)S(1)}) custom-call(s32[9]{0:T(128)S(1)} %pad_add_fusion.1.refs_0_, bf16[1024,1024]{1,0:T(8,128)(2,1)S(1)} %copy-done.15, bf16[1024,1792]{1,0:T(8,128)(2,1)S(1)} %copy-done.11), custom_call_target="tpu_custom_call" | custom-call | flops 1879048192 | bytes 1835008 | tf_op jit(solution)/shard_map/pallas_call | solution.py:61
  11.8 5.6 %shard_map.83 = (bf16[512,896]{1,0:T(8,128)(2,1)}, f32[512,896]{1,0:T(8,128)S(1)}, f32[8,128]{1,0:T(8,128)S(1)}) custom-call(s32[9]{0:T(128)S(1)} %pad_add_fusion.1.refs_0_, bf16[1024,1024]{1,0:T(8,128)(2,1)S(1)} %collective-permute-done.refs_1_, bf16[1024,896]{1,0:T(8,128)(2,1)} %collective-permute-done.1.refs_2_, ...), custom_call_target="tpu_custom_call" | custom-call | flops 1879048192 | bytes 1835008 | tf_op jit(solution)/shard_map/pallas_call | solution.py:61
  17.4 1.7 collective-permute-start.2
  19.0 2.9 %shard_map.84 = (f32[1024,896]{1,0:T(8,128)S(1)}, f32[8,128]{1,0:T(8,128)S(1)}) custom-call(s32[9]{0:T(128)S(1)} %pad_add_fusion.1.refs_0_, bf16[1024,1024]{1,0:T(8,128)(2,1)S(1)} %copy-done.16, bf16[1024,1792]{1,0:T(8,128)(2,1)S(1)} %copy-done.13, f32[8,128]{1,0:T(8,128)S(1)} %get-tuple-element.34.refs_3_), custom_call_target="tpu_custom_call" | custom-call | flops 1879048192 | bytes 1835008 | tf_op jit(solution)/shard_map/pallas_call | solution.py:61
  22.0 4.4 %shard_map.85 = (bf16[512,896]{1,0:T(8,128)(2,1)S(1)}, f32[512,896]{1,0:T(8,128)S(1)}, f32[8,128]{1,0:T(8,128)S(1)}) custom-call(s32[9]{0:T(128)S(1)} %pad_add_fusion.1.refs_0_, bf16[1024,1024]{1,0:T(8,128)(2,1)S(1)} %collective-permute-done.refs_1_, bf16[1024,896]{1,0:T(8,128)(2,1)} %collective-permute-done.3.refs_2_, ...), custom_call_target="tpu_custom_call" | custom-call | flops 1879048192 | bytes 1835008 | tf_op jit(solution)/shard_map/pallas_call | solution.py:61
  26.4 1.2 copy-done.8
  27.6 0.9 copy-done.17
  28.6 0.5 slice.43
  29.7 0.5 convert_reduce_fusion
  30.3 0.4 select_reduce_fusion
  30.7 0.5 collective-permute-start.5
  31.1 0.1 select_reduce_fusion.2
  31.3 0.2 fusion.3.refs_5_.refs_2_
  31.5 0.1 fusion.1.refs_3_.refs_1_
  31.6 0.1 fusion.2.refs_4_.refs_2_
  31.8 1.5 copy-done.5
  33.2 0.2 shard_map.86
  33.4 3.2 %collective-permute-start.4 = (bf16[256,896]{1,0:T(8,128)(2,1)S(1)}, bf16[256,896]{1,0:T(8,128)(2,1)S(1)}, u32[]{:S(2)}, u32[]{:S(2)}) collective-permute-start(bf16[256,896]{1,0:T(8,128)(2,1)S(1)} %get-tuple-element.39), channel_id=1, source_target_pairs={{0,6},{1,3},{2,4},{3,1},{4,2},{5,7},{6,0},{7,5},{8,14},{9,11},{10,... | collective-permute-start | bytes 1376264 | tf_op jit(solution)/shard_map/ppermute | solution.py:345
  36.6 12.7 %collective-permute-done.5.refs_1_ = bf16[512,896]{1,0:T(8,128)(2,1)S(1)} collective-permute-done((bf16[512,896]{1,0:T(8,128)(2,1)}, bf16[512,896]{1,0:T(8,128)(2,1)S(1)}, u32[]{:S(2)}, u32[]{:S(2)}) %collective-permute-start.5) | collective-permute-done | bytes 917536 | tf_op jit(solution)/shard_map/ppermute | solution.py:345
  49.3 0.7 shard_map.87
  50.0 2.2 %collective-permute-start.6 = (bf16[256,896]{1,0:T(8,128)(2,1)S(1)}, bf16[256,896]{1,0:T(8,128)(2,1)S(1)}, u32[]{:S(2)}, u32[]{:S(2)}) collective-permute-start(bf16[256,896]{1,0:T(8,128)(2,1)S(1)} %get-tuple-element.44), channel_id=1, source_target_pairs={{0,6},{1,3},{2,4},{3,1},{4,2},{5,7},{6,0},{7,5},{8,14},{9,11},{10,... | collective-permute-start | bytes 1376264 | tf_op jit(solution)/shard_map/ppermute | solution.py:345
  52.2 7.5 %collective-permute-done.6.refs_3_ = bf16[256,896]{1,0:T(8,128)(2,1)S(1)} collective-permute-done((bf16[256,896]{1,0:T(8,128)(2,1)S(1)}, bf16[256,896]{1,0:T(8,128)(2,1)S(1)}, u32[]{:S(2)}, u32[]{:S(2)}) %collective-permute-start.6) | collective-permute-done | bytes 458784 | tf_op jit(solution)/shard_map/ppermute | solution.py:345
  59.7 0.7 shard_map.88
  60.3 2.2 %collective-permute-start.7 = (bf16[256,896]{1,0:T(8,128)(2,1)S(1)}, bf16[256,896]{1,0:T(8,128)(2,1)S(1)}, u32[]{:S(2)}, u32[]{:S(2)}) collective-permute-start(bf16[256,896]{1,0:T(8,128)(2,1)S(1)} %get-tuple-element.45), channel_id=1, source_target_pairs={{0,6},{1,3},{2,4},{3,1},{4,2},{5,7},{6,0},{7,5},{8,14},{9,11},{10,... | collective-permute-start | bytes 1376264 | tf_op jit(solution)/shard_map/ppermute | solution.py:345
  62.5 7.5 %collective-permute-done.7 = bf16[256,896]{1,0:T(8,128)(2,1)S(1)} collective-permute-done((bf16[256,896]{1,0:T(8,128)(2,1)S(1)}, bf16[256,896]{1,0:T(8,128)(2,1)S(1)}, u32[]{:S(2)}, u32[]{:S(2)}) %collective-permute-start.7) | collective-permute-done | bytes 458784 | tf_op jit(solution)/shard_map/ppermute | solution.py:345
  70.3 13.3 %collective-permute-done.8 = bf16[512,896]{1,0:T(8,128)(2,1)S(1)} collective-permute-done((bf16[512,896]{1,0:T(8,128)(2,1)S(1)}, bf16[512,896]{1,0:T(8,128)(2,1)S(1)}, u32[]{:S(2)}, u32[]{:S(2)}) %collective-permute-start.8) | collective-permute-done | bytes 917536 | tf_op jit(solution)/shard_map/ppermute | solution.py:345
  83.6 0.1 constant_dynamic-update-slice_fusion.refs_3_.refs_2_
  83.7 0.3 collective-permute-start.9
  84.0 3.8 %collective-permute-done.9.refs_4_.refs_3_ = bf16[1024,896]{1,0:T(8,128)(2,1)S(1)} collective-permute-done((bf16[1024,896]{1,0:T(8,128)(2,1)S(1)}, bf16[1024,896]{1,0:T(8,128)(2,1)S(1)}, u32[]{:S(2)}, u32[]{:S(2)}) %collective-permute-start.9) | collective-permute-done | bytes 1835040 | tf_op jit(solution)/shard_map/ppermute | solution.py:345
  87.8 2.0 %shard_map.89 = (bf16[256,1792]{1,0:T(8,128)(2,1)S(1)}, f32[8,128]{1,0:T(8,128)S(1)}) custom-call(s32[9]{0:T(128)S(1)} %pad_add_fusion.1.refs_0_, bf16[256,1024]{1,0:T(8,128)(2,1)S(1)} %fusion.1.refs_3_.refs_1_, bf16[256,1024]{1,0:T(8,128)(2,1)S(1)} %fusion.2.refs_4_.refs_2_, bf16[1024,896]{1,0:T(8,128)(2,1)S(1)} %constant_dynamic-update-slice_fusion.refs_3_.refs_2_, ...), custom_call_target="tpu_custom_call" | custom-call | flops 939524096 | bytes 3670016 | tf_op jit(solution)/shard_map/pallas_call | solution.py:61
  89.8 1.0 copy-done.10
  90.8 7.9 %all-to-all-start = ((bf16[16,16,1792]{2,1,0:T(8,128)(2,1)}), bf16[16,16,1792]{2,1,0:T(8,128)(2,1)S(1)}, u32[]{:S(2)}, u32[]{:S(2)}) async-start(bf16[16,16,1792]{2,1,0:T(8,128)(2,1)} %bitcast.18), calls=%async_computation | async-start | bytes 1835008 | tf_op jit(solution)/shard_map/all_to_all | solution.py:366
  98.7 1.5 copy-done.7
  100.2 2.0 %copy-done.14 = bf16[1792,1024]{1,0:T(8,128)(2,1)S(1)} copy-done((bf16[1792,1024]{1,0:T(8,128)(2,1)S(1)}, bf16[1792,1024]{1,0:T(8,128)(2,1)}, u32[]{:S(2)}) %copy-start.14) | copy-done | bytes 3670040
  102.2 5.0 %shard_map.90 = (f32[1024,1024]{1,0:T(8,128)S(1)}, f32[8,128]{1,0:T(8,128)S(1)}) custom-call(s32[9]{0:T(128)S(1)} %pad_add_fusion.1.refs_0_, bf16[1792,1024]{1,0:T(8,128)(2,1)S(1)} %copy-done.14, bf16[1024,896]{1,0:T(8,128)(2,1)S(1)} %constant_dynamic-update-slice_fusion.refs_3_.refs_2_, bf16[1024,896]{1,0:T(8,128)(2,1)S(1)} %copy-done.7, ...), custom_call_target="tpu_custom_call" | custom-call | flops 3758096384 | bytes 7340032 | tf_op jit(solution)/shard_map/pallas_call | solution.py:61
  107.3 2.0 %copy-done.1 = f32[1024,1024]{1,0:T(8,128)} copy-done((f32[1024,1024]{1,0:T(8,128)}, f32[1024,1024]{1,0:T(8,128)S(1)}, u32[]{:S(2)}) %copy-start.1) | copy-done | bytes 4194328
  109.3 6.0 %all-to-all-done.refs_0_ = bf16[16,16,1792]{2,1,0:T(8,128)(2,1)S(1)} async-done(((bf16[16,16,1792]{2,1,0:T(8,128)(2,1)}), bf16[16,16,1792]{2,1,0:T(8,128)(2,1)S(1)}, u32[]{:S(2)}, u32[]{:S(2)}) %all-to-all-start) | async-done | bytes 917536 | tf_op jit(solution)/shard_map/all_to_all | solution.py:366
  115.2 3.1 %copy-done = bf16[2,28672,64]{1,2,0:T(8,128)(2,1)S(1)} copy-done((bf16[2,28672,64]{1,2,0:T(8,128)(2,1)S(1)}, bf16[2,28672,64]{1,2,0:T(8,128)(2,1)}, u32[]{:S(2)}) %copy-start) | copy-done | bytes 7340056
  118.3 1.6 copy-done.3
  119.9 5.7 %shard_map.91 = (bf16[8,16,1024]{2,1,0:T(8,128)(2,1)}, f32[8,128]{1,0:T(8,128)}) custom-call(bf16[16,16,1792]{2,1,0:T(8,128)(2,1)S(1)} %all-to-all-done.refs_0_, bf16[128,28672]{1,0:T(8,128)(2,1)S(1)} %bitcast.15, bf16[128,8192]{1,0:T(8,128)(2,1)S(1)} %bitcast.16, f32[8,128]{1,0:T(8,128)S(1)} %get-tuple-element.49.refs_3_), custom_call_target="tpu_custom_call" | custom-call | flops 117440512 | bytes 7340032 | tf_op jit(solution)/shard_map/pallas_call | solution.py:61
  125.6 3.6 %all-to-all-start.1 = ((bf16[8,16,1024]{2,1,0:T(8,128)(2,1)}), bf16[8,16,1024]{2,1,0:T(8,128)(2,1)S(1)}, u32[]{:S(2)}, u32[]{:S(2)}) async-start(bf16[8,16,1024]{2,1,0:T(8,128)(2,1)} %get-tuple-element.50), calls=%async_computation.1 | async-start | bytes 524288 | tf_op jit(solution)/shard_map/all_to_all | solution.py:369
  129.4 7.4 %all-to-all-done.1 = bf16[8,16,1024]{2,1,0:T(8,128)(2,1)S(1)} async-done(((bf16[8,16,1024]{2,1,0:T(8,128)(2,1)}), bf16[8,16,1024]{2,1,0:T(8,128)(2,1)S(1)}, u32[]{:S(2)}, u32[]{:S(2)}) %all-to-all-start.1) | async-done | bytes 262176 | tf_op jit(solution)/shard_map/all_to_all | solution.py:369
  136.8 2.2 %copy-done.2 = f32[1024,1024]{1,0:T(8,128)S(1)} copy-done((f32[1024,1024]{1,0:T(8,128)S(1)}, f32[1024,1024]{1,0:T(8,128)}, u32[]{:S(2)}) %copy-start.2) | copy-done | bytes 4194328
  139.0 1.7 %shard_map.92 = (bf16[512,512]{1,0:T(8,128)(2,1)S(1)}, f32[512,512]{1,0:T(8,128)S(1)}, bf16[512,512]{1,0:T(8,128)(2,1)S(1)}, f32[512,512]{1,0:T(8,128)S(1)}, f32[8,128]{1,0:T(8,128)}) custom-call(s32[32]{0:T(128)S(1)} %pad_add_fusion.refs_0_, f32[1024,1024]{1,0:T(8,128)S(1)} %copy-done.2, bf16[1024,128]{1,0:T(8,128)(2,1)S(1)} %fusion.3.refs_5_.refs_2_, ...), custom_call_target="tpu_custom_call" | custom-call | flops 268435456 | bytes 10485760 | tf_op jit(solution)/shard_map/pallas_call | solution.py:61
  140.7 0.7 collective-permute-start.10
  141.5 9.6 %collective-permute-done.10 = bf16[512,512]{1,0:T(8,128)(2,1)S(1)} collective-permute-done((bf16[512,512]{1,0:T(8,128)(2,1)S(1)}, bf16[512,512]{1,0:T(8,128)(2,1)S(1)}, u32[]{:S(2)}, u32[]{:S(2)}) %collective-permute-start.10) | collective-permute-done | bytes 524320 | tf_op jit(solution)/shard_map/ppermute | solution.py:382
  151.1 0.2 convert_add_fusion.1
  151.4 0.2 convert_add_fusion
  151.6 1.8 %collective-permute-start.15 = (bf16[256,512]{1,0:T(8,128)(2,1)S(1)}, bf16[256,512]{1,0:T(8,128)(2,1)S(1)}, u32[]{:S(2)}, u32[]{:S(2)}) collective-permute-start(bf16[256,512]{1,0:T(8,128)(2,1)S(1)} %slice.82), channel_id=1, source_target_pairs={{0,96},{1,25},{8,104},{9,17},{16,112},{17,9},{24,120},{25,1},{32,6... | collective-permute-start | bytes 786440 | tf_op jit(solution)/shard_map/ppermute | solution.py:382
  153.4 4.3 %collective-permute-done.11 = bf16[256,512]{1,0:T(8,128)(2,1)S(1)} collective-permute-done((bf16[256,512]{1,0:T(8,128)(2,1)S(1)}, bf16[256,512]{1,0:T(8,128)(2,1)S(1)}, u32[]{:S(2)}, u32[]{:S(2)}) %collective-permute-start.11) | collective-permute-done | bytes 262176 | tf_op jit(solution)/shard_map/ppermute | solution.py:382
  157.9 0.3 collective-permute-start.12
  158.2 1.1 collective-permute-done.15
  159.4 0.6 collective-permute-start.16
  160.0 4.1 %collective-permute-done.12 = bf16[128,512]{1,0:T(8,128)(2,1)S(1)} collective-permute-done((bf16[128,512]{1,0:T(8,128)(2,1)S(1)}, bf16[128,512]{1,0:T(8,128)(2,1)S(1)}, u32[]{:S(2)}, u32[]{:S(2)}) %collective-permute-start.12) | collective-permute-done | bytes 131104 | tf_op jit(solution)/shard_map/ppermute | solution.py:382
  164.3 0.2 collective-permute-done.16
  164.5 2.0 %collective-permute-start.17 = (f32[64,512]{1,0:T(8,128)S(1)}, f32[64,512]{1,0:T(8,128)S(1)}, u32[]{:S(2)}, u32[]{:S(2)}) collective-permute-start(f32[64,512]{1,0:T(8,128)S(1)} %slice.67), channel_id=1, source_target_pairs={{0,24},{1,97},{8,16},{9,105},{16,8},{17,113},{24,0},{25,121},{32,5... | collective-permute-start | bytes 393224 | tf_op jit(solution)/shard_map/ppermute | solution.py:382
  166.5 2.8 %collective-permute-done.13 = f32[64,512]{1,0:T(8,128)S(1)} collective-permute-done((f32[64,512]{1,0:T(8,128)S(1)}, f32[64,512]{1,0:T(8,128)S(1)}, u32[]{:S(2)}, u32[]{:S(2)}) %collective-permute-start.13) | collective-permute-done | bytes 131104 | tf_op jit(solution)/shard_map/ppermute | solution.py:382
  169.3 1.5 collective-permute-done.17
  170.8 0.7 pad_maximum_fusion.1
  (69 shorter events, 1.3 us)
Async XLA Ops:
  0.0 11.8 %collective-permute-start = (bf16[1024,1024]{1,0:T(8,128)(2,1)}, bf16[1024,1024]{1,0:T(8,128)(2,1)S(1)}, u32[]{:S(2)}, u32[]{:S(2)}) collective-permute-start(bf16[1024,1024]{1,0:T(8,128)(2,1)} %refs_1_.4), channel_id=1, source_target_pairs={{0,1},{1,0},{2,3},{3,2},{4,5},{5,4},{6,7},{7,6},{8,9},{9,8},{10,11... | collective-permute-start | bytes 6291464 | tf_op jit(solution)/shard_map/ppermute | solution.py:345
  0.0 3.5 %copy-start.12 = (bf16[1024,1792]{1,0:T(8,128)(2,1)S(1)}, bf16[1024,1792]{1,0:T(8,128)(2,1)}, u32[]{:S(2)}) copy-start(bf16[1024,1792]{1,0:T(8,128)(2,1)} %refs_2_.3) | copy-start | bytes 11010052
  3.0 8.7 %collective-permute-start.1 = (bf16[1024,896]{1,0:T(8,128)(2,1)}, bf16[1024,896]{1,0:T(8,128)(2,1)}, u32[]{:S(2)}, u32[]{:S(2)}) collective-permute-start(bf16[1024,896]{1,0:T(8,128)(2,1)} %constant_dynamic-slice_fusion.1), channel_id=1, source_target_pairs={{0,1},{1,0},{2,3},{3,2},{4,5},{5,4},{6,7},{7,6},{8,9},{9,8},{10,11... | collective-permute-start | bytes 5505032 | tf_op jit(solution)/shard_map/ppermute | solution.py:345
  4.9 17.0 %collective-permute-start.3 = (bf16[1024,896]{1,0:T(8,128)(2,1)}, bf16[1024,896]{1,0:T(8,128)(2,1)}, u32[]{:S(2)}, u32[]{:S(2)}) collective-permute-start(bf16[1024,896]{1,0:T(8,128)(2,1)} %constant_dynamic-slice_fusion), channel_id=1, source_target_pairs={{0,1},{1,0},{2,3},{3,2},{4,5},{5,4},{6,7},{7,6},{8,9},{9,8},{10,11... | collective-permute-start | bytes 5505032 | tf_op jit(solution)/shard_map/ppermute | solution.py:345
  5.0 2.0 %copy-start.11 = (bf16[1024,1792]{1,0:T(8,128)(2,1)S(1)}, bf16[1024,1792]{1,0:T(8,128)(2,1)}, u32[]{:S(2)}) copy-start(bf16[1024,1792]{1,0:T(8,128)(2,1)} %refs_2_.2) | copy-start | bytes 11010052
  7.1 1.6 copy-start.15
  11.8 7.3 %copy-start.13 = (bf16[1024,1792]{1,0:T(8,128)(2,1)S(1)}, bf16[1024,1792]{1,0:T(8,128)(2,1)}, u32[]{:S(2)}) copy-start(bf16[1024,1792]{1,0:T(8,128)(2,1)} %refs_2_.3) | copy-start | bytes 11010052
  11.8 7.2 %copy-start.16 = (bf16[1024,1024]{1,0:T(8,128)(2,1)S(1)}, bf16[1024,1024]{1,0:T(8,128)(2,1)}, u32[]{:S(2)}) copy-start(bf16[1024,1024]{1,0:T(8,128)(2,1)} %refs_1_.4) | copy-start | bytes 6291460
  17.4 4.6 %copy-start.4 = (f32[512,896]{1,0:T(8,128)}, f32[512,896]{1,0:T(8,128)S(1)}, u32[]{:S(2)}) copy-start(f32[512,896]{1,0:T(8,128)S(1)} %get-tuple-element.32.refs_0_) | copy-start | bytes 5505028
  17.4 14.4 %collective-permute-start.2 = (bf16[512,896]{1,0:T(8,128)(2,1)}, bf16[512,896]{1,0:T(8,128)(2,1)S(1)}, u32[]{:S(2)}, u32[]{:S(2)}) collective-permute-start(bf16[512,896]{1,0:T(8,128)(2,1)} %get-tuple-element.33), channel_id=1, source_target_pairs={{0,2},{1,7},{2,0},{3,5},{4,6},{5,3},{6,4},{7,1},{8,10},{9,15},{10,... | collective-permute-start | bytes 2752520 | tf_op jit(solution)/shard_map/ppermute | solution.py:345
  22.0 7.7 %copy-start.18 = (s32[1024,1]{0,1:T(1,128)S(1)}, s32[1024,1]{0,1:T(1,128)}, u32[]{:S(2)}) copy-start(s32[1024,1]{0,1:T(1,128)} %param.12) | copy-start | bytes 12292
  22.0 8.3 %copy-start.19 = (s32[256]{0:T(256)S(1)}, s32[256]{0:T(256)}, u32[]{:S(2)}) copy-start(s32[256]{0:T(256)} %param.13) | copy-start | bytes 3076
  26.4 1.2 copy-start.8
  27.6 0.9 copy-start.17
  30.7 18.6 %collective-permute-start.5 = (bf16[512,896]{1,0:T(8,128)(2,1)}, bf16[512,896]{1,0:T(8,128)(2,1)S(1)}, u32[]{:S(2)}, u32[]{:S(2)}) collective-permute-start(bf16[512,896]{1,0:T(8,128)(2,1)} %copy-done.17), channel_id=1, source_target_pairs={{0,2},{1,7},{2,0},{3,5},{4,6},{5,3},{6,4},{7,1},{8,10},{9,15},{10,... | collective-permute-start | bytes 2752520 | tf_op jit(solution)/shard_map/ppermute | solution.py:345
  31.7 1.5 copy-start.5
  33.2 16.0 %copy-start.9 = (f32[512,896]{1,0:T(8,128)S(1)}, f32[512,896]{1,0:T(8,128)}, u32[]{:S(2)}) copy-start(f32[512,896]{1,0:T(8,128)} %copy-done.8) | copy-start | bytes 5505028
  33.4 18.8 %collective-permute-start.4 = (bf16[256,896]{1,0:T(8,128)(2,1)S(1)}, bf16[256,896]{1,0:T(8,128)(2,1)S(1)}, u32[]{:S(2)}, u32[]{:S(2)}) collective-permute-start(bf16[256,896]{1,0:T(8,128)(2,1)S(1)} %get-tuple-element.39), channel_id=1, source_target_pairs={{0,6},{1,3},{2,4},{3,1},{4,2},{5,7},{6,0},{7,5},{8,14},{9,11},{10,... | collective-permute-start | bytes 1376264 | tf_op jit(solution)/shard_map/ppermute | solution.py:345
  50.0 9.7 %collective-permute-start.6 = (bf16[256,896]{1,0:T(8,128)(2,1)S(1)}, bf16[256,896]{1,0:T(8,128)(2,1)S(1)}, u32[]{:S(2)}, u32[]{:S(2)}) collective-permute-start(bf16[256,896]{1,0:T(8,128)(2,1)S(1)} %get-tuple-element.44), channel_id=1, source_target_pairs={{0,6},{1,3},{2,4},{3,1},{4,2},{5,7},{6,0},{7,5},{8,14},{9,11},{10,... | collective-permute-start | bytes 1376264 | tf_op jit(solution)/shard_map/ppermute | solution.py:345
  60.3 9.7 %collective-permute-start.7 = (bf16[256,896]{1,0:T(8,128)(2,1)S(1)}, bf16[256,896]{1,0:T(8,128)(2,1)S(1)}, u32[]{:S(2)}, u32[]{:S(2)}) collective-permute-start(bf16[256,896]{1,0:T(8,128)(2,1)S(1)} %get-tuple-element.45), channel_id=1, source_target_pairs={{0,6},{1,3},{2,4},{3,1},{4,2},{5,7},{6,0},{7,5},{8,14},{9,11},{10,... | collective-permute-start | bytes 1376264 | tf_op jit(solution)/shard_map/ppermute | solution.py:345
  70.1 13.5 %collective-permute-start.8 = (bf16[512,896]{1,0:T(8,128)(2,1)S(1)}, bf16[512,896]{1,0:T(8,128)(2,1)S(1)}, u32[]{:S(2)}, u32[]{:S(2)}) collective-permute-start(bf16[512,896]{1,0:T(8,128)(2,1)S(1)} %pad_maximum_fusion), channel_id=1, source_target_pairs={{0,2},{1,7},{2,0},{3,5},{4,6},{5,3},{6,4},{7,1},{8,10},{9,15},{10,... | collective-permute-start | bytes 2752520 | tf_op jit(solution)/shard_map/ppermute | solution.py:345
  83.7 4.0 %collective-permute-start.9 = (bf16[1024,896]{1,0:T(8,128)(2,1)S(1)}, bf16[1024,896]{1,0:T(8,128)(2,1)S(1)}, u32[]{:S(2)}, u32[]{:S(2)}) collective-permute-start(bf16[1024,896]{1,0:T(8,128)(2,1)S(1)} %constant_dynamic-update-slice_fusion.refs_3_.refs_2_), channel_id=1, source_target_pairs={{0,1},{1,0},{2,3},{3,2},{4,5},{5,4},{6,7},{7,6},{8,9},{9,8},{10,11... | collective-permute-start | bytes 5505032 | tf_op jit(solution)/shard_map/ppermute | solution.py:345
  87.8 2.1 %copy-start.6 = (bf16[1024,896]{1,0:T(8,128)(2,1)}, bf16[1024,896]{1,0:T(8,128)(2,1)S(1)}, u32[]{:S(2)}) copy-start(bf16[1024,896]{1,0:T(8,128)(2,1)S(1)} %collective-permute-done.9.refs_4_.refs_3_) | copy-start | bytes 5505028
  89.8 1.0 copy-start.10
  90.8 24.4 %all-to-all-start = ((bf16[16,16,1792]{2,1,0:T(8,128)(2,1)}), bf16[16,16,1792]{2,1,0:T(8,128)(2,1)S(1)}, u32[]{:S(2)}, u32[]{:S(2)}) async-start(bf16[16,16,1792]{2,1,0:T(8,128)(2,1)} %bitcast.18), calls=%async_computation | async-start | bytes 1835008 | tf_op jit(solution)/shard_map/all_to_all | solution.py:366
  98.7 1.5 copy-start.7
  100.2 2.0 %copy-start.14 = (bf16[1792,1024]{1,0:T(8,128)(2,1)S(1)}, bf16[1792,1024]{1,0:T(8,128)(2,1)}, u32[]{:S(2)}) copy-start(bf16[1792,1024]{1,0:T(8,128)(2,1)} %refs_1_.5) | copy-start | bytes 11010052
  107.3 2.0 %copy-start.1 = (f32[1024,1024]{1,0:T(8,128)}, f32[1024,1024]{1,0:T(8,128)S(1)}, u32[]{:S(2)}) copy-start(f32[1024,1024]{1,0:T(8,128)S(1)} %get-tuple-element.47.refs_1_) | copy-start | bytes 12582916
  115.2 3.1 %copy-start = (bf16[2,28672,64]{1,2,0:T(8,128)(2,1)S(1)}, bf16[2,28672,64]{1,2,0:T(8,128)(2,1)}, u32[]{:S(2)}) copy-start(bf16[2,28672,64]{1,2,0:T(8,128)(2,1)} %param.14) | copy-start | bytes 22020100
  118.3 1.6 copy-start.3
  125.6 11.2 %all-to-all-start.1 = ((bf16[8,16,1024]{2,1,0:T(8,128)(2,1)}), bf16[8,16,1024]{2,1,0:T(8,128)(2,1)S(1)}, u32[]{:S(2)}, u32[]{:S(2)}) async-start(bf16[8,16,1024]{2,1,0:T(8,128)(2,1)} %get-tuple-element.50), calls=%async_computation.1 | async-start | bytes 524288 | tf_op jit(solution)/shard_map/all_to_all | solution.py:369
  136.8 2.2 %copy-start.2 = (f32[1024,1024]{1,0:T(8,128)S(1)}, f32[1024,1024]{1,0:T(8,128)}, u32[]{:S(2)}) copy-start(f32[1024,1024]{1,0:T(8,128)} %copy-done.1) | copy-start | bytes 12582916
  140.7 10.4 %collective-permute-start.10 = (bf16[512,512]{1,0:T(8,128)(2,1)S(1)}, bf16[512,512]{1,0:T(8,128)(2,1)S(1)}, u32[]{:S(2)}, u32[]{:S(2)}) collective-permute-start(bf16[512,512]{1,0:T(8,128)(2,1)S(1)} %get-tuple-element.52), channel_id=1, source_target_pairs={{0,96},{1,25},{8,104},{9,17},{16,112},{17,9},{24,120},{25,1},{32,6... | collective-permute-start | bytes 1572872 | tf_op jit(solution)/shard_map/ppermute | solution.py:382
  141.4 10.0 %collective-permute-start.14 = (bf16[512,512]{1,0:T(8,128)(2,1)S(1)}, bf16[512,512]{1,0:T(8,128)(2,1)S(1)}, u32[]{:S(2)}, u32[]{:S(2)}) collective-permute-start(bf16[512,512]{1,0:T(8,128)(2,1)S(1)} %get-tuple-element.54), channel_id=1, source_target_pairs={{0,32},{1,9},{8,40},{9,1},{16,48},{17,25},{24,56},{25,17},{32,0},{... | collective-permute-start | bytes 1572872 | tf_op jit(solution)/shard_map/ppermute | solution.py:382
  151.3 6.5 %collective-permute-start.11 = (bf16[256,512]{1,0:T(8,128)(2,1)S(1)}, bf16[256,512]{1,0:T(8,128)(2,1)S(1)}, u32[]{:S(2)}, u32[]{:S(2)}) collective-permute-start(bf16[256,512]{1,0:T(8,128)(2,1)S(1)} %slice.83), channel_id=1, source_target_pairs={{0,32},{1,9},{8,40},{9,1},{16,48},{17,25},{24,56},{25,17},{32,0},{... | collective-permute-start | bytes 786440 | tf_op jit(solution)/shard_map/ppermute | solution.py:382
  151.6 7.7 %collective-permute-start.15 = (bf16[256,512]{1,0:T(8,128)(2,1)S(1)}, bf16[256,512]{1,0:T(8,128)(2,1)S(1)}, u32[]{:S(2)}, u32[]{:S(2)}) collective-permute-start(bf16[256,512]{1,0:T(8,128)(2,1)S(1)} %slice.82), channel_id=1, source_target_pairs={{0,96},{1,25},{8,104},{9,17},{16,112},{17,9},{24,120},{25,1},{32,6... | collective-permute-start | bytes 786440 | tf_op jit(solution)/shard_map/ppermute | solution.py:382
  157.9 6.3 %collective-permute-start.12 = (bf16[128,512]{1,0:T(8,128)(2,1)S(1)}, bf16[128,512]{1,0:T(8,128)(2,1)S(1)}, u32[]{:S(2)}, u32[]{:S(2)}) collective-permute-start(bf16[128,512]{1,0:T(8,128)(2,1)S(1)} %slice.85), channel_id=1, source_target_pairs={{0,24},{1,97},{8,16},{9,105},{16,8},{17,113},{24,0},{25,121},{32,5... | collective-permute-start | bytes 393224 | tf_op jit(solution)/shard_map/ppermute | solution.py:382
  159.4 5.0 %collective-permute-start.16 = (bf16[128,512]{1,0:T(8,128)(2,1)S(1)}, bf16[128,512]{1,0:T(8,128)(2,1)S(1)}, u32[]{:S(2)}, u32[]{:S(2)}) collective-permute-start(bf16[128,512]{1,0:T(8,128)(2,1)S(1)} %slice.84), channel_id=1, source_target_pairs={{0,8},{1,33},{8,0},{9,41},{16,24},{17,49},{24,16},{25,57},{32,40},... | collective-permute-start | bytes 393224 | tf_op jit(solution)/shard_map/ppermute | solution.py:382
  164.2 5.0 %collective-permute-start.13 = (f32[64,512]{1,0:T(8,128)S(1)}, f32[64,512]{1,0:T(8,128)S(1)}, u32[]{:S(2)}, u32[]{:S(2)}) collective-permute-start(f32[64,512]{1,0:T(8,128)S(1)} %slice.61), channel_id=1, source_target_pairs={{0,8},{1,33},{8,0},{9,41},{16,24},{17,49},{24,16},{25,57},{32,40},... | collective-permute-start | bytes 393224 | tf_op jit(solution)/shard_map/ppermute | solution.py:382
  164.5 6.3 %collective-permute-start.17 = (f32[64,512]{1,0:T(8,128)S(1)}, f32[64,512]{1,0:T(8,128)S(1)}, u32[]{:S(2)}, u32[]{:S(2)}) collective-permute-start(f32[64,512]{1,0:T(8,128)S(1)} %slice.67), channel_id=1, source_target_pairs={{0,24},{1,97},{8,16},{9,105},{16,8},{17,113},{24,0},{25,121},{32,5... | collective-permute-start | bytes 393224 | tf_op jit(solution)/shard_map/ppermute | solution.py:382

commit v3 on v2

v3 whole, which is shorter than its diff:
```python
import jax
import jax.numpy as jnp
from jax import lax
from jax.experimental import pallas as pl
from jax.experimental.pallas import tpu as pltpu
from jax.sharding import Mesh, PartitionSpec as P

BF = jnp.bfloat16
F32 = jnp.float32
TILE = 256
STEP_TYPES = (BF, BF, BF, F32)
VM_SPLIT, VM_OWN, VM_SUMS, VM_LOW, VM_DOWN, VM_LAND = 20, 20, 20, 16, 20, 16
WIDTHS = (512, 384)
FLOPS = 2 * 10**10
STREAMS = (((0, 1, 2, 3), (2, 3, 0, 1)), ((1, 0, 3, 2), (3, 2, 1, 0)))


def flip_a(v):
    return v ^ 1


def flip_b(v):
    return 3 - v


def gray(v):
    return v ^ (v >> 1)


def hid_perm(dims):
    pairs = []
    for x in range(4):
        for z in range(4):
            for k in range(2):
                move = flip_b if dims[k] % 2 == 0 else flip_a
                to = (move(x), z) if dims[k] < 2 else (x, move(z))
                pairs.append(((x * 4 + z) * 2 + k, (to[0] * 4 + to[1]) * 2 + k))
    return pairs


def dot(a, b):
    return jnp.dot(a, b, preferred_element_type=F32)


def take(ref, table, start, count, rows):
    return jnp.concatenate(
        [ref[pl.ds(pl.multiple_of(table[start + p] * rows, rows), rows), :] for p in range(count)], 0
    )


def call(body, grid, ins, outs, mib, after=(), table=None, flops=1):
    first = 0 if table is None else 1
    token_spec = pl.BlockSpec((8, 128), lambda *i: (0, 0))

    def kernel(*refs):
        used = refs[: first + len(ins)] + refs[first + len(ins) + len(after) :]
        used[first + len(ins) + len(outs)][...] = jnp.zeros((8, 128), F32)
        body(*used[: first + len(ins) + len(outs)], *used[first + len(ins) + len(outs) + 1 :])

    specs = [spec for _, spec in ins] + [pl.BlockSpec(memory_space=pl.ANY)] * len(after)
    args = [] if table is None else [table]
    args += [v for v, _ in ins] + list(after)
    return pl.pallas_call(
        kernel,
        out_shape=[jax.ShapeDtypeStruct(*o[0]) for o in outs]
        + [jax.ShapeDtypeStruct((8, 128), F32)],
        grid_spec=pltpu.PrefetchScalarGridSpec(
            num_scalar_prefetch=first,
            grid=(grid,),
            in_specs=specs,
            out_specs=[o[1] for o in outs] + [token_spec],
        ),
        compiler_params=pltpu.CompilerParams(
            vmem_limit_bytes=mib * 2**20, dimension_semantics=("arbitrary",)
        ),
        cost_estimate=pl.CostEstimate(flops=flops, bytes_accessed=1, transcendentals=0),
    )(*args)


def block_of(*shape):
    return pl.BlockSpec(shape, lambda *_: (0,) * len(shape))


def whole(v):
    return v, pl.BlockSpec(v.shape, lambda *_: (0,) * v.ndim)


def split_columns(table, gate, up, offset, count, after):
    depth = gate.shape[0]
    width = gate.shape[1] // 2

    def body(table, gate, up, out):
        out[0] = gate[:, offset : offset + count]
        out[1] = up[:, offset : offset + count]

    block = pl.BlockSpec((depth, width), lambda j, t: (0, 1 - t[0]))
    return call(
        body, 1, [(gate, block), (up, block)],
        [(((2, depth, count), BF), block_of(2, depth, count))],
        VM_SPLIT, after, table,
    )


def own_sums(table, tokens, gate, up, offset, count, after=()):
    rows, depth = tokens.shape
    width = gate.shape[1] // 2

    def body(table, tokens, gate, up, out):
        left = take(tokens, table, 1, 4, rows // 4)
        for i, weight in enumerate((gate, up)):
            for start in range(0, count, TILE):
                stop = min(start + TILE, count)
                out[i, :, start:stop] = dot(left, weight[:, offset + start : offset + stop])

    block = pl.BlockSpec((depth, width), lambda j, t: (0, t[0]))
    return call(
        body, 1, [whole(tokens), (gate, block), (up, block)],
        [(((2, rows, count), F32), block_of(2, rows, count))],
        VM_OWN, after, table,
    )


def add_sums(table, far_tokens, far, own, after=()):
    rows = far_tokens.shape[0]
    count = far.shape[2]
    half = rows // 2

    def body(table, far_tokens, far, own, sent, kept):
        left = take(far_tokens, table, 1, 4, rows // 4)
        for i in range(2):
            for start in range(0, count, TILE):
                at = slice(start, min(start + TILE, count))
                total = dot(left, far[i, :, at]) + own[i, :, at]
                kept[i, :, at] = total[:half]
                sent[i, :, at] = total[half:].astype(sent.dtype)

    shape = (2, half, count)
    return call(
        body, 1, [whole(far_tokens), whole(far), whole(own)],
        [((shape, BF), block_of(*shape)), ((shape, F32), block_of(*shape))],
        VM_SUMS, after, table,
    )


def add_halves(kept, arrived, after=()):
    two, rows, width = kept.shape
    half = rows // 2

    def body(kept_in, arrived, sent, kept):
        for i in range(2):
            total = kept_in[i] + arrived[i].astype(F32)
            kept[i] = total[:half]
            sent[i] = total[half:].astype(sent.dtype)

    shape = (two, half, width)
    return call(
        body, 1, [whole(kept), whole(arrived)],
        [((shape, BF), block_of(*shape)), ((shape, F32), block_of(*shape))],
        16, after, None, FLOPS,
    )


def activate(sums, arrived, after=()):
    two, rows, width = sums.shape

    def body(sums, arrived, out):
        gate, up = (sums[i] + arrived[i].astype(F32) for i in range(2))
        out[...] = (jax.nn.silu(gate) * up).astype(BF)

    return call(
        body, 1, [whole(sums), whole(arrived)],
        [(((rows, width), BF), block_of(rows, width))],
        12, after, None, FLOPS,
    )


def join(first, second, after=()):
    rows, width = first.shape

    def body(first, second, out):
        out[:rows] = first[...]
        out[rows:] = second[...]

    return call(
        body, 1, [whole(first), whole(second)],
        [(((2 * rows, width), BF), block_of(2 * rows, width))],
        12, after, None, FLOPS,
    )


def pack(table, selector, pairs):
    slots, rows = selector.shape
    half = sum(mine.shape[1] for mine, _ in pairs)

    def body(table, selector, *refs):
        out, start = refs[-1], 0
        for i, ref in enumerate(refs[:-1]):
            turn, count = i % 2, ref.shape[1]
            ordered = take(ref, table, 9 + 4 * turn, 4, rows // 4)
            value = dot(selector[...], ordered).astype(out.dtype)
            for side in range(2):
                @pl.when((table[0] ^ turn) == side)
                def _():
                    first = side * half + start
                    out[:, first : first + count] = value
            start += count * turn

    return call(
        body, 1, [whole(selector)] + [whole(v) for pair in pairs for v in pair],
        [(((slots, 2 * half), BF), block_of(slots, 2 * half))],
        20, (), table,
    )


def down(table, weight, pairs, after):
    depth, width = weight.shape
    rows = pairs[0].shape[0]
    half = depth // 2

    def body(table, weight, *refs):
        out = refs[-1]
        left = []
        for i, ref in enumerate(refs[:-1]):
            left.append(ref[...] if i % 2 == 0 else take(ref, table, 5, 4, rows // 4))
        for start in range(0, width, TILE):
            at = slice(start, start + TILE)
            total, offset = 0.0, 0
            for i, value in enumerate(left):
                side = table[0] if i % 2 == 0 else 1 - table[0]
                count = value.shape[1]
                first = pl.multiple_of(side * half + offset, 128)
                total = total + dot(value, weight[pl.ds(first, count), at])
                offset += count * (i % 2)
            out[:, at] = total

    return call(
        body, 1, [whole(weight)] + [whole(v) for v in pairs],
        [(((rows, width), F32), block_of(rows, width))],
        VM_DOWN, after, table,
    )


def low_rank(arrived, factor, after):
    groups, slots, width = arrived.shape
    ranks = factor.shape[0]

    def body(rows, factor, out):
        low = jnp.zeros((slots, ranks), F32)
        for h in range(groups):
            low = low + lax.dot_general(
                rows[h],
                factor[:, h * width : (h + 1) * width],
                (((1,), (1,)), ((), ())),
                preferred_element_type=F32,
            )
        out[...] = low

    return call(
        body, 1, [whole(arrived), whole(factor)],
        [(((slots, ranks), F32), block_of(slots, ranks))],
        VM_LOW, after,
    )


def up_project(low, factor, per_dev, pieces):
    slots, ranks = low.shape
    piece = factor.shape[1] // pieces

    def body(low, factor, out):
        total = low[...]
        row = lax.broadcasted_iota(jnp.int32, total.shape, 0) // (slots // per_dev)
        column = lax.broadcasted_iota(jnp.int32, total.shape, 1) // (ranks // per_dev)
        own = jnp.where(row == column, total, 0.0).astype(BF)
        for j in range(pieces):
            out[j] = dot(own, factor[:, j * piece : (j + 1) * piece]).astype(out.dtype)

    return call(
        body, 1, [whole(low), whole(factor)],
        [(((pieces, slots, piece), BF), block_of(pieces, slots, piece))],
        12,
    )


def halve(table, base):
    rows, columns = base.shape
    width = columns // 2
    count = 8
    block = rows // 2 // count
    half = block_of(rows // 2, width)

    def body(table, base, *outs):
        for stream in range(2):
            at = slice(stream * width, (stream + 1) * width)
            for ref, start in ((outs[2 * stream], count), (outs[2 * stream + 1], 0)):
                first = stream * 2 * count + start
                for p in range(count):
                    source = pl.multiple_of(table[first + p] * block, block)
                    ref[p * block : (p + 1) * block, :] = base[pl.ds(source, block), at].astype(
                        ref.dtype
                    )

    shape = (rows // 2, width)
    outs = [((shape, BF), half), ((shape, F32), half)] * 2
    return call(body, 1, [whole(base)], outs, 24, (), table)


def land_own(table, kept, arrived, landing, returned):
    half, width = kept[0].shape
    count = 8
    block = half // count

    def body(table, *refs):
        landing, returned = refs[4:6]
        for stream in range(2):
            first = (4 + 2 * stream) * count
            rows = dot(
                take(landing, table, first, count, block),
                returned[:, stream * width : (stream + 1) * width],
            )
            total = refs[stream][...] + refs[2 + stream][...].astype(F32)
            refs[6 + stream][...] = total + rows

    ins = [whole(v) for v in (*kept, *arrived, landing, returned)]
    outs = [(((half, width), F32), block_of(half, width))] * 2
    return call(body, 1, ins, outs, VM_LAND, (), table)


def land_other(table, kept, landings, returned):
    rows, width = kept[0].shape
    count = 8
    block, half = rows // count, rows // 2

    def body(table, *refs):
        for stream in range(2):
            first = (4 + 2 * stream) * count
            left = take(refs[2 + stream], table, first, count, block)
            total = refs[stream][...] + dot(left, refs[4 + stream][...])
            refs[6 + 2 * stream][...] = total[half:].astype(BF)
            refs[7 + 2 * stream][...] = total[:half]

    ins = [whole(v) for v in (*kept, *landings, *returned)]
    outs = [(((half, width), BF), block_of(half, width)), (((half, width), F32), block_of(half, width))]
    return call(body, 1, ins, outs * 2, VM_LAND, (), table)


def per_device(
    tokens, gate_weight, up_weight, down_weight, adapter_id, owner_slot, adapt_down, adapt_up
):
    x, z, y, c = (lax.axis_index(n) for n in ("x", "z", "y", "c"))
    row_count = tokens.shape[0]
    d_local = down_weight.shape[1]
    adapter_count = owner_slot.shape[0]
    per_dev, ff_count, rank = adapt_down.shape
    capacity = 2 * row_count // adapter_count
    slots = per_dev * capacity
    wid_axes, hid_axes = ("y", "c"), ("x", "z")
    wid_index, hid_index = y * 2 + c, x * 4 + z

    swap_perm = [(i, i ^ 1) for i in range(8)]
    first = (flip_a, flip_b)
    perm1 = [(v * 2 + k, first[k](v) * 2 + k) for v in range(4) for k in range(2)]
    perm2 = [(v * 2 + k, first[1 - k](v) * 2 + k) for v in range(4) for k in range(2)]

    gray_y = gray(y)
    low_y, high_y = gray_y & 1, gray_y >> 1
    four = jnp.arange(4, dtype=jnp.int32)

    def at_place(core):
        one, two = four >> 1, four & 1
        low = jnp.where(core == 0, one, two) ^ low_y
        high = jnp.where(core == 0, two, one) ^ high_y
        return low * 2 + high

    def place_of(core, blocks):
        low, high = (blocks >> 1) ^ low_y, (blocks & 1) ^ high_y
        return jnp.where(core == 0, low * 2 + high, high * 2 + low)

    home_blocks = at_place(c)
    table = jnp.concatenate([
        c[None], home_blocks, place_of(1 - c, home_blocks), place_of(c, four), place_of(1 - c, four)
    ])

    bits = jnp.stack([gray(x) >> 1, gray(x) & 1, gray(z) >> 1, gray(z) & 1])
    sixteen = jnp.arange(16, dtype=jnp.int32)
    land_tables, land_blocks = [], []
    for dims in STREAMS:
        found = []
        for d in range(4):
            shift = jnp.where(c == 0, 3 - dims[0].index(d), 3 - dims[1].index(d))
            found.append(((sixteen >> shift) & 1) ^ bits[d])
        at_x, at_z = gray(found[0] * 2 + found[1]), gray(found[2] * 2 + found[3])
        land_tables.append(place_of(c, at_x) * 4 + at_z)
        land_blocks.append(at_x * 4 + at_z)
    land_table = jnp.concatenate(land_tables + land_blocks)
    partners = []
    for dims in STREAMS:
        to = [
            jnp.where(
                (dims[k][0] < 2) == (v is x),
                flip_b(v) if dims[k][0] % 2 == 0 else flip_a(v),
                v,
            )
            for k in range(2)
            for v in (x, z)
        ]
        partners.append(jnp.where(c == 0, to[0] * 4 + to[1], to[2] * 4 + to[3]))
    place_index = jnp.stack([wid_index, hid_index, *partners]).astype(jnp.int32)
    (
        tokens, gate_weight, up_weight, table, land_table, place_index, adapter_id, owner_slot
    ) = lax.optimization_barrier((
        tokens, gate_weight, up_weight, table, land_table, place_index, adapter_id, owner_slot
    ))

    def selections(token):
        row_adapter = adapter_id[:, 0] + token[0, 0].astype(jnp.int32)
        adapter_range = jnp.arange(adapter_count, dtype=jnp.int32)
        row_slot = jnp.sum(
            jnp.where(row_adapter[:, None] == adapter_range[None, :], owner_slot[None, :], 0), axis=1
        )
        positions = jnp.arange(row_count, dtype=jnp.int32)
        earlier = (row_adapter[:, None] == row_adapter[None, :]) & (
            positions[None, :] < positions[:, None]
        )
        row_rank = jnp.sum(earlier.astype(jnp.int32), axis=1)
        shift = per_dev.bit_length() - 1
        owner_hid, owner_wid = row_slot >> (shift + 3), (row_slot >> shift) & 7
        place = (row_slot & (per_dev - 1)) * capacity + row_rank

        send_index = jnp.where(owner_wid == place_index[0:1], owner_hid * slots + place, -1)
        send_slots = jnp.arange(16 * slots, dtype=jnp.int32)[:, None]
        selector = (send_slots == send_index[None, :]).astype(BF)
        land_slots = jnp.arange(8 * slots, dtype=jnp.int32)[None, :]
        landings = []
        for i in range(3):
            index = jnp.where(owner_hid == place_index[1 + i : 2 + i], owner_wid * slots + place, -1)
            landings.append((index[:, None] == land_slots).astype(BF))
        return selector, landings

    down_factor = adapt_down.transpose(0, 2, 1).reshape(per_dev * rank, ff_count)
    up_factor = adapt_up.reshape(per_dev * rank, adapt_up.shape[2])

    swap, one, two = (
        lambda v, perm=perm: lax.ppermute(v, wid_axes, perm) for perm in (swap_perm, perm1, perm2)
    )
    far_tokens = swap(tokens)
    offsets = [sum(WIDTHS[:i]) for i in range(len(WIDTHS))]
    chunks = range(len(WIDTHS))
    sent, kept, hidden, theirs = ([None, None] for _ in range(4))
    weights = (gate_weight, up_weight)
    far, token = split_columns(table, *weights, offsets[0], WIDTHS[0], [])
    far = swap(far)
    token = [token, far_tokens]
    for i in chunks:
        own, token = own_sums(table, tokens, *weights, offsets[i], WIDTHS[i], token)
        this = far
        if i + 1 < len(WIDTHS):
            far, token = split_columns(
                table, *weights, offsets[i + 1], WIDTHS[i + 1], [token]
            )
            far = swap(far)
        sent[i], kept[i], token = add_sums(table, far_tokens, this, own, [token])
        token = [token]
    for i in chunks:
        sent[i], kept[i], token = add_halves(kept[i], one(sent[i]), token)
        token = [token]
    for i in chunks:
        hidden[i], token = activate(kept[i], two(sent[i]), token)
        token = [token]
        if i == 0:
            selector, landings = selections(token[0])
    for i in chunks:
        hidden[i], token = join(hidden[i], two(hidden[i]), token)
        token = [token]
    for i in chunks:
        hidden[i], token = join(hidden[i], one(hidden[i]), token)
        theirs[i] = swap(hidden[i])
        token = [token]
    pairs = [(hidden[i], theirs[i]) for i in chunks]
    packed, token = pack(table, selector, pairs)
    packed = packed.reshape(16, slots, packed.shape[1])
    arrived = lax.all_to_all(packed, hid_axes, split_axis=0, concat_axis=0, tiled=True)
    def cross(v, stream, step):
        perm = hid_perm([STREAMS[stream][k][step] for k in range(2)])
        return lax.ppermute(v, ("x", "z", "c"), perm)

    base, _ = down(table, down_weight, [v for pair in pairs for v in pair], [token])
    *ends, token = halve(land_table, base)
    kept = ends[1::2]
    sums = [cross(ends[2 * stream], stream, 0) for stream in range(2)]
    low, _ = low_rank(arrived, down_factor, [token])
    adapted, _ = up_project(low, up_factor, per_dev, 8)
    returned = lax.all_to_all(adapted, wid_axes, split_axis=0, concat_axis=0, tiled=True)
    returned = returned.reshape(8 * slots, d_local)
    width = d_local // 2
    others = [
        cross(returned[:, stream * width : (stream + 1) * width], stream, 0) for stream in range(2)
    ]
    *totals, _ = land_own(land_table, kept, sums, landings[0], returned)
    *ends, _ = land_other(land_table, totals, landings[1:], others)
    outs = []
    for stream in range(2):
        going, value = ends[2 * stream], ends[2 * stream + 1]
        for step in range(1, 4):
            if step > 1:
                half = value.shape[0] // 2
                going, value = value[half:].astype(STEP_TYPES[step]), value[:half]
            value = value + cross(going, stream, step).astype(F32)
        outs.append(value)
    return jnp.concatenate(outs, 1).astype(BF)


def solution(mesh):
    fine = Mesh(mesh.devices.reshape(4, 4, 4, 2), ("x", "z", "y", "c"))
    hid, wid = ("x", "z"), ("y", "c")
    return jax.shard_map(
        per_device,
        mesh=fine,
        in_specs=(
            P(None, wid),
            P(wid, hid),
            P(wid, hid),
            P(hid, wid),
            P(),
            P(),
            P(hid + wid, None, None),
            P(hid + wid, None, None),
        ),
        out_specs=P(hid, wid),
        check_vma=False,
    )
```

time: 172 us -> 150 us (0.87)
  waiting for transfers between devices: 81.8 us -> 53.5 us
  starting transfers between devices: 27.7 us -> 41 us
  local copies, waits for them, and re-layouts: 26 us -> 16.5 us
  other arithmetic: 3.07 us -> 5.23 us
    ppermute x10 -> x13, waiting for transfers between devices: 44.8 us -> 33.5 us  [per_device(): lax.ppermute(v, wid_axes, perm)]
    ppermute x8 -> x10, waiting for transfers between devices: 23.6 us -> 12.7 us  [cross(): return lax.ppermute(v, ('x', 'z', 'c'), perm)]
    ppermute x8 -> x10, starting transfers between devices: 5.66 us -> 14.4 us  [cross(): return lax.ppermute(v, ('x', 'z', 'c'), perm)]
    all_to_all x1, waiting for transfers between devices: 5.97 us -> 0.01 us  [per_device(): lax.all_to_all(packed, hid_axes, split_axis=0, concat_axis=0, tiled=True)]
    unnamed x45 -> x38, local copies, waits for them, and re-layouts: 20.8 us -> 15.2 us
    dynamic_slice x2 -> x0, local copies, waits for them, and re-layouts: 4.43 us -> none  [per_device(): lax.dynamic_slice_in_dim(w, (1 - c) * ff_half, ff_half, 1)]
    ppermute x10 -> x13, starting transfers between devices: 10.5 us -> 14.2 us  [per_device(): lax.ppermute(v, wid_axes, perm)]
    select_n x1, other arithmetic: 0.02 us -> 2.51 us  [selections(): jnp.where(owner_hid == place_index[1 + i:2 + i], owner_wid * slots + plac...]
  transfers between devices with their start and end apart: 20 -> 25, of which waited for: 14 -> 14; matrix products, arithmetic and copies ran while one was open for 4% -> 4% of each run, Pallas kernels for 13% -> 19%
where the time goes in v3:
time: 150 us; the launch traced here: 149 us
  waiting for transfers between devices  53.5 us (36%)
  starting transfers between devices  41 us (27%)
  Pallas kernels  32 us (21%)
  local copies, waits for them, and re-layouts  16.5 us (11%)
  other arithmetic  5.23 us (3%)
    ppermute x13, waiting for transfers between devices, per_device(): lax.ppermute(v, wid_axes, perm)  33.5 us
    pallas_call x21, Pallas kernels, call(): pl.pallas_call(kernel, out_shape=[jax.ShapeDtypeStruct(*o[0]) for o in ou...  32 us
    unnamed x38, local copies, waits for them, and re-layouts  15.2 us
    ppermute x10, starting transfers between devices, cross(): return lax.ppermute(v, ('x', 'z', 'c'), perm)  14.4 us
    ppermute x13, starting transfers between devices, per_device(): lax.ppermute(v, wid_axes, perm)  14.2 us
    ppermute x10, waiting for transfers between devices, cross(): return lax.ppermute(v, ('x', 'z', 'c'), perm)  12.7 us
    all_to_all x1, starting transfers between devices, per_device(): lax.all_to_all(packed, hid_axes, split_axis=0, concat_axis=0, tiled=True)  8.05 us
    all_to_all x1, waiting for transfers between devices, per_device(): lax.all_to_all(adapted, wid_axes, split_axis=0, concat_axis=0, tiled=True)  7.33 us
  transfers between devices with their start and end apart: 25, of which 14 were waited for; matrix products, arithmetic and copies ran while one was open for 4% of the time, Pallas kernels for 19%

profile of v3, /device:TPU:0, one launch (start us, length us, event | category | flops | bytes accessed | tf_op | source)
XLA Modules:
  0.0 149.3 jit_solution(3292128514056964422)
XLA Ops:
  0.4 2.0 %copy-done = bf16[1024,1792]{1,0:T(8,128)(2,1)S(1)} copy-done((bf16[1024,1792]{1,0:T(8,128)(2,1)S(1)}, bf16[1024,1792]{1,0:T(8,128)(2,1)}, u32[]{:S(2)}) %copy-start) | copy-done | bytes 3670040
  2.4 2.0 %copy-done.2 = bf16[1024,1792]{1,0:T(8,128)(2,1)S(1)} copy-done((bf16[1024,1792]{1,0:T(8,128)(2,1)S(1)}, bf16[1024,1792]{1,0:T(8,128)(2,1)}, u32[]{:S(2)}) %copy-start.2) | copy-done | bytes 3670040
  4.5 0.8 shard_map.82
  5.3 0.6 collective-permute-start.1
  6.1 2.9 %shard_map.83 = (f32[2,1024,512]{2,1,0:T(8,128)S(1)}, f32[8,128]{1,0:T(8,128)S(1)}) custom-call(s32[17]{0:T(128)S(1)} %concatenate.10.refs_0_, bf16[1024,1024]{1,0:T(8,128)(2,1)S(1)} %copy-done.4, bf16[1024,1792]{1,0:T(8,128)(2,1)S(1)} %copy-done, bf16[1024,1792]{1,0:T(8,128)(2,1)S(1)} %copy-done.2, f32[8,128]{1,0:T(8,128)S(1)} %get-tuple-element.66.refs_4_, ...), custom_call_target="tpu_custom_call" | custom-call | flops 1 | bytes 1 | tf_op jit(solution)/shard_map/pallas_call | solution.py:63
  9.0 0.8 shard_map.84
  9.8 0.6 collective-permute-start.3
  10.4 2.9 %shard_map.85 = (bf16[2,512,512]{2,1,0:T(8,128)(2,1)S(1)}, f32[2,512,512]{2,1,0:T(8,128)S(1)}, f32[8,128]{1,0:T(8,128)S(1)}) custom-call(s32[17]{0:T(128)S(1)} %concatenate.10.refs_0_, bf16[1024,1024]{1,0:T(8,128)(2,1)S(1)} %collective-permute-done.refs_5_.refs_1_, bf16[2,1024,512]{2,1,0:T(8,128)(2,1)S(1)} %collective-permute-done.1.refs_2_, ...), custom_call_target="tpu_custom_call" | custom-call | flops 1 | bytes 1 | tf_op jit(solution)/shard_map/pallas_call | solution.py:63
  13.3 1.7 %collective-permute-start.2 = (bf16[2,512,512]{2,1,0:T(8,128)(2,1)S(1)}, bf16[2,512,512]{2,1,0:T(8,128)(2,1)S(1)}, u32[]{:S(2)}, u32[]{:S(2)}) collective-permute-start(bf16[2,512,512]{2,1,0:T(8,128)(2,1)S(1)} %get-tuple-element.71), channel_id=1, source_target_pairs={{0,2},{1,7},{2,0},{3,5},{4,6},{5,3},{6,4},{7,1},{8,10},{9,15},{10,... | collective-permute-start | bytes 3145736 | tf_op jit(solution)/shard_map/ppermute | solution.py:443
  15.0 0.7 fusion.18
  15.7 2.9 %shard_map.86 = (f32[2,1024,384]{2,1,0:T(8,128)S(1)}, f32[8,128]{1,0:T(8,128)S(1)}) custom-call(s32[17]{0:T(128)S(1)} %concatenate.10.refs_0_, bf16[1024,1024]{1,0:T(8,128)(2,1)S(1)} %copy-done.4, bf16[1024,1792]{1,0:T(8,128)(2,1)S(1)} %copy-done.1, bf16[1024,1792]{1,0:T(8,128)(2,1)S(1)} %copy-done.3, f32[8,128]{1,0:T(8,128)S(1)} %get-tuple-element.73.refs_4_), custom_call_target="tpu_custom_call" | custom-call | flops 1 | bytes 1 | tf_op jit(solution)/shard_map/pallas_call | solution.py:63
  18.6 2.9 %shard_map.87 = (bf16[2,512,384]{2,1,0:T(8,128)(2,1)S(1)}, f32[2,512,384]{2,1,0:T(8,128)S(1)}, f32[8,128]{1,0:T(8,128)S(1)}) custom-call(s32[17]{0:T(128)S(1)} %concatenate.10.refs_0_, bf16[1024,1024]{1,0:T(8,128)(2,1)S(1)} %collective-permute-done.refs_5_.refs_1_, bf16[2,1024,384]{2,1,0:T(8,128)(2,1)S(1)} %collective-permute-done.3.refs_2_, ...), custom_call_target="tpu_custom_call" | custom-call | flops 1 | bytes 1 | tf_op jit(solution)/shard_map/pallas_call | solution.py:63
  21.5 0.4 collective-permute-start.5
  21.9 6.2 %collective-permute-done.2.refs_1_ = bf16[2,512,512]{2,1,0:T(8,128)(2,1)S(1)} collective-permute-done((bf16[2,512,512]{2,1,0:T(8,128)(2,1)S(1)}, bf16[2,512,512]{2,1,0:T(8,128)(2,1)S(1)}, u32[]{:S(2)}, u32[]{:S(2)}) %collective-permute-start.2) | collective-permute-done | bytes 1048608 | tf_op jit(solution)/shard_map/ppermute | solution.py:443
  28.3 3.2 %collective-permute-start.4 = (bf16[2,256,512]{2,1,0:T(8,128)(2,1)S(1)}, bf16[2,256,512]{2,1,0:T(8,128)(2,1)S(1)}, u32[]{:S(2)}, u32[]{:S(2)}) collective-permute-start(bf16[2,256,512]{2,1,0:T(8,128)(2,1)S(1)} %get-tuple-element.78), channel_id=1, source_target_pairs={{0,6},{1,3},{2,4},{3,1},{4,2},{5,7},{6,0},{7,5},{8,14},{9,11},{10,... | collective-permute-start | bytes 1572872 | tf_op jit(solution)/shard_map/ppermute | solution.py:443
  31.5 10.3 %collective-permute-done.5.refs_1_ = bf16[2,512,384]{2,1,0:T(8,128)(2,1)S(1)} collective-permute-done((bf16[2,512,384]{2,1,0:T(8,128)(2,1)S(1)}, bf16[2,512,384]{2,1,0:T(8,128)(2,1)S(1)}, u32[]{:S(2)}, u32[]{:S(2)}) %collective-permute-start.5) | collective-permute-done | bytes 786464 | tf_op jit(solution)/shard_map/ppermute | solution.py:443
  42.0 3.3 %collective-permute-start.7 = (bf16[2,256,384]{2,1,0:T(8,128)(2,1)S(1)}, bf16[2,256,384]{2,1,0:T(8,128)(2,1)S(1)}, u32[]{:S(2)}, u32[]{:S(2)}) collective-permute-start(bf16[2,256,384]{2,1,0:T(8,128)(2,1)S(1)} %get-tuple-element.85), channel_id=1, source_target_pairs={{0,6},{1,3},{2,4},{3,1},{4,2},{5,7},{6,0},{7,5},{8,14},{9,11},{10,... | collective-permute-start | bytes 1179656 | tf_op jit(solution)/shard_map/ppermute | solution.py:443
  45.5 0.5 slice.47
  46.7 0.3 collective-permute-start.6
  47.0 4.1 %collective-permute-done.7.refs_1_ = bf16[2,256,384]{2,1,0:T(8,128)(2,1)S(1)} collective-permute-done((bf16[2,256,384]{2,1,0:T(8,128)(2,1)S(1)}, bf16[2,256,384]{2,1,0:T(8,128)(2,1)S(1)}, u32[]{:S(2)}, u32[]{:S(2)}) %collective-permute-start.7) | collective-permute-done | bytes 393248 | tf_op jit(solution)/shard_map/ppermute | solution.py:443
  51.2 3.3 %collective-permute-start.9 = (bf16[256,384]{1,0:T(8,128)(2,1)S(1)}, bf16[256,384]{1,0:T(8,128)(2,1)S(1)}, u32[]{:S(2)}, u32[]{:S(2)}) collective-permute-start(bf16[256,384]{1,0:T(8,128)(2,1)S(1)} %get-tuple-element.89.refs_0_), channel_id=1, source_target_pairs={{0,6},{1,3},{2,4},{3,1},{4,2},{5,7},{6,0},{7,5},{8,14},{9,11},{10,... | collective-permute-start | bytes 589832 | tf_op jit(solution)/shard_map/ppermute | solution.py:443
  54.6 0.5 collective-permute-start.8
  55.1 5.2 %collective-permute-done.9.refs_1_ = bf16[256,384]{1,0:T(8,128)(2,1)S(1)} collective-permute-done((bf16[256,384]{1,0:T(8,128)(2,1)S(1)}, bf16[256,384]{1,0:T(8,128)(2,1)S(1)}, u32[]{:S(2)}, u32[]{:S(2)}) %collective-permute-start.9) | collective-permute-done | bytes 196640 | tf_op jit(solution)/shard_map/ppermute | solution.py:443
  60.5 3.4 %collective-permute-done.8.refs_1_ = bf16[512,512]{1,0:T(8,128)(2,1)S(1)} collective-permute-done((bf16[512,512]{1,0:T(8,128)(2,1)S(1)}, bf16[512,512]{1,0:T(8,128)(2,1)S(1)}, u32[]{:S(2)}, u32[]{:S(2)}) %collective-permute-start.8) | collective-permute-done | bytes 524320 | tf_op jit(solution)/shard_map/ppermute | solution.py:443
  64.0 4.2 %collective-permute-done.11.refs_1_ = bf16[512,384]{1,0:T(8,128)(2,1)S(1)} collective-permute-done((bf16[512,384]{1,0:T(8,128)(2,1)S(1)}, bf16[512,384]{1,0:T(8,128)(2,1)S(1)}, u32[]{:S(2)}, u32[]{:S(2)}) %collective-permute-start.11) | collective-permute-done | bytes 393248 | tf_op jit(solution)/shard_map/ppermute | solution.py:443
  68.2 0.7 shard_map.95
  68.9 0.4 select_reduce_fusion
  69.3 0.5 convert_reduce_fusion
  69.8 2.5 %compare_select_fusion = (s32[1024]{0:T(1024)S(1)}, s32[1024]{0:T(1024)S(1)}, s32[1024]{0:T(1024)S(1)}, s32[1024]{0:T(1024)S(1)}) fusion(s32[1024]{0:T(1024)S(1)} %select_reduce_fusion, s32[]{:T(128)} %bitcast.15, s32[1024]{0:T(1024)S(1)} %convert_reduce_fusion, s32[]{:T(128)} %bitcast.14, s32[]{:T(128)} %bitcast.8, s32[]{:T(128)} %bitcast.7), kind=kLoop, calls=%fused_computation.28 | loop fusion | flops 18432 | bytes 24592 | tf_op jit(solution)/shard_map/jit(_where)/select_n | solution.py:435
  72.5 2.4 %shard_map.96 = (bf16[256,1792]{1,0:T(8,128)(2,1)S(1)}, f32[8,128]{1,0:T(8,128)S(1)}) custom-call(s32[17]{0:T(128)S(1)} %concatenate.10.refs_0_, bf16[256,1024]{1,0:T(8,128)(2,1)S(1)} %fusion.1.refs_1_, bf16[1024,512]{1,0:T(8,128)(2,1)S(1)} %get-tuple-element.92.refs_2_, bf16[1024,512]{1,0:T(8,128)(2,1)S(1)} %collective-permute-done.10.refs_3_, ...), custom_call_target="tpu_custom_call" | custom-call | flops 1 | bytes 1 | tf_op jit(solution)/shard_map/pallas_call | solution.py:63
  74.9 0.9 copy-done.7
  75.8 0.9 copy-done.14
  76.7 8.1 %all-to-all-start = ((bf16[16,16,1792]{2,1,0:T(8,128)(2,1)}), bf16[16,16,1792]{2,1,0:T(8,128)(2,1)S(1)}, u32[]{:S(2)}, u32[]{:S(2)}) async-start(bf16[16,16,1792]{2,1,0:T(8,128)(2,1)} %bitcast.21), calls=%async_computation | async-start | bytes 1835008 | tf_op jit(solution)/shard_map/all_to_all | solution.py:481
  85.0 2.0 %copy-done.6 = bf16[1792,1024]{1,0:T(8,128)(2,1)S(1)} copy-done((bf16[1792,1024]{1,0:T(8,128)(2,1)S(1)}, bf16[1792,1024]{1,0:T(8,128)(2,1)}, u32[]{:S(2)}) %copy-start.6) | copy-done | bytes 3670040
  87.0 1.1 copy-done.8
  88.2 1.1 copy-done.10
  89.3 0.7 copy-done.16
  90.0 5.5 %shard_map.97 = (f32[1024,1024]{1,0:T(8,128)S(1)}, f32[8,128]{1,0:T(8,128)}) custom-call(s32[17]{0:T(128)S(1)} %copy-done.16, bf16[1792,1024]{1,0:T(8,128)(2,1)S(1)} %copy-done.6, bf16[1024,512]{1,0:T(8,128)(2,1)S(1)} %get-tuple-element.92.refs_2_, bf16[1024,512]{1,0:T(8,128)(2,1)S(1)} %collective-permute-done.10.refs_3_, bf16[1024,384]{1,0:T(8,128)(2,1)S(1)} %copy-done.8, ...), custom_call_target="tpu_custom_call" | custom-call | flops 1 | bytes 1 | tf_op jit(solution)/shard_map/pallas_call | solution.py:63
  95.5 1.8 %shard_map.98 = (bf16[512,512]{1,0:T(8,128)(2,1)}, f32[512,512]{1,0:T(8,128)S(1)}, bf16[512,512]{1,0:T(8,128)(2,1)}, f32[512,512]{1,0:T(8,128)S(1)}, f32[8,128]{1,0:T(8,128)S(1)}) custom-call(s32[64]{0:T(128)S(1)} %pad_add_fusion.refs_0_, f32[1024,1024]{1,0:T(8,128)S(1)} %get-tuple-element.100.refs_1_), custom_call_target="tpu_custom_call" | custom-call | flops 1 | bytes 1 | tf_op jit(solution)/shard_map/pallas_call | solution.py:63
  97.2 1.0 copy-done.12
  98.2 3.1 %collective-permute-start.13 = (bf16[512,512]{1,0:T(8,128)(2,1)}, bf16[512,512]{1,0:T(8,128)(2,1)}, u32[]{:S(2)}, u32[]{:S(2)}) collective-permute-start(bf16[512,512]{1,0:T(8,128)(2,1)} %get-tuple-element.103), channel_id=1, source_target_pairs={{0,96},{1,25},{8,104},{9,17},{16,112},{17,9},{24,120},{25,1},{32,6... | collective-permute-start | bytes 1572872 | tf_op jit(solution)/shard_map/ppermute | solution.py:484
  101.4 0.2 collective-permute-start.14
  101.6 3.1 %copy-done.5 = bf16[2,28672,64]{1,2,0:T(8,128)(2,1)S(1)} copy-done((bf16[2,28672,64]{1,2,0:T(8,128)(2,1)S(1)}, bf16[2,28672,64]{1,2,0:T(8,128)(2,1)}, u32[]{:S(2)}) %copy-start.5) | copy-done | bytes 7340056
  104.7 2.4 %shard_map.99 = (f32[16,128]{1,0:T(8,128)S(1)}, f32[8,128]{1,0:T(8,128)}) custom-call(bf16[16,16,1792]{2,1,0:T(8,128)(2,1)S(1)} %all-to-all-done.refs_0_, bf16[128,28672]{1,0:T(8,128)(2,1)S(1)} %bitcast.17, f32[8,128]{1,0:T(8,128)S(1)} %get-tuple-element.106.refs_2_), custom_call_target="tpu_custom_call" | custom-call | flops 1 | bytes 1 | tf_op jit(solution)/shard_map/pallas_call | solution.py:63
  107.2 1.1 shard_map.100
  108.3 4.4 %all-to-all-start.1 = ((bf16[8,16,1024]{2,1,0:T(8,128)(2,1)}), bf16[8,16,1024]{2,1,0:T(8,128)(2,1)S(1)}, u32[]{:S(2)}, u32[]{:S(2)}) async-start(bf16[8,16,1024]{2,1,0:T(8,128)(2,1)} %get-tuple-element.108), calls=%async_computation.1 | async-start | bytes 524288 | tf_op jit(solution)/shard_map/all_to_all | solution.py:492
  112.9 7.3 %all-to-all-done.1 = bf16[8,16,1024]{2,1,0:T(8,128)(2,1)S(1)} async-done(((bf16[8,16,1024]{2,1,0:T(8,128)(2,1)}), bf16[8,16,1024]{2,1,0:T(8,128)(2,1)S(1)}, u32[]{:S(2)}, u32[]{:S(2)}) %all-to-all-start.1) | async-done | bytes 262176 | tf_op jit(solution)/shard_map/all_to_all | solution.py:492
  120.2 1.8 %collective-permute-start.15 = (bf16[128,512]{1,0:T(8,128)(2,1)S(1)}, bf16[128,512]{1,0:T(8,128)(2,1)S(1)}, u32[]{:S(2)}, u32[]{:S(2)}) collective-permute-start(bf16[128,512]{1,0:T(8,128)(2,1)S(1)} %get-tuple-element.122), channel_id=1, source_target_pairs={{0,96},{1,25},{8,104},{9,17},{16,112},{17,9},{24,120},{25,1},{32,6... | collective-permute-start | bytes 393224 | tf_op jit(solution)/shard_map/ppermute | solution.py:484
  122.0 0.2 collective-permute-start.16
  122.5 2.7 %shard_map.101 = (f32[512,512]{1,0:T(8,128)S(1)}, f32[512,512]{1,0:T(8,128)S(1)}, f32[8,128]{1,0:T(8,128)}) custom-call(s32[64]{0:T(128)S(1)} %pad_add_fusion.refs_0_, f32[512,512]{1,0:T(8,128)S(1)} %get-tuple-element.101.refs_1_, f32[512,512]{1,0:T(8,128)S(1)} %copy-done.13, bf16[512,512]{1,0:T(8,128)(2,1)} %collective-permute-done.13.refs_3_, ...), custom_call_target="tpu_custom_call" | custom-call | flops 1 | bytes 1 | tf_op jit(solution)/shard_map/pallas_call | solution.py:63
  125.2 1.3 collective-permute-done.15.refs_5_
  126.5 0.5 collective-permute-done.16.refs_6_
  127.0 1.5 shard_map.102
  128.7 2.5 %collective-permute-start.20 = (bf16[256,512]{1,0:T(8,128)(2,1)S(1)}, bf16[256,512]{1,0:T(8,128)(2,1)S(1)}, u32[]{:S(2)}, u32[]{:S(2)}) collective-permute-start(bf16[256,512]{1,0:T(8,128)(2,1)S(1)} %get-tuple-element.114), channel_id=1, source_target_pairs={{0,96},{1,25},{8,104},{9,17},{16,112},{17,9},{24,120},{25,1},{32,6... | collective-permute-start | bytes 786440 | tf_op jit(solution)/shard_map/ppermute | solution.py:484
  131.2 3.7 %collective-permute-done.17 = bf16[256,512]{1,0:T(8,128)(2,1)S(1)} collective-permute-done((bf16[256,512]{1,0:T(8,128)(2,1)S(1)}, bf16[256,512]{1,0:T(8,128)(2,1)S(1)}, u32[]{:S(2)}, u32[]{:S(2)}) %collective-permute-start.17) | collective-permute-done | bytes 262176 | tf_op jit(solution)/shard_map/ppermute | solution.py:484
  134.9 2.3 %collective-permute-start.18 = (bf16[128,512]{1,0:T(8,128)(2,1)S(1)}, bf16[128,512]{1,0:T(8,128)(2,1)S(1)}, u32[]{:S(2)}, u32[]{:S(2)}) collective-permute-start(bf16[128,512]{1,0:T(8,128)(2,1)S(1)} %slice.83), channel_id=1, source_target_pairs={{0,24},{1,97},{8,16},{9,105},{16,8},{17,113},{24,0},{25,121},{32,5... | collective-permute-start | bytes 393224 | tf_op jit(solution)/shard_map/ppermute | solution.py:484
  137.3 1.3 collective-permute-start.21
  138.6 2.6 %collective-permute-done.18 = bf16[128,512]{1,0:T(8,128)(2,1)S(1)} collective-permute-done((bf16[128,512]{1,0:T(8,128)(2,1)S(1)}, bf16[128,512]{1,0:T(8,128)(2,1)S(1)}, u32[]{:S(2)}, u32[]{:S(2)}) %collective-permute-start.18) | collective-permute-done | bytes 131104 | tf_op jit(solution)/shard_map/ppermute | solution.py:484
  141.2 0.6 collective-permute-start.19
  141.8 0.5 collective-permute-done.21
  142.4 2.1 %collective-permute-start.22 = (f32[64,512]{1,0:T(8,128)S(1)}, f32[64,512]{1,0:T(8,128)S(1)}, u32[]{:S(2)}, u32[]{:S(2)}) collective-permute-start(f32[64,512]{1,0:T(8,128)S(1)} %slice.71), channel_id=1, source_target_pairs={{0,24},{1,97},{8,16},{9,105},{16,8},{17,113},{24,0},{25,121},{32,5... | collective-permute-start | bytes 393224 | tf_op jit(solution)/shard_map/ppermute | solution.py:484
  144.5 1.8 %collective-permute-done.19 = f32[64,512]{1,0:T(8,128)S(1)} collective-permute-done((f32[64,512]{1,0:T(8,128)S(1)}, f32[64,512]{1,0:T(8,128)S(1)}, u32[]{:S(2)}, u32[]{:S(2)}) %collective-permute-start.19) | collective-permute-done | bytes 131104 | tf_op jit(solution)/shard_map/ppermute | solution.py:484
  146.3 2.4 %collective-permute-done.22 = f32[64,512]{1,0:T(8,128)S(1)} collective-permute-done((f32[64,512]{1,0:T(8,128)S(1)}, f32[64,512]{1,0:T(8,128)S(1)}, u32[]{:S(2)}, u32[]{:S(2)}) %collective-permute-start.22) | collective-permute-done | bytes 131104 | tf_op jit(solution)/shard_map/ppermute | solution.py:484
  148.7 0.7 pad_maximum_fusion
  (75 shorter events, 2.9 us)
Async XLA Ops:
  0.4 72.1 %copy-start.15 = (s32[17]{0:T(128)}, s32[17]{0:T(128)S(1)}, u32[]{:S(2)}) copy-start(s32[17]{0:T(128)S(1)} %concatenate.10.refs_0_) | copy-start | bytes 208
  0.4 5.5 %collective-permute-start = (bf16[1024,1024]{1,0:T(8,128)(2,1)}, bf16[1024,1024]{1,0:T(8,128)(2,1)S(1)}, u32[]{:S(2)}, u32[]{:S(2)}) collective-permute-start(bf16[1024,1024]{1,0:T(8,128)(2,1)} %refs_1_.4), channel_id=1, source_target_pairs={{0,1},{1,0},{2,3},{3,2},{4,5},{5,4},{6,7},{7,6},{8,9},{9,8},{10,11... | collective-permute-start | bytes 6291464 | tf_op jit(solution)/shard_map/ppermute | solution.py:443
  0.4 2.0 %copy-start = (bf16[1024,1792]{1,0:T(8,128)(2,1)S(1)}, bf16[1024,1792]{1,0:T(8,128)(2,1)}, u32[]{:S(2)}) copy-start(bf16[1024,1792]{1,0:T(8,128)(2,1)} %refs_2_.3) | copy-start | bytes 11010052
  2.4 2.0 %copy-start.2 = (bf16[1024,1792]{1,0:T(8,128)(2,1)S(1)}, bf16[1024,1792]{1,0:T(8,128)(2,1)}, u32[]{:S(2)}) copy-start(bf16[1024,1792]{1,0:T(8,128)(2,1)} %refs_3_.1) | copy-start | bytes 11010052
  4.5 1.6 %copy-start.4 = (bf16[1024,1024]{1,0:T(8,128)(2,1)S(1)}, bf16[1024,1024]{1,0:T(8,128)(2,1)}, u32[]{:S(2)}) copy-start(bf16[1024,1024]{1,0:T(8,128)(2,1)} %refs_1_.4) | copy-start | bytes 6291460
  5.3 5.1 %collective-permute-start.1 = (bf16[2,1024,512]{2,1,0:T(8,128)(2,1)S(1)}, bf16[2,1024,512]{2,1,0:T(8,128)(2,1)S(1)}, u32[]{:S(2)}, u32[]{:S(2)}) collective-permute-start(bf16[2,1024,512]{2,1,0:T(8,128)(2,1)S(1)} %get-tuple-element.65), channel_id=1, source_target_pairs={{0,1},{1,0},{2,3},{3,2},{4,5},{5,4},{6,7},{7,6},{8,9},{9,8},{10,11... | collective-permute-start | bytes 6291464 | tf_op jit(solution)/shard_map/ppermute | solution.py:443
  9.8 8.8 %collective-permute-start.3 = (bf16[2,1024,384]{2,1,0:T(8,128)(2,1)S(1)}, bf16[2,1024,384]{2,1,0:T(8,128)(2,1)S(1)}, u32[]{:S(2)}, u32[]{:S(2)}) collective-permute-start(bf16[2,1024,384]{2,1,0:T(8,128)(2,1)S(1)} %get-tuple-element.72), channel_id=1, source_target_pairs={{0,1},{1,0},{2,3},{3,2},{4,5},{5,4},{6,7},{7,6},{8,9},{9,8},{10,11... | collective-permute-start | bytes 4718600 | tf_op jit(solution)/shard_map/ppermute | solution.py:443
  10.4 5.3 %copy-start.1 = (bf16[1024,1792]{1,0:T(8,128)(2,1)S(1)}, bf16[1024,1792]{1,0:T(8,128)(2,1)}, u32[]{:S(2)}) copy-start(bf16[1024,1792]{1,0:T(8,128)(2,1)} %refs_2_.3) | copy-start | bytes 11010052
  10.4 5.3 %copy-start.3 = (bf16[1024,1792]{1,0:T(8,128)(2,1)S(1)}, bf16[1024,1792]{1,0:T(8,128)(2,1)}, u32[]{:S(2)}) copy-start(bf16[1024,1792]{1,0:T(8,128)(2,1)} %refs_3_.1) | copy-start | bytes 11010052
  13.3 14.9 %collective-permute-start.2 = (bf16[2,512,512]{2,1,0:T(8,128)(2,1)S(1)}, bf16[2,512,512]{2,1,0:T(8,128)(2,1)S(1)}, u32[]{:S(2)}, u32[]{:S(2)}) collective-permute-start(bf16[2,512,512]{2,1,0:T(8,128)(2,1)S(1)} %get-tuple-element.71), channel_id=1, source_target_pairs={{0,2},{1,7},{2,0},{3,5},{4,6},{5,3},{6,4},{7,1},{8,10},{9,15},{10,... | collective-permute-start | bytes 3145736 | tf_op jit(solution)/shard_map/ppermute | solution.py:443
  21.5 20.3 %collective-permute-start.5 = (bf16[2,512,384]{2,1,0:T(8,128)(2,1)S(1)}, bf16[2,512,384]{2,1,0:T(8,128)(2,1)S(1)}, u32[]{:S(2)}, u32[]{:S(2)}) collective-permute-start(bf16[2,512,384]{2,1,0:T(8,128)(2,1)S(1)} %get-tuple-element.80), channel_id=1, source_target_pairs={{0,2},{1,7},{2,0},{3,5},{4,6},{5,3},{6,4},{7,1},{8,10},{9,15},{10,... | collective-permute-start | bytes 2359304 | tf_op jit(solution)/shard_map/ppermute | solution.py:443
  28.3 17.0 %collective-permute-start.4 = (bf16[2,256,512]{2,1,0:T(8,128)(2,1)S(1)}, bf16[2,256,512]{2,1,0:T(8,128)(2,1)S(1)}, u32[]{:S(2)}, u32[]{:S(2)}) collective-permute-start(bf16[2,256,512]{2,1,0:T(8,128)(2,1)S(1)} %get-tuple-element.78), channel_id=1, source_target_pairs={{0,6},{1,3},{2,4},{3,1},{4,2},{5,7},{6,0},{7,5},{8,14},{9,11},{10,... | collective-permute-start | bytes 1572872 | tf_op jit(solution)/shard_map/ppermute | solution.py:443
  42.0 9.1 %collective-permute-start.7 = (bf16[2,256,384]{2,1,0:T(8,128)(2,1)S(1)}, bf16[2,256,384]{2,1,0:T(8,128)(2,1)S(1)}, u32[]{:S(2)}, u32[]{:S(2)}) collective-permute-start(bf16[2,256,384]{2,1,0:T(8,128)(2,1)S(1)} %get-tuple-element.85), channel_id=1, source_target_pairs={{0,6},{1,3},{2,4},{3,1},{4,2},{5,7},{6,0},{7,5},{8,14},{9,11},{10,... | collective-permute-start | bytes 1179656 | tf_op jit(solution)/shard_map/ppermute | solution.py:443
  45.3 1.6 %copy-start.17 = (s32[1024,1]{0,1:T(1,128)S(1)}, s32[1024,1]{0,1:T(1,128)}, u32[]{:S(2)}) copy-start(s32[1024,1]{0,1:T(1,128)} %param.12) | copy-start | bytes 12292
  46.7 7.9 %collective-permute-start.6 = (bf16[256,512]{1,0:T(8,128)(2,1)S(1)}, bf16[256,512]{1,0:T(8,128)(2,1)S(1)}, u32[]{:S(2)}, u32[]{:S(2)}) collective-permute-start(bf16[256,512]{1,0:T(8,128)(2,1)S(1)} %get-tuple-element.83.refs_0_), channel_id=1, source_target_pairs={{0,6},{1,3},{2,4},{3,1},{4,2},{5,7},{6,0},{7,5},{8,14},{9,11},{10,... | collective-permute-start | bytes 786440 | tf_op jit(solution)/shard_map/ppermute | solution.py:443
  51.2 9.1 %collective-permute-start.9 = (bf16[256,384]{1,0:T(8,128)(2,1)S(1)}, bf16[256,384]{1,0:T(8,128)(2,1)S(1)}, u32[]{:S(2)}, u32[]{:S(2)}) collective-permute-start(bf16[256,384]{1,0:T(8,128)(2,1)S(1)} %get-tuple-element.89.refs_0_), channel_id=1, source_target_pairs={{0,6},{1,3},{2,4},{3,1},{4,2},{5,7},{6,0},{7,5},{8,14},{9,11},{10,... | collective-permute-start | bytes 589832 | tf_op jit(solution)/shard_map/ppermute | solution.py:443
  54.6 9.3 %collective-permute-start.8 = (bf16[512,512]{1,0:T(8,128)(2,1)S(1)}, bf16[512,512]{1,0:T(8,128)(2,1)S(1)}, u32[]{:S(2)}, u32[]{:S(2)}) collective-permute-start(bf16[512,512]{1,0:T(8,128)(2,1)S(1)} %get-tuple-element.88.refs_0_), channel_id=1, source_target_pairs={{0,2},{1,7},{2,0},{3,5},{4,6},{5,3},{6,4},{7,1},{8,10},{9,15},{10,... | collective-permute-start | bytes 1572872 | tf_op jit(solution)/shard_map/ppermute | solution.py:443
  60.4 7.9 %collective-permute-start.11 = (bf16[512,384]{1,0:T(8,128)(2,1)S(1)}, bf16[512,384]{1,0:T(8,128)(2,1)S(1)}, u32[]{:S(2)}, u32[]{:S(2)}) collective-permute-start(bf16[512,384]{1,0:T(8,128)(2,1)S(1)} %get-tuple-element.93.refs_0_), channel_id=1, source_target_pairs={{0,2},{1,7},{2,0},{3,5},{4,6},{5,3},{6,4},{7,1},{8,10},{9,15},{10,... | collective-permute-start | bytes 1179656 | tf_op jit(solution)/shard_map/ppermute | solution.py:443
  63.9 8.5 %collective-permute-start.10 = (bf16[1024,512]{1,0:T(8,128)(2,1)S(1)}, bf16[1024,512]{1,0:T(8,128)(2,1)S(1)}, u32[]{:S(2)}, u32[]{:S(2)}) collective-permute-start(bf16[1024,512]{1,0:T(8,128)(2,1)S(1)} %get-tuple-element.92.refs_2_), channel_id=1, source_target_pairs={{0,1},{1,0},{2,3},{3,2},{4,5},{5,4},{6,7},{7,6},{8,9},{9,8},{10,11... | collective-permute-start | bytes 3145736 | tf_op jit(solution)/shard_map/ppermute | solution.py:443
  68.2 0.7 copy-start.18
  68.9 3.5 %collective-permute-start.12 = (bf16[1024,384]{1,0:T(8,128)(2,1)S(1)}, bf16[1024,384]{1,0:T(8,128)(2,1)S(1)}, u32[]{:S(2)}, u32[]{:S(2)}) collective-permute-start(bf16[1024,384]{1,0:T(8,128)(2,1)S(1)} %get-tuple-element.95.refs_4_), channel_id=1, source_target_pairs={{0,1},{1,0},{2,3},{3,2},{4,5},{5,4},{6,7},{7,6},{8,9},{9,8},{10,11... | collective-permute-start | bytes 2359304 | tf_op jit(solution)/shard_map/ppermute | solution.py:443
  72.4 2.4 %copy-start.9 = (bf16[1024,384]{1,0:T(8,128)(2,1)}, bf16[1024,384]{1,0:T(8,128)(2,1)S(1)}, u32[]{:S(2)}) copy-start(bf16[1024,384]{1,0:T(8,128)(2,1)S(1)} %collective-permute-done.12.refs_5_) | copy-start | bytes 2359300
  74.9 0.9 copy-start.7
  75.8 0.9 copy-start.14
  76.7 24.9 %all-to-all-start = ((bf16[16,16,1792]{2,1,0:T(8,128)(2,1)}), bf16[16,16,1792]{2,1,0:T(8,128)(2,1)S(1)}, u32[]{:S(2)}, u32[]{:S(2)}) async-start(bf16[16,16,1792]{2,1,0:T(8,128)(2,1)} %bitcast.21), calls=%async_computation | async-start | bytes 1835008 | tf_op jit(solution)/shard_map/all_to_all | solution.py:481
  85.0 2.0 %copy-start.6 = (bf16[1792,1024]{1,0:T(8,128)(2,1)S(1)}, bf16[1792,1024]{1,0:T(8,128)(2,1)}, u32[]{:S(2)}) copy-start(bf16[1792,1024]{1,0:T(8,128)(2,1)} %refs_1_.5) | copy-start | bytes 11010052
  87.0 1.1 copy-start.8
  88.2 1.1 copy-start.10
  89.3 0.7 copy-start.16
  97.2 1.0 copy-start.12
  98.2 24.2 %collective-permute-start.13 = (bf16[512,512]{1,0:T(8,128)(2,1)}, bf16[512,512]{1,0:T(8,128)(2,1)}, u32[]{:S(2)}, u32[]{:S(2)}) collective-permute-start(bf16[512,512]{1,0:T(8,128)(2,1)} %get-tuple-element.103), channel_id=1, source_target_pairs={{0,96},{1,25},{8,104},{9,17},{16,112},{17,9},{24,120},{25,1},{32,6... | collective-permute-start | bytes 1572872 | tf_op jit(solution)/shard_map/ppermute | solution.py:484
  101.4 21.1 %collective-permute-start.14 = (bf16[512,512]{1,0:T(8,128)(2,1)}, bf16[512,512]{1,0:T(8,128)(2,1)}, u32[]{:S(2)}, u32[]{:S(2)}) collective-permute-start(bf16[512,512]{1,0:T(8,128)(2,1)} %get-tuple-element.104), channel_id=1, source_target_pairs={{0,32},{1,9},{8,40},{9,1},{16,48},{17,25},{24,56},{25,17},{32,0},{... | collective-permute-start | bytes 1572872 | tf_op jit(solution)/shard_map/ppermute | solution.py:484
  101.6 3.1 %copy-start.5 = (bf16[2,28672,64]{1,2,0:T(8,128)(2,1)S(1)}, bf16[2,28672,64]{1,2,0:T(8,128)(2,1)}, u32[]{:S(2)}) copy-start(bf16[2,28672,64]{1,2,0:T(8,128)(2,1)} %param.14) | copy-start | bytes 22020100
  104.7 2.4 %copy-start.11 = (bf16[2,64,8192]{2,1,0:T(8,128)(2,1)S(1)}, bf16[2,64,8192]{2,1,0:T(8,128)(2,1)}, u32[]{:S(2)}) copy-start(bf16[2,64,8192]{2,1,0:T(8,128)(2,1)} %param.15) | copy-start | bytes 6291460
  107.2 15.3 %copy-start.13 = (f32[512,512]{1,0:T(8,128)S(1)}, f32[512,512]{1,0:T(8,128)}, u32[]{:S(2)}) copy-start(f32[512,512]{1,0:T(8,128)} %copy-done.12) | copy-start | bytes 3145732
  108.3 11.9 %all-to-all-start.1 = ((bf16[8,16,1024]{2,1,0:T(8,128)(2,1)}), bf16[8,16,1024]{2,1,0:T(8,128)(2,1)S(1)}, u32[]{:S(2)}, u32[]{:S(2)}) async-start(bf16[8,16,1024]{2,1,0:T(8,128)(2,1)} %get-tuple-element.108), calls=%async_computation.1 | async-start | bytes 524288 | tf_op jit(solution)/shard_map/all_to_all | solution.py:492
  120.2 6.3 %collective-permute-start.15 = (bf16[128,512]{1,0:T(8,128)(2,1)S(1)}, bf16[128,512]{1,0:T(8,128)(2,1)S(1)}, u32[]{:S(2)}, u32[]{:S(2)}) collective-permute-start(bf16[128,512]{1,0:T(8,128)(2,1)S(1)} %get-tuple-element.122), channel_id=1, source_target_pairs={{0,96},{1,25},{8,104},{9,17},{16,112},{17,9},{24,120},{25,1},{32,6... | collective-permute-start | bytes 393224 | tf_op jit(solution)/shard_map/ppermute | solution.py:484
  122.0 5.0 %collective-permute-start.16 = (bf16[128,512]{1,0:T(8,128)(2,1)S(1)}, bf16[128,512]{1,0:T(8,128)(2,1)S(1)}, u32[]{:S(2)}, u32[]{:S(2)}) collective-permute-start(bf16[128,512]{1,0:T(8,128)(2,1)S(1)} %get-tuple-element.121), channel_id=1, source_target_pairs={{0,32},{1,9},{8,40},{9,1},{16,48},{17,25},{24,56},{25,17},{32,0},{... | collective-permute-start | bytes 393224 | tf_op jit(solution)/shard_map/ppermute | solution.py:484
  128.4 6.4 %collective-permute-start.17 = (bf16[256,512]{1,0:T(8,128)(2,1)S(1)}, bf16[256,512]{1,0:T(8,128)(2,1)S(1)}, u32[]{:S(2)}, u32[]{:S(2)}) collective-permute-start(bf16[256,512]{1,0:T(8,128)(2,1)S(1)} %get-tuple-element.112), channel_id=1, source_target_pairs={{0,32},{1,9},{8,40},{9,1},{16,48},{17,25},{24,56},{25,17},{32,0},{... | collective-permute-start | bytes 786440 | tf_op jit(solution)/shard_map/ppermute | solution.py:484
  128.7 8.5 %collective-permute-start.20 = (bf16[256,512]{1,0:T(8,128)(2,1)S(1)}, bf16[256,512]{1,0:T(8,128)(2,1)S(1)}, u32[]{:S(2)}, u32[]{:S(2)}) collective-permute-start(bf16[256,512]{1,0:T(8,128)(2,1)S(1)} %get-tuple-element.114), channel_id=1, source_target_pairs={{0,96},{1,25},{8,104},{9,17},{16,112},{17,9},{24,120},{25,1},{32,6... | collective-permute-start | bytes 786440 | tf_op jit(solution)/shard_map/ppermute | solution.py:484
  134.9 6.3 %collective-permute-start.18 = (bf16[128,512]{1,0:T(8,128)(2,1)S(1)}, bf16[128,512]{1,0:T(8,128)(2,1)S(1)}, u32[]{:S(2)}, u32[]{:S(2)}) collective-permute-start(bf16[128,512]{1,0:T(8,128)(2,1)S(1)} %slice.83), channel_id=1, source_target_pairs={{0,24},{1,97},{8,16},{9,105},{16,8},{17,113},{24,0},{25,121},{32,5... | collective-permute-start | bytes 393224 | tf_op jit(solution)/shard_map/ppermute | solution.py:484
  137.3 5.0 %collective-permute-start.21 = (bf16[128,512]{1,0:T(8,128)(2,1)S(1)}, bf16[128,512]{1,0:T(8,128)(2,1)S(1)}, u32[]{:S(2)}, u32[]{:S(2)}) collective-permute-start(bf16[128,512]{1,0:T(8,128)(2,1)S(1)} %slice.82), channel_id=1, source_target_pairs={{0,8},{1,33},{8,0},{9,41},{16,24},{17,49},{24,16},{25,57},{32,40},... | collective-permute-start | bytes 393224 | tf_op jit(solution)/shard_map/ppermute | solution.py:484
  141.2 5.0 %collective-permute-start.19 = (f32[64,512]{1,0:T(8,128)S(1)}, f32[64,512]{1,0:T(8,128)S(1)}, u32[]{:S(2)}, u32[]{:S(2)}) collective-permute-start(f32[64,512]{1,0:T(8,128)S(1)} %slice.67), channel_id=1, source_target_pairs={{0,8},{1,33},{8,0},{9,41},{16,24},{17,49},{24,16},{25,57},{32,40},... | collective-permute-start | bytes 393224 | tf_op jit(solution)/shard_map/ppermute | solution.py:484
  142.4 6.3 %collective-permute-start.22 = (f32[64,512]{1,0:T(8,128)S(1)}, f32[64,512]{1,0:T(8,128)S(1)}, u32[]{:S(2)}, u32[]{:S(2)}) collective-permute-start(f32[64,512]{1,0:T(8,128)S(1)} %slice.71), channel_id=1, source_target_pairs={{0,24},{1,97},{8,16},{9,105},{16,8},{17,113},{24,0},{25,121},{32,5... | collective-permute-start | bytes 393224 | tf_op jit(solution)/shard_map/ppermute | solution.py:484

commit v4 on v3

--- a/solution.py
+++ b/solution.py
@@ -8,7 +8,7 @@
 BF = jnp.bfloat16
 F32 = jnp.float32
 TILE = 256
-STEP_TYPES = (BF, BF, BF, F32)
+STEP_TYPES = (BF, BF, BF, BF)
 VM_SPLIT, VM_OWN, VM_SUMS, VM_LOW, VM_DOWN, VM_LAND = 20, 20, 20, 16, 20, 16
 WIDTHS = (512, 384)
 FLOPS = 2 * 10**10
@@ -85,58 +85,55 @@
     return v, pl.BlockSpec(v.shape, lambda *_: (0,) * v.ndim)
 
 
-def split_columns(table, gate, up, offset, count, after):
-    depth = gate.shape[0]
-    width = gate.shape[1] // 2
-
-    def body(table, gate, up, out):
-        out[0] = gate[:, offset : offset + count]
-        out[1] = up[:, offset : offset + count]
+def split_columns(table, weight, offset, count, after):
+    depth, width = weight.shape[0], weight.shape[1] // 2
+
+    def body(table, weight, out):
+        out[...] = weight[:, offset : offset + count]
 
     block = pl.BlockSpec((depth, width), lambda j, t: (0, 1 - t[0]))
     return call(
-        body, 1, [(gate, block), (up, block)],
-        [(((2, depth, count), BF), block_of(2, depth, count))],
+        body, 1, [(weight, block)], [(((depth, count), BF), block_of(depth, count))],
         VM_SPLIT, after, table,
     )
 
 
-def own_sums(table, tokens, gate, up, offset, count, after=()):
+def own_sums(table, tokens, weight, offset, count, after=()):
     rows, depth = tokens.shape
-    width = gate.shape[1] // 2
-
-    def body(table, tokens, gate, up, out):
+    width = weight.shape[1] // 2
+
+    def body(table, tokens, weight, out):
         left = take(tokens, table, 1, 4, rows // 4)
-        for i, weight in enumerate((gate, up)):
-            for start in range(0, count, TILE):
-                stop = min(start + TILE, count)
-                out[i, :, start:stop] = dot(left, weight[:, offset + start : offset + stop])
+        for start in range(0, count, TILE):
+            stop = min(start + TILE, count)
+            out[:, start:stop] = dot(left, weight[:, offset + start : offset + stop])
 
     block = pl.BlockSpec((depth, width), lambda j, t: (0, t[0]))
     return call(
-        body, 1, [whole(tokens), (gate, block), (up, block)],
-        [(((2, rows, count), F32), block_of(2, rows, count))],
+        body, 1, [whole(tokens), (weight, block)],
+        [(((rows, count), F32), block_of(rows, count))],
         VM_OWN, after, table,
     )
 
 
 def add_sums(table, far_tokens, far, own, after=()):
     rows = far_tokens.shape[0]
-    count = far.shape[2]
+    count = far[0].shape[1]
     half = rows // 2
 
-    def body(table, far_tokens, far, own, sent, kept):
+    def body(table, far_tokens, *refs):
+        sent, kept = refs[4:]
         left = take(far_tokens, table, 1, 4, rows // 4)
         for i in range(2):
             for start in range(0, count, TILE):
                 at = slice(start, min(start + TILE, count))
-                total = dot(left, far[i, :, at]) + own[i, :, at]
+                total = dot(left, refs[i][:, at]) + refs[2 + i][:, at]
                 kept[i, :, at] = total[:half]
                 sent[i, :, at] = total[half:].astype(sent.dtype)
 
     shape = (2, half, count)
     return call(
-        body, 1, [whole(far_tokens), whole(far), whole(own)],
+        body, 1, [whole(v) for v in (far_tokens, *far, *own)],
         [((shape, BF), block_of(*shape)), ((shape, F32), block_of(*shape))],
         VM_SUMS, after, table,
     )
@@ -188,16 +185,27 @@
     )
 
 
-def pack(table, selector, pairs):
-    slots, rows = selector.shape
+def pack(table, row_slot, row_rank, pairs, per_dev, capacity, after):
+    rows = row_slot.shape[1]
+    slots = 16 * per_dev * capacity
     half = sum(mine.shape[1] for mine, _ in pairs)
-
-    def body(table, selector, *refs):
+    shift = per_dev.bit_length() - 1
+
+    def body(table, row_slot, row_rank, *refs):
         out, start = refs[-1], 0
+        slot = row_slot[...]
+        place = (slot & (per_dev - 1)) * capacity + row_rank[...]
+        index = jnp.where(
+            ((slot >> shift) & 7) == table[17],
+            (slot >> (shift + 3)) * (per_dev * capacity) + place,
+            -1,
+        )
+        at = lax.broadcasted_iota(jnp.int32, (slots, rows), 0)
+        selector = jnp.where(at == index, 1.0, 0.0).astype(BF)
         for i, ref in enumerate(refs[:-1]):
             turn, count = i % 2, ref.shape[1]
             ordered = take(ref, table, 9 + 4 * turn, 4, rows // 4)
-            value = dot(selector[...], ordered).astype(out.dtype)
+            value = dot(selector, ordered).astype(out.dtype)
             for side in range(2):
                 @pl.when((table[0] ^ turn) == side)
                 def _():
@@ -206,9 +214,9 @@
             start += count * turn
 
     return call(
-        body, 1, [whole(selector)] + [whole(v) for pair in pairs for v in pair],
+        body, 1, [whole(row_slot), whole(row_rank)] + [whole(v) for pair in pairs for v in pair],
         [(((slots, 2 * half), BF), block_of(slots, 2 * half))],
-        20, (), table,
+        20, after, table,
     )
 
 
@@ -377,7 +385,8 @@
 
     home_blocks = at_place(c)
     table = jnp.concatenate([
-        c[None], home_blocks, place_of(1 - c, home_blocks), place_of(c, four), place_of(1 - c, four)
+        c[None], home_blocks, place_of(1 - c, home_blocks), place_of(c, four), place_of(1 - c, four),
+        wid_index[None],
     ])
 
     bits = jnp.stack([gray(x) >> 1, gray(x) & 1, gray(z) >> 1, gray(z) & 1])
@@ -422,19 +431,16 @@
             positions[None, :] < positions[:, None]
         )
         row_rank = jnp.sum(earlier.astype(jnp.int32), axis=1)
+        return row_slot, row_rank
+
+    def landing_index(row_slot, row_rank):
         shift = per_dev.bit_length() - 1
         owner_hid, owner_wid = row_slot >> (shift + 3), (row_slot >> shift) & 7
         place = (row_slot & (per_dev - 1)) * capacity + row_rank
-
-        send_index = jnp.where(owner_wid == place_index[0:1], owner_hid * slots + place, -1)
-        send_slots = jnp.arange(16 * slots, dtype=jnp.int32)[:, None]
-        selector = (send_slots == send_index[None, :]).astype(BF)
-        land_slots = jnp.arange(8 * slots, dtype=jnp.int32)[None, :]
-        landings = []
-        for i in range(3):
-            index = jnp.where(owner_hid == place_index[1 + i : 2 + i], owner_wid * slots + place, -1)
-            landings.append((index[:, None] == land_slots).astype(BF))
-        return selector, landings
+        return [
+            jnp.where(owner_hid == place_index[1 + i : 2 + i], owner_wid * slots + place, -1)
+            for i in range(3)
+        ]
 
     down_factor = adapt_down.transpose(0, 2, 1).reshape(per_dev * rank, ff_count)
     up_factor = adapt_up.reshape(per_dev * rank, adapt_up.shape[2])
@@ -447,18 +453,17 @@
     chunks = range(len(WIDTHS))
     sent, kept, hidden, theirs = ([None, None] for _ in range(4))
     weights = (gate_weight, up_weight)
-    far, token = split_columns(table, *weights, offsets[0], WIDTHS[0], [])
-    far = swap(far)
-    token = [token, far_tokens]
+    token = []
     for i in chunks:
-        own, token = own_sums(table, tokens, *weights, offsets[i], WIDTHS[i], token)
-        this = far
-        if i + 1 < len(WIDTHS):
-            far, token = split_columns(
-                table, *weights, offsets[i + 1], WIDTHS[i + 1], [token]
-            )
-            far = swap(far)
-        sent[i], kept[i], token = add_sums(table, far_tokens, this, own, [token])
+        far, own = [None, None], [None, None]
+        for k in range(2):
+            far[k], token = split_columns(table, weights[k], offsets[i], WIDTHS[i], token)
+            far[k] = swap(far[k])
+            own[k], token = own_sums(table, tokens, weights[k], offsets[i], WIDTHS[i], [token])
+            token = [token]
+            if i == 0 and k == 0:
+                token.append(far_tokens)
+        sent[i], kept[i], token = add_sums(table, far_tokens, far, own, token)
         token = [token]
     for i in chunks:
         sent[i], kept[i], token = add_halves(kept[i], one(sent[i]), token)
@@ -467,7 +472,7 @@
         hidden[i], token = activate(kept[i], two(sent[i]), token)
         token = [token]
         if i == 0:
-            selector, landings = selections(token[0])
+            row_slot, row_rank = selections(token[0])
     for i in chunks:
         hidden[i], token = join(hidden[i], two(hidden[i]), token)
         token = [token]
@@ -476,7 +481,10 @@
         theirs[i] = swap(hidden[i])
         token = [token]
     pairs = [(hidden[i], theirs[i]) for i in chunks]
-    packed, token = pack(table, selector, pairs)
+    indices = landing_index(row_slot, row_rank)
+    packed, token = pack(
+        table, row_slot[None, :], row_rank[None, :], pairs, per_dev, capacity, indices
+    )
     packed = packed.reshape(16, slots, packed.shape[1])
     arrived = lax.all_to_all(packed, hid_axes, split_axis=0, concat_axis=0, tiled=True)
     def cross(v, stream, step):
@@ -489,6 +497,8 @@
     sums = [cross(ends[2 * stream], stream, 0) for stream in range(2)]
     low, _ = low_rank(arrived, down_factor, [token])
     adapted, _ = up_project(low, up_factor, per_dev, 8)
+    land_slots = jnp.arange(8 * slots, dtype=jnp.int32)[None, :]
+    landings = [(index[:, None] == land_slots).astype(BF) for index in indices]
     returned = lax.all_to_all(adapted, wid_axes, split_axis=0, concat_axis=0, tiled=True)
     returned = returned.reshape(8 * slots, d_local)
     width = d_local // 2

time: 150 us -> 147 us (0.980)
  starting transfers between devices: 41 us -> 37.5 us
  local copies, waits for them, and re-layouts: 16.5 us -> 13.9 us
  Pallas kernels: 32 us -> 34.5 us
  waiting for transfers between devices: 53.5 us -> 55 us
    unnamed x38 -> x36, local copies, waits for them, and re-layouts: 15.2 us -> 12.6 us
    pallas_call x21 -> x25, Pallas kernels: 32 us -> 34.5 us  [call(): pl.pallas_call(kernel, out_shape=[jax.ShapeDtypeStruct(*o[0]) for o in ou...]
    ppermute x10, starting transfers between devices: 14.4 us -> 12.3 us  [cross(): return lax.ppermute(v, ('x', 'z', 'c'), perm)]
    ppermute x13 -> x15, starting transfers between devices: 14.2 us -> 13.9 us  [per_device(): lax.ppermute(v, wid_axes, perm)]
    ppermute x13 -> x15, waiting for transfers between devices: 33.5 us -> 33.3 us  [per_device(): lax.ppermute(v, wid_axes, perm)]
  transfers between devices with their start and end apart: 25 -> 27, of which waited for: 14 -> 16; matrix products, arithmetic and copies ran while one was open for 4% -> 3% of each run, Pallas kernels for 19% -> 19%
where the time goes in v4:
time: 147 us
  waiting for transfers between devices  55 us (37%)
  starting transfers between devices  37.5 us (26%)
  Pallas kernels  34.5 us (23%)
  local copies, waits for them, and re-layouts  13.9 us (9%)
  other arithmetic  4.46 us (3%)
    pallas_call x25, Pallas kernels, call(): pl.pallas_call(kernel, out_shape=[jax.ShapeDtypeStruct(*o[0]) for o in ou...  34.5 us
    ppermute x15, waiting for transfers between devices, per_device(): lax.ppermute(v, wid_axes, perm)  33.3 us
    ppermute x15, starting transfers between devices, per_device(): lax.ppermute(v, wid_axes, perm)  13.9 us
    ppermute x10, waiting for transfers between devices, cross(): return lax.ppermute(v, ('x', 'z', 'c'), perm)  13.8 us
    unnamed x36, local copies, waits for them, and re-layouts  12.6 us
    ppermute x10, starting transfers between devices, cross(): return lax.ppermute(v, ('x', 'z', 'c'), perm)  12.3 us
    all_to_all x1, starting transfers between devices, per_device(): lax.all_to_all(packed, hid_axes, split_axis=0, concat_axis=0, tiled=True)  7.88 us
    all_to_all x1, waiting for transfers between devices, per_device(): lax.all_to_all(adapted, wid_axes, split_axis=0, concat_axis=0, tiled=True)  7.25 us
  transfers between devices with their start and end apart: 27, of which 16 were waited for; matrix products, arithmetic and copies ran while one was open for 3% of the time, Pallas kernels for 19%

profile of v4, /device:TPU:0, one launch (start us, length us, event | category | flops | bytes accessed | tf_op | source)
XLA Modules:
  0.0 146.6 jit_solution(10466517959939442195)
XLA Ops:
  0.4 2.0 %copy-done = bf16[1024,1792]{1,0:T(8,128)(2,1)S(1)} copy-done((bf16[1024,1792]{1,0:T(8,128)(2,1)S(1)}, bf16[1024,1792]{1,0:T(8,128)(2,1)}, u32[]{:S(2)}) %copy-start) | copy-done | bytes 3670040
  2.4 0.7 shard_map.82
  3.1 0.6 collective-permute-start.1
  4.0 1.8 %shard_map.83 = (f32[1024,512]{1,0:T(8,128)S(1)}, f32[8,128]{1,0:T(8,128)S(1)}) custom-call(s32[18]{0:T(128)S(1)} %concatenate.10.refs_0_, bf16[1024,1024]{1,0:T(8,128)(2,1)S(1)} %copy-done.3, bf16[1024,1792]{1,0:T(8,128)(2,1)S(1)} %copy-done, f32[8,128]{1,0:T(8,128)S(1)} %get-tuple-element.74.refs_3_), custom_call_target="tpu_custom_call" | custom-call | flops 1 | bytes 1 | tf_op jit(solution)/shard_map/pallas_call | solution.py:63
  5.9 0.7 shard_map.84
  6.5 0.6 collective-permute-start.2
  7.1 1.8 %shard_map.85 = (f32[1024,512]{1,0:T(8,128)S(1)}, f32[8,128]{1,0:T(8,128)S(1)}) custom-call(s32[18]{0:T(128)S(1)} %concatenate.10.refs_0_, bf16[1024,1024]{1,0:T(8,128)(2,1)S(1)} %copy-done.3, bf16[1024,1792]{1,0:T(8,128)(2,1)S(1)} %copy-done.2, f32[8,128]{1,0:T(8,128)S(1)} %get-tuple-element.78.refs_3_), custom_call_target="tpu_custom_call" | custom-call | flops 1 | bytes 1 | tf_op jit(solution)/shard_map/pallas_call | solution.py:63
  8.9 0.5 collective-permute-done.2.refs_3_
  9.4 2.9 %shard_map.86 = (bf16[2,512,512]{2,1,0:T(8,128)(2,1)S(1)}, f32[2,512,512]{2,1,0:T(8,128)S(1)}, f32[8,128]{1,0:T(8,128)S(1)}) custom-call(s32[18]{0:T(128)S(1)} %concatenate.10.refs_0_, bf16[1024,1024]{1,0:T(8,128)(2,1)S(1)} %collective-permute-done.refs_3_.refs_1_, bf16[1024,512]{1,0:T(8,128)(2,1)S(1)} %collective-permute-done.1.refs_2_, ...), custom_call_target="tpu_custom_call" | custom-call | flops 1 | bytes 1 | tf_op jit(solution)/shard_map/pallas_call | solution.py:63
  12.3 1.7 %collective-permute-start.3 = (bf16[2,512,512]{2,1,0:T(8,128)(2,1)S(1)}, bf16[2,512,512]{2,1,0:T(8,128)(2,1)S(1)}, u32[]{:S(2)}, u32[]{:S(2)}) collective-permute-start(bf16[2,512,512]{2,1,0:T(8,128)(2,1)S(1)} %get-tuple-element.82), channel_id=1, source_target_pairs={{0,2},{1,7},{2,0},{3,5},{4,6},{5,3},{6,4},{7,1},{8,10},{9,15},{10,... | collective-permute-start | bytes 3145736 | tf_op jit(solution)/shard_map/ppermute | solution.py:449
  14.0 0.7 shard_map.87
  14.7 1.6 %collective-permute-start.4 = (bf16[1024,384]{1,0:T(8,128)(2,1)S(1)}, bf16[1024,384]{1,0:T(8,128)(2,1)S(1)}, u32[]{:S(2)}, u32[]{:S(2)}) collective-permute-start(bf16[1024,384]{1,0:T(8,128)(2,1)S(1)} %get-tuple-element.84), channel_id=1, source_target_pairs={{0,1},{1,0},{2,3},{3,2},{4,5},{5,4},{6,7},{7,6},{8,9},{9,8},{10,11... | collective-permute-start | bytes 2359304 | tf_op jit(solution)/shard_map/ppermute | solution.py:449
  16.3 1.8 %shard_map.88 = (f32[1024,384]{1,0:T(8,128)S(1)}, f32[8,128]{1,0:T(8,128)S(1)}) custom-call(s32[18]{0:T(128)S(1)} %concatenate.10.refs_0_, bf16[1024,1024]{1,0:T(8,128)(2,1)S(1)} %copy-done.3, bf16[1024,1792]{1,0:T(8,128)(2,1)S(1)} %copy-done.1, f32[8,128]{1,0:T(8,128)S(1)} %get-tuple-element.85.refs_3_), custom_call_target="tpu_custom_call" | custom-call | flops 1 | bytes 1 | tf_op jit(solution)/shard_map/pallas_call | solution.py:63
  18.2 0.7 shard_map.89
  19.0 0.6 fusion.17
  19.6 1.8 %shard_map.90 = (f32[1024,384]{1,0:T(8,128)S(1)}, f32[8,128]{1,0:T(8,128)S(1)}) custom-call(s32[18]{0:T(128)S(1)} %concatenate.10.refs_0_, bf16[1024,1024]{1,0:T(8,128)(2,1)S(1)} %copy-done.3, bf16[1024,1792]{1,0:T(8,128)(2,1)S(1)} %copy-done.2, f32[8,128]{1,0:T(8,128)S(1)} %get-tuple-element.89.refs_3_), custom_call_target="tpu_custom_call" | custom-call | flops 1 | bytes 1 | tf_op jit(solution)/shard_map/pallas_call | solution.py:63
  21.4 2.9 %shard_map.91 = (bf16[2,512,384]{2,1,0:T(8,128)(2,1)S(1)}, f32[2,512,384]{2,1,0:T(8,128)S(1)}, f32[8,128]{1,0:T(8,128)S(1)}) custom-call(s32[18]{0:T(128)S(1)} %concatenate.10.refs_0_, bf16[1024,1024]{1,0:T(8,128)(2,1)S(1)} %collective-permute-done.refs_3_.refs_1_, bf16[1024,384]{1,0:T(8,128)(2,1)S(1)} %collective-permute-done.4.refs_2_, ...), custom_call_target="tpu_custom_call" | custom-call | flops 1 | bytes 1 | tf_op jit(solution)/shard_map/pallas_call | solution.py:63
  24.5 2.6 %collective-permute-done.3.refs_1_ = bf16[2,512,512]{2,1,0:T(8,128)(2,1)S(1)} collective-permute-done((bf16[2,512,512]{2,1,0:T(8,128)(2,1)S(1)}, bf16[2,512,512]{2,1,0:T(8,128)(2,1)S(1)}, u32[]{:S(2)}, u32[]{:S(2)}) %collective-permute-start.3) | collective-permute-done | bytes 1048608 | tf_op jit(solution)/shard_map/ppermute | solution.py:449
  27.3 3.2 %collective-permute-start.6 = (bf16[2,256,512]{2,1,0:T(8,128)(2,1)S(1)}, bf16[2,256,512]{2,1,0:T(8,128)(2,1)S(1)}, u32[]{:S(2)}, u32[]{:S(2)}) collective-permute-start(bf16[2,256,512]{2,1,0:T(8,128)(2,1)S(1)} %get-tuple-element.94), channel_id=1, source_target_pairs={{0,6},{1,3},{2,4},{3,1},{4,2},{5,7},{6,0},{7,5},{8,14},{9,11},{10,... | collective-permute-start | bytes 1572872 | tf_op jit(solution)/shard_map/ppermute | solution.py:449
  30.5 11.5 %collective-permute-done.7.refs_1_ = bf16[2,512,384]{2,1,0:T(8,128)(2,1)S(1)} collective-permute-done((bf16[2,512,384]{2,1,0:T(8,128)(2,1)S(1)}, bf16[2,512,384]{2,1,0:T(8,128)(2,1)S(1)}, u32[]{:S(2)}, u32[]{:S(2)}) %collective-permute-start.7) | collective-permute-done | bytes 786464 | tf_op jit(solution)/shard_map/ppermute | solution.py:449
  42.2 1.8 %collective-permute-start.9 = (bf16[2,256,384]{2,1,0:T(8,128)(2,1)S(1)}, bf16[2,256,384]{2,1,0:T(8,128)(2,1)S(1)}, u32[]{:S(2)}, u32[]{:S(2)}) collective-permute-start(bf16[2,256,384]{2,1,0:T(8,128)(2,1)S(1)} %get-tuple-element.101), channel_id=1, source_target_pairs={{0,6},{1,3},{2,4},{3,1},{4,2},{5,7},{6,0},{7,5},{8,14},{9,11},{10,... | collective-permute-start | bytes 1179656 | tf_op jit(solution)/shard_map/ppermute | solution.py:449
  44.2 1.6 %collective-permute-start.8 = (bf16[256,512]{1,0:T(8,128)(2,1)S(1)}, bf16[256,512]{1,0:T(8,128)(2,1)S(1)}, u32[]{:S(2)}, u32[]{:S(2)}) collective-permute-start(bf16[256,512]{1,0:T(8,128)(2,1)S(1)} %get-tuple-element.99.refs_0_), channel_id=1, source_target_pairs={{0,6},{1,3},{2,4},{3,1},{4,2},{5,7},{6,0},{7,5},{8,14},{9,11},{10,... | collective-permute-start | bytes 786440 | tf_op jit(solution)/shard_map/ppermute | solution.py:449
  45.8 0.5 slice.46
  46.9 4.3 %collective-permute-done.9.refs_1_ = bf16[2,256,384]{2,1,0:T(8,128)(2,1)S(1)} collective-permute-done((bf16[2,256,384]{2,1,0:T(8,128)(2,1)S(1)}, bf16[2,256,384]{2,1,0:T(8,128)(2,1)S(1)}, u32[]{:S(2)}, u32[]{:S(2)}) %collective-permute-start.9) | collective-permute-done | bytes 393248 | tf_op jit(solution)/shard_map/ppermute | solution.py:449
  51.4 1.8 %collective-permute-start.11 = (bf16[256,384]{1,0:T(8,128)(2,1)S(1)}, bf16[256,384]{1,0:T(8,128)(2,1)S(1)}, u32[]{:S(2)}, u32[]{:S(2)}) collective-permute-start(bf16[256,384]{1,0:T(8,128)(2,1)S(1)} %get-tuple-element.105.refs_0_), channel_id=1, source_target_pairs={{0,6},{1,3},{2,4},{3,1},{4,2},{5,7},{6,0},{7,5},{8,14},{9,11},{10,... | collective-permute-start | bytes 589832 | tf_op jit(solution)/shard_map/ppermute | solution.py:449
  53.2 0.8 collective-permute-done.8.refs_1_
  54.2 6.3 %collective-permute-done.11.refs_1_ = bf16[256,384]{1,0:T(8,128)(2,1)S(1)} collective-permute-done((bf16[256,384]{1,0:T(8,128)(2,1)S(1)}, bf16[256,384]{1,0:T(8,128)(2,1)S(1)}, u32[]{:S(2)}, u32[]{:S(2)}) %collective-permute-start.11) | collective-permute-done | bytes 196640 | tf_op jit(solution)/shard_map/ppermute | solution.py:449
  60.6 2.8 %collective-permute-done.10.refs_1_ = bf16[512,512]{1,0:T(8,128)(2,1)S(1)} collective-permute-done((bf16[512,512]{1,0:T(8,128)(2,1)S(1)}, bf16[512,512]{1,0:T(8,128)(2,1)S(1)}, u32[]{:S(2)}, u32[]{:S(2)}) %collective-permute-start.10) | collective-permute-done | bytes 524320 | tf_op jit(solution)/shard_map/ppermute | solution.py:449
  63.5 0.5 collective-permute-start.12
  63.9 4.5 %collective-permute-done.13.refs_1_ = bf16[512,384]{1,0:T(8,128)(2,1)S(1)} collective-permute-done((bf16[512,384]{1,0:T(8,128)(2,1)S(1)}, bf16[512,384]{1,0:T(8,128)(2,1)S(1)}, u32[]{:S(2)}, u32[]{:S(2)}) %collective-permute-start.13) | collective-permute-done | bytes 393248 | tf_op jit(solution)/shard_map/ppermute | solution.py:449
  68.4 0.7 shard_map.99
  69.4 0.5 convert_reduce_fusion
  70.0 1.9 %compare_select_fusion = (s32[1024]{0:T(1024)S(1)}, s32[1024]{0:T(1024)S(1)}, s32[1024]{0:T(1024)S(1)}) fusion(s32[1024]{0:T(1024)S(1)} %select_reduce_fusion, s32[]{:T(128)} %bitcast.11, s32[1024]{0:T(1024)S(1)} %convert_reduce_fusion, s32[]{:T(128)} %bitcast.10, s32[]{:T(128)} %bitcast.9), kind=kLoop, calls=%fused_computation.25 | loop fusion | flops 14336 | bytes 20492 | tf_op jit(solution)/shard_map/jit(_where)/select_n | solution.py:441
  71.9 2.4 %shard_map.100 = (bf16[256,1792]{1,0:T(8,128)(2,1)S(1)}, f32[8,128]{1,0:T(8,128)S(1)}) custom-call(s32[18]{0:T(128)S(1)} %copy-done.15, s32[1,1024]{1,0:T(1,128)S(1)} %bitcast.23, s32[1,1024]{1,0:T(1,128)S(1)} %bitcast.24, bf16[1024,512]{1,0:T(8,128)(2,1)S(1)} %get-tuple-element.108.refs_3_.refs_2_, ...), custom_call_target="tpu_custom_call" | custom-call | flops 1 | bytes 1 | tf_op jit(solution)/shard_map/pallas_call | solution.py:63
  74.3 0.9 copy-done.6
  75.1 0.9 copy-done.13
  76.1 7.9 %all-to-all-start = ((bf16[16,16,1792]{2,1,0:T(8,128)(2,1)}), bf16[16,16,1792]{2,1,0:T(8,128)(2,1)S(1)}, u32[]{:S(2)}, u32[]{:S(2)}) async-start(bf16[16,16,1792]{2,1,0:T(8,128)(2,1)} %bitcast.22), calls=%async_computation | async-start | bytes 1835008 | tf_op jit(solution)/shard_map/all_to_all | solution.py:489
  84.2 2.0 %copy-done.5 = bf16[1792,1024]{1,0:T(8,128)(2,1)S(1)} copy-done((bf16[1792,1024]{1,0:T(8,128)(2,1)S(1)}, bf16[1792,1024]{1,0:T(8,128)(2,1)}, u32[]{:S(2)}) %copy-start.5) | copy-done | bytes 3670040
  86.2 1.1 copy-done.7
  87.4 1.1 copy-done.9
  88.5 5.5 %shard_map.101 = (f32[1024,1024]{1,0:T(8,128)S(1)}, f32[8,128]{1,0:T(8,128)}) custom-call(s32[18]{0:T(128)S(1)} %copy-done.15, bf16[1792,1024]{1,0:T(8,128)(2,1)S(1)} %copy-done.5, bf16[1024,512]{1,0:T(8,128)(2,1)S(1)} %get-tuple-element.108.refs_3_.refs_2_, bf16[1024,512]{1,0:T(8,128)(2,1)S(1)} %collective-permute-done.12.refs_4_.refs_3_, ...), custom_call_target="tpu_custom_call" | custom-call | flops 1 | bytes 1 | tf_op jit(solution)/shard_map/pallas_call | solution.py:63
  94.0 1.8 %shard_map.102 = (bf16[512,512]{1,0:T(8,128)(2,1)}, f32[512,512]{1,0:T(8,128)S(1)}, bf16[512,512]{1,0:T(8,128)(2,1)}, f32[512,512]{1,0:T(8,128)S(1)}, f32[8,128]{1,0:T(8,128)S(1)}) custom-call(s32[64]{0:T(128)S(1)} %pad_add_fusion.refs_0_, f32[1024,1024]{1,0:T(8,128)S(1)} %get-tuple-element.116.refs_1_), custom_call_target="tpu_custom_call" | custom-call | flops 1 | bytes 1 | tf_op jit(solution)/shard_map/pallas_call | solution.py:63
  95.8 1.0 copy-done.11
  96.8 3.1 %collective-permute-start.15 = (bf16[512,512]{1,0:T(8,128)(2,1)}, bf16[512,512]{1,0:T(8,128)(2,1)}, u32[]{:S(2)}, u32[]{:S(2)}) collective-permute-start(bf16[512,512]{1,0:T(8,128)(2,1)} %get-tuple-element.119), channel_id=1, source_target_pairs={{0,96},{1,25},{8,104},{9,17},{16,112},{17,9},{24,120},{25,1},{32,6... | collective-permute-start | bytes 1572872 | tf_op jit(solution)/shard_map/ppermute | solution.py:492
  100.2 0.6 all-to-all-done.refs_0_
  100.9 3.1 %copy-done.4 = bf16[2,28672,64]{1,2,0:T(8,128)(2,1)S(1)} copy-done((bf16[2,28672,64]{1,2,0:T(8,128)(2,1)S(1)}, bf16[2,28672,64]{1,2,0:T(8,128)(2,1)}, u32[]{:S(2)}) %copy-start.4) | copy-done | bytes 7340056
  103.9 2.4 %shard_map.103 = (f32[16,128]{1,0:T(8,128)S(1)}, f32[8,128]{1,0:T(8,128)}) custom-call(bf16[16,16,1792]{2,1,0:T(8,128)(2,1)S(1)} %all-to-all-done.refs_0_, bf16[128,28672]{1,0:T(8,128)(2,1)S(1)} %bitcast.18, f32[8,128]{1,0:T(8,128)S(1)} %get-tuple-element.122.refs_2_), custom_call_target="tpu_custom_call" | custom-call | flops 1 | bytes 1 | tf_op jit(solution)/shard_map/pallas_call | solution.py:63
  106.4 1.1 shard_map.104
  107.5 3.4 %all-to-all-start.1 = ((bf16[8,16,1024]{2,1,0:T(8,128)(2,1)}), bf16[8,16,1024]{2,1,0:T(8,128)(2,1)S(1)}, u32[]{:S(2)}, u32[]{:S(2)}) async-start(bf16[8,16,1024]{2,1,0:T(8,128)(2,1)} %get-tuple-element.124), calls=%async_computation.1 | async-start | bytes 524288 | tf_op jit(solution)/shard_map/all_to_all | solution.py:502
  111.1 7.2 %all-to-all-done.1 = bf16[8,16,1024]{2,1,0:T(8,128)(2,1)S(1)} async-done(((bf16[8,16,1024]{2,1,0:T(8,128)(2,1)}), bf16[8,16,1024]{2,1,0:T(8,128)(2,1)S(1)}, u32[]{:S(2)}, u32[]{:S(2)}) %all-to-all-start.1) | async-done | bytes 262176 | tf_op jit(solution)/shard_map/all_to_all | solution.py:502
  118.4 1.0 collective-permute-start.17
  119.9 2.7 %shard_map.105 = (f32[512,512]{1,0:T(8,128)S(1)}, f32[512,512]{1,0:T(8,128)S(1)}, f32[8,128]{1,0:T(8,128)}) custom-call(s32[64]{0:T(128)S(1)} %pad_add_fusion.refs_0_, f32[512,512]{1,0:T(8,128)S(1)} %get-tuple-element.117.refs_1_, f32[512,512]{1,0:T(8,128)S(1)} %copy-done.12, bf16[512,512]{1,0:T(8,128)(2,1)} %collective-permute-done.15.refs_3_, ...), custom_call_target="tpu_custom_call" | custom-call | flops 1 | bytes 1 | tf_op jit(solution)/shard_map/pallas_call | solution.py:63
  122.6 2.0 %collective-permute-done.17.refs_5_ = bf16[128,512]{1,0:T(8,128)(2,1)S(1)} collective-permute-done((bf16[128,512]{1,0:T(8,128)(2,1)S(1)}, bf16[128,512]{1,0:T(8,128)(2,1)S(1)}, u32[]{:S(2)}, u32[]{:S(2)}) %collective-permute-start.17) | collective-permute-done | bytes 131104 | tf_op jit(solution)/shard_map/ppermute | solution.py:492
  124.6 1.5 %shard_map.106 = (bf16[256,512]{1,0:T(8,128)(2,1)S(1)}, f32[256,512]{1,0:T(8,128)S(1)}, bf16[256,512]{1,0:T(8,128)(2,1)S(1)}, f32[256,512]{1,0:T(8,128)S(1)}, f32[8,128]{1,0:T(8,128)}) custom-call(s32[64]{0:T(128)S(1)} %pad_add_fusion.refs_0_, f32[512,512]{1,0:T(8,128)S(1)} %get-tuple-element.125.refs_1_, f32[512,512]{1,0:T(8,128)S(1)} %get-tuple-element.126.refs_2_, ...), custom_call_target="tpu_custom_call" | custom-call | flops 1 | bytes 1 | tf_op jit(solution)/shard_map/pallas_call | solution.py:63
  126.1 2.0 %collective-permute-start.22 = (bf16[256,512]{1,0:T(8,128)(2,1)S(1)}, bf16[256,512]{1,0:T(8,128)(2,1)S(1)}, u32[]{:S(2)}, u32[]{:S(2)}) collective-permute-start(bf16[256,512]{1,0:T(8,128)(2,1)S(1)} %get-tuple-element.130), channel_id=1, source_target_pairs={{0,96},{1,25},{8,104},{9,17},{16,112},{17,9},{24,120},{25,1},{32,6... | collective-permute-start | bytes 786440 | tf_op jit(solution)/shard_map/ppermute | solution.py:492
  128.1 5.6 %collective-permute-done.22 = bf16[256,512]{1,0:T(8,128)(2,1)S(1)} collective-permute-done((bf16[256,512]{1,0:T(8,128)(2,1)S(1)}, bf16[256,512]{1,0:T(8,128)(2,1)S(1)}, u32[]{:S(2)}, u32[]{:S(2)}) %collective-permute-start.22) | collective-permute-done | bytes 262176 | tf_op jit(solution)/shard_map/ppermute | solution.py:492
  133.8 1.3 collective-permute-start.23
  135.2 2.0 %collective-permute-start.20 = (bf16[128,512]{1,0:T(8,128)(2,1)S(1)}, bf16[128,512]{1,0:T(8,128)(2,1)S(1)}, u32[]{:S(2)}, u32[]{:S(2)}) collective-permute-start(bf16[128,512]{1,0:T(8,128)(2,1)S(1)} %slice.83), channel_id=1, source_target_pairs={{0,24},{1,97},{8,16},{9,105},{16,8},{17,113},{24,0},{25,121},{32,5... | collective-permute-start | bytes 393224 | tf_op jit(solution)/shard_map/ppermute | solution.py:492
  137.2 1.6 %collective-permute-done.23 = bf16[128,512]{1,0:T(8,128)(2,1)S(1)} collective-permute-done((bf16[128,512]{1,0:T(8,128)(2,1)S(1)}, bf16[128,512]{1,0:T(8,128)(2,1)S(1)}, u32[]{:S(2)}, u32[]{:S(2)}) %collective-permute-start.23) | collective-permute-done | bytes 131104 | tf_op jit(solution)/shard_map/ppermute | solution.py:492
  138.9 2.1 %collective-permute-start.24 = (bf16[64,512]{1,0:T(8,128)(2,1)S(1)}, bf16[64,512]{1,0:T(8,128)(2,1)S(1)}, u32[]{:S(2)}, u32[]{:S(2)}) collective-permute-start(bf16[64,512]{1,0:T(8,128)(2,1)S(1)} %slice.84), channel_id=1, source_target_pairs={{0,24},{1,97},{8,16},{9,105},{16,8},{17,113},{24,0},{25,121},{32,5... | collective-permute-start | bytes 196616 | tf_op jit(solution)/shard_map/ppermute | solution.py:492
  141.0 0.5 collective-permute-done.20
  141.7 2.7 %collective-permute-done.24 = bf16[64,512]{1,0:T(8,128)(2,1)S(1)} collective-permute-done((bf16[64,512]{1,0:T(8,128)(2,1)S(1)}, bf16[64,512]{1,0:T(8,128)(2,1)S(1)}, u32[]{:S(2)}, u32[]{:S(2)}) %collective-permute-start.24) | collective-permute-done | bytes 65568 | tf_op jit(solution)/shard_map/ppermute | solution.py:492
  144.5 1.4 collective-permute-done.21
  145.9 0.7 pad_maximum_fusion
  (80 shorter events, 4.1 us)
Async XLA Ops:
  0.4 21.1 %copy-start.14 = (s32[18]{0:T(128)}, s32[18]{0:T(128)S(1)}, u32[]{:S(2)}) copy-start(s32[18]{0:T(128)S(1)} %concatenate.10.refs_0_) | copy-start | bytes 220
  0.4 5.5 %collective-permute-start = (bf16[1024,1024]{1,0:T(8,128)(2,1)}, bf16[1024,1024]{1,0:T(8,128)(2,1)S(1)}, u32[]{:S(2)}, u32[]{:S(2)}) collective-permute-start(bf16[1024,1024]{1,0:T(8,128)(2,1)} %refs_1_.8), channel_id=1, source_target_pairs={{0,1},{1,0},{2,3},{3,2},{4,5},{5,4},{6,7},{7,6},{8,9},{9,8},{10,11... | collective-permute-start | bytes 6291464 | tf_op jit(solution)/shard_map/ppermute | solution.py:449
  0.4 2.0 %copy-start = (bf16[1024,1792]{1,0:T(8,128)(2,1)S(1)}, bf16[1024,1792]{1,0:T(8,128)(2,1)}, u32[]{:S(2)}) copy-start(bf16[1024,1792]{1,0:T(8,128)(2,1)} %refs_2_.2) | copy-start | bytes 11010052
  2.4 1.6 %copy-start.3 = (bf16[1024,1024]{1,0:T(8,128)(2,1)S(1)}, bf16[1024,1024]{1,0:T(8,128)(2,1)}, u32[]{:S(2)}) copy-start(bf16[1024,1024]{1,0:T(8,128)(2,1)} %refs_1_.8) | copy-start | bytes 6291460
  3.1 2.7 %copy-start.2 = (bf16[1024,1792]{1,0:T(8,128)(2,1)S(1)}, bf16[1024,1792]{1,0:T(8,128)(2,1)}, u32[]{:S(2)}) copy-start(bf16[1024,1792]{1,0:T(8,128)(2,1)} %refs_2_.3) | copy-start | bytes 11010052
  3.1 5.8 %collective-permute-start.1 = (bf16[1024,512]{1,0:T(8,128)(2,1)S(1)}, bf16[1024,512]{1,0:T(8,128)(2,1)S(1)}, u32[]{:S(2)}, u32[]{:S(2)}) collective-permute-start(bf16[1024,512]{1,0:T(8,128)(2,1)S(1)} %get-tuple-element.72), channel_id=1, source_target_pairs={{0,1},{1,0},{2,3},{3,2},{4,5},{5,4},{6,7},{7,6},{8,9},{9,8},{10,11... | collective-permute-start | bytes 3145736 | tf_op jit(solution)/shard_map/ppermute | solution.py:449
  6.5 2.9 %collective-permute-start.2 = (bf16[1024,512]{1,0:T(8,128)(2,1)S(1)}, bf16[1024,512]{1,0:T(8,128)(2,1)S(1)}, u32[]{:S(2)}, u32[]{:S(2)}) collective-permute-start(bf16[1024,512]{1,0:T(8,128)(2,1)S(1)} %get-tuple-element.76), channel_id=1, source_target_pairs={{0,1},{1,0},{2,3},{3,2},{4,5},{5,4},{6,7},{7,6},{8,9},{9,8},{10,11... | collective-permute-start | bytes 3145736 | tf_op jit(solution)/shard_map/ppermute | solution.py:449
  9.4 4.6 %copy-start.1 = (bf16[1024,1792]{1,0:T(8,128)(2,1)S(1)}, bf16[1024,1792]{1,0:T(8,128)(2,1)}, u32[]{:S(2)}) copy-start(bf16[1024,1792]{1,0:T(8,128)(2,1)} %refs_2_.2) | copy-start | bytes 11010052
  12.3 14.9 %collective-permute-start.3 = (bf16[2,512,512]{2,1,0:T(8,128)(2,1)S(1)}, bf16[2,512,512]{2,1,0:T(8,128)(2,1)S(1)}, u32[]{:S(2)}, u32[]{:S(2)}) collective-permute-start(bf16[2,512,512]{2,1,0:T(8,128)(2,1)S(1)} %get-tuple-element.82), channel_id=1, source_target_pairs={{0,2},{1,7},{2,0},{3,5},{4,6},{5,3},{6,4},{7,1},{8,10},{9,15},{10,... | collective-permute-start | bytes 3145736 | tf_op jit(solution)/shard_map/ppermute | solution.py:449
  14.7 6.7 %collective-permute-start.4 = (bf16[1024,384]{1,0:T(8,128)(2,1)S(1)}, bf16[1024,384]{1,0:T(8,128)(2,1)S(1)}, u32[]{:S(2)}, u32[]{:S(2)}) collective-permute-start(bf16[1024,384]{1,0:T(8,128)(2,1)S(1)} %get-tuple-element.84), channel_id=1, source_target_pairs={{0,1},{1,0},{2,3},{3,2},{4,5},{5,4},{6,7},{7,6},{8,9},{9,8},{10,11... | collective-permute-start | bytes 2359304 | tf_op jit(solution)/shard_map/ppermute | solution.py:449
  18.9 2.6 %collective-permute-start.5 = (bf16[1024,384]{1,0:T(8,128)(2,1)S(1)}, bf16[1024,384]{1,0:T(8,128)(2,1)S(1)}, u32[]{:S(2)}, u32[]{:S(2)}) collective-permute-start(bf16[1024,384]{1,0:T(8,128)(2,1)S(1)} %get-tuple-element.87), channel_id=1, source_target_pairs={{0,1},{1,0},{2,3},{3,2},{4,5},{5,4},{6,7},{7,6},{8,9},{9,8},{10,11... | collective-permute-start | bytes 2359304 | tf_op jit(solution)/shard_map/ppermute | solution.py:449
  24.3 17.7 %collective-permute-start.7 = (bf16[2,512,384]{2,1,0:T(8,128)(2,1)S(1)}, bf16[2,512,384]{2,1,0:T(8,128)(2,1)S(1)}, u32[]{:S(2)}, u32[]{:S(2)}) collective-permute-start(bf16[2,512,384]{2,1,0:T(8,128)(2,1)S(1)} %get-tuple-element.96), channel_id=1, source_target_pairs={{0,2},{1,7},{2,0},{3,5},{4,6},{5,3},{6,4},{7,1},{8,10},{9,15},{10,... | collective-permute-start | bytes 2359304 | tf_op jit(solution)/shard_map/ppermute | solution.py:449
  27.3 16.7 %collective-permute-start.6 = (bf16[2,256,512]{2,1,0:T(8,128)(2,1)S(1)}, bf16[2,256,512]{2,1,0:T(8,128)(2,1)S(1)}, u32[]{:S(2)}, u32[]{:S(2)}) collective-permute-start(bf16[2,256,512]{2,1,0:T(8,128)(2,1)S(1)} %get-tuple-element.94), channel_id=1, source_target_pairs={{0,6},{1,3},{2,4},{3,1},{4,2},{5,7},{6,0},{7,5},{8,14},{9,11},{10,... | collective-permute-start | bytes 1572872 | tf_op jit(solution)/shard_map/ppermute | solution.py:449
  42.2 9.1 %collective-permute-start.9 = (bf16[2,256,384]{2,1,0:T(8,128)(2,1)S(1)}, bf16[2,256,384]{2,1,0:T(8,128)(2,1)S(1)}, u32[]{:S(2)}, u32[]{:S(2)}) collective-permute-start(bf16[2,256,384]{2,1,0:T(8,128)(2,1)S(1)} %get-tuple-element.101), channel_id=1, source_target_pairs={{0,6},{1,3},{2,4},{3,1},{4,2},{5,7},{6,0},{7,5},{8,14},{9,11},{10,... | collective-permute-start | bytes 1179656 | tf_op jit(solution)/shard_map/ppermute | solution.py:449
  44.2 9.9 %collective-permute-start.8 = (bf16[256,512]{1,0:T(8,128)(2,1)S(1)}, bf16[256,512]{1,0:T(8,128)(2,1)S(1)}, u32[]{:S(2)}, u32[]{:S(2)}) collective-permute-start(bf16[256,512]{1,0:T(8,128)(2,1)S(1)} %get-tuple-element.99.refs_0_), channel_id=1, source_target_pairs={{0,6},{1,3},{2,4},{3,1},{4,2},{5,7},{6,0},{7,5},{8,14},{9,11},{10,... | collective-permute-start | bytes 786440 | tf_op jit(solution)/shard_map/ppermute | solution.py:449
  51.4 9.1 %collective-permute-start.11 = (bf16[256,384]{1,0:T(8,128)(2,1)S(1)}, bf16[256,384]{1,0:T(8,128)(2,1)S(1)}, u32[]{:S(2)}, u32[]{:S(2)}) collective-permute-start(bf16[256,384]{1,0:T(8,128)(2,1)S(1)} %get-tuple-element.105.refs_0_), channel_id=1, source_target_pairs={{0,6},{1,3},{2,4},{3,1},{4,2},{5,7},{6,0},{7,5},{8,14},{9,11},{10,... | collective-permute-start | bytes 589832 | tf_op jit(solution)/shard_map/ppermute | solution.py:449
  54.1 9.3 %collective-permute-start.10 = (bf16[512,512]{1,0:T(8,128)(2,1)S(1)}, bf16[512,512]{1,0:T(8,128)(2,1)S(1)}, u32[]{:S(2)}, u32[]{:S(2)}) collective-permute-start(bf16[512,512]{1,0:T(8,128)(2,1)S(1)} %get-tuple-element.104.refs_0_), channel_id=1, source_target_pairs={{0,2},{1,7},{2,0},{3,5},{4,6},{5,3},{6,4},{7,1},{8,10},{9,15},{10,... | collective-permute-start | bytes 1572872 | tf_op jit(solution)/shard_map/ppermute | solution.py:449
  60.5 7.9 %collective-permute-start.13 = (bf16[512,384]{1,0:T(8,128)(2,1)S(1)}, bf16[512,384]{1,0:T(8,128)(2,1)S(1)}, u32[]{:S(2)}, u32[]{:S(2)}) collective-permute-start(bf16[512,384]{1,0:T(8,128)(2,1)S(1)} %get-tuple-element.109.refs_0_), channel_id=1, source_target_pairs={{0,2},{1,7},{2,0},{3,5},{4,6},{5,3},{6,4},{7,1},{8,10},{9,15},{10,... | collective-permute-start | bytes 1179656 | tf_op jit(solution)/shard_map/ppermute | solution.py:449
  63.5 8.4 %collective-permute-start.12 = (bf16[1024,512]{1,0:T(8,128)(2,1)S(1)}, bf16[1024,512]{1,0:T(8,128)(2,1)S(1)}, u32[]{:S(2)}, u32[]{:S(2)}) collective-permute-start(bf16[1024,512]{1,0:T(8,128)(2,1)S(1)} %get-tuple-element.108.refs_3_.refs_2_), channel_id=1, source_target_pairs={{0,1},{1,0},{2,3},{3,2},{4,5},{5,4},{6,7},{7,6},{8,9},{9,8},{10,11... | collective-permute-start | bytes 3145736 | tf_op jit(solution)/shard_map/ppermute | solution.py:449
  68.4 0.7 copy-start.16
  68.4 0.7 copy-start.17
  68.4 3.5 %copy-start.15 = (s32[18]{0:T(128)S(1)}, s32[18]{0:T(128)}, u32[]{:S(2)}) copy-start(s32[18]{0:T(128)} %copy-done.14) | copy-start | bytes 220
  69.0 2.8 %collective-permute-start.14 = (bf16[1024,384]{1,0:T(8,128)(2,1)S(1)}, bf16[1024,384]{1,0:T(8,128)(2,1)S(1)}, u32[]{:S(2)}, u32[]{:S(2)}) collective-permute-start(bf16[1024,384]{1,0:T(8,128)(2,1)S(1)} %get-tuple-element.111.refs_5_.refs_4_), channel_id=1, source_target_pairs={{0,1},{1,0},{2,3},{3,2},{4,5},{5,4},{6,7},{7,6},{8,9},{9,8},{10,11... | collective-permute-start | bytes 2359304 | tf_op jit(solution)/shard_map/ppermute | solution.py:449
  71.8 2.4 %copy-start.8 = (bf16[1024,384]{1,0:T(8,128)(2,1)}, bf16[1024,384]{1,0:T(8,128)(2,1)S(1)}, u32[]{:S(2)}) copy-start(bf16[1024,384]{1,0:T(8,128)(2,1)S(1)} %collective-permute-done.14.refs_6_.refs_5_) | copy-start | bytes 2359300
  74.3 0.9 copy-start.6
  75.1 0.9 copy-start.13
  76.1 24.8 %all-to-all-start = ((bf16[16,16,1792]{2,1,0:T(8,128)(2,1)}), bf16[16,16,1792]{2,1,0:T(8,128)(2,1)S(1)}, u32[]{:S(2)}, u32[]{:S(2)}) async-start(bf16[16,16,1792]{2,1,0:T(8,128)(2,1)} %bitcast.22), calls=%async_computation | async-start | bytes 1835008 | tf_op jit(solution)/shard_map/all_to_all | solution.py:489
  84.2 2.0 %copy-start.5 = (bf16[1792,1024]{1,0:T(8,128)(2,1)S(1)}, bf16[1792,1024]{1,0:T(8,128)(2,1)}, u32[]{:S(2)}) copy-start(bf16[1792,1024]{1,0:T(8,128)(2,1)} %refs_1_.9) | copy-start | bytes 11010052
  86.2 1.1 copy-start.7
  87.4 1.1 copy-start.9
  95.8 1.0 copy-start.11
  96.8 23.1 %collective-permute-start.15 = (bf16[512,512]{1,0:T(8,128)(2,1)}, bf16[512,512]{1,0:T(8,128)(2,1)}, u32[]{:S(2)}, u32[]{:S(2)}) collective-permute-start(bf16[512,512]{1,0:T(8,128)(2,1)} %get-tuple-element.119), channel_id=1, source_target_pairs={{0,96},{1,25},{8,104},{9,17},{16,112},{17,9},{24,120},{25,1},{32,6... | collective-permute-start | bytes 1572872 | tf_op jit(solution)/shard_map/ppermute | solution.py:492
  100.0 20.0 %collective-permute-start.16 = (bf16[512,512]{1,0:T(8,128)(2,1)}, bf16[512,512]{1,0:T(8,128)(2,1)}, u32[]{:S(2)}, u32[]{:S(2)}) collective-permute-start(bf16[512,512]{1,0:T(8,128)(2,1)} %get-tuple-element.120), channel_id=1, source_target_pairs={{0,32},{1,9},{8,40},{9,1},{16,48},{17,25},{24,56},{25,17},{32,0},{... | collective-permute-start | bytes 1572872 | tf_op jit(solution)/shard_map/ppermute | solution.py:492
  100.9 3.1 %copy-start.4 = (bf16[2,28672,64]{1,2,0:T(8,128)(2,1)S(1)}, bf16[2,28672,64]{1,2,0:T(8,128)(2,1)}, u32[]{:S(2)}) copy-start(bf16[2,28672,64]{1,2,0:T(8,128)(2,1)} %param.14) | copy-start | bytes 22020100
  103.9 2.4 %copy-start.10 = (bf16[2,64,8192]{2,1,0:T(8,128)(2,1)S(1)}, bf16[2,64,8192]{2,1,0:T(8,128)(2,1)}, u32[]{:S(2)}) copy-start(bf16[2,64,8192]{2,1,0:T(8,128)(2,1)} %param.15) | copy-start | bytes 6291460
  106.4 13.5 %copy-start.12 = (f32[512,512]{1,0:T(8,128)S(1)}, f32[512,512]{1,0:T(8,128)}, u32[]{:S(2)}) copy-start(f32[512,512]{1,0:T(8,128)} %copy-done.11) | copy-start | bytes 3145732
  107.5 10.9 %all-to-all-start.1 = ((bf16[8,16,1024]{2,1,0:T(8,128)(2,1)}), bf16[8,16,1024]{2,1,0:T(8,128)(2,1)S(1)}, u32[]{:S(2)}, u32[]{:S(2)}) async-start(bf16[8,16,1024]{2,1,0:T(8,128)(2,1)} %get-tuple-element.124), calls=%async_computation.1 | async-start | bytes 524288 | tf_op jit(solution)/shard_map/all_to_all | solution.py:502
  118.4 6.3 %collective-permute-start.17 = (bf16[128,512]{1,0:T(8,128)(2,1)S(1)}, bf16[128,512]{1,0:T(8,128)(2,1)S(1)}, u32[]{:S(2)}, u32[]{:S(2)}) collective-permute-start(bf16[128,512]{1,0:T(8,128)(2,1)S(1)} %get-tuple-element.138), channel_id=1, source_target_pairs={{0,96},{1,25},{8,104},{9,17},{16,112},{17,9},{24,120},{25,1},{32,6... | collective-permute-start | bytes 393224 | tf_op jit(solution)/shard_map/ppermute | solution.py:492
  119.4 5.2 %collective-permute-start.18 = (bf16[128,512]{1,0:T(8,128)(2,1)S(1)}, bf16[128,512]{1,0:T(8,128)(2,1)S(1)}, u32[]{:S(2)}, u32[]{:S(2)}) collective-permute-start(bf16[128,512]{1,0:T(8,128)(2,1)S(1)} %get-tuple-element.137), channel_id=1, source_target_pairs={{0,32},{1,9},{8,40},{9,1},{16,48},{17,25},{24,56},{25,17},{32,0},{... | collective-permute-start | bytes 393224 | tf_op jit(solution)/shard_map/ppermute | solution.py:492
  126.1 7.6 %collective-permute-start.22 = (bf16[256,512]{1,0:T(8,128)(2,1)S(1)}, bf16[256,512]{1,0:T(8,128)(2,1)S(1)}, u32[]{:S(2)}, u32[]{:S(2)}) collective-permute-start(bf16[256,512]{1,0:T(8,128)(2,1)S(1)} %get-tuple-element.130), channel_id=1, source_target_pairs={{0,96},{1,25},{8,104},{9,17},{16,112},{17,9},{24,120},{25,1},{32,6... | collective-permute-start | bytes 786440 | tf_op jit(solution)/shard_map/ppermute | solution.py:492
  128.1 7.0 %collective-permute-start.19 = (bf16[256,512]{1,0:T(8,128)(2,1)S(1)}, bf16[256,512]{1,0:T(8,128)(2,1)S(1)}, u32[]{:S(2)}, u32[]{:S(2)}) collective-permute-start(bf16[256,512]{1,0:T(8,128)(2,1)S(1)} %get-tuple-element.128), channel_id=1, source_target_pairs={{0,32},{1,9},{8,40},{9,1},{16,48},{17,25},{24,56},{25,17},{32,0},{... | collective-permute-start | bytes 786440 | tf_op jit(solution)/shard_map/ppermute | solution.py:492
  133.8 5.0 %collective-permute-start.23 = (bf16[128,512]{1,0:T(8,128)(2,1)S(1)}, bf16[128,512]{1,0:T(8,128)(2,1)S(1)}, u32[]{:S(2)}, u32[]{:S(2)}) collective-permute-start(bf16[128,512]{1,0:T(8,128)(2,1)S(1)} %slice.82), channel_id=1, source_target_pairs={{0,8},{1,33},{8,0},{9,41},{16,24},{17,49},{24,16},{25,57},{32,40},... | collective-permute-start | bytes 393224 | tf_op jit(solution)/shard_map/ppermute | solution.py:492
  135.2 6.3 %collective-permute-start.20 = (bf16[128,512]{1,0:T(8,128)(2,1)S(1)}, bf16[128,512]{1,0:T(8,128)(2,1)S(1)}, u32[]{:S(2)}, u32[]{:S(2)}) collective-permute-start(bf16[128,512]{1,0:T(8,128)(2,1)S(1)} %slice.83), channel_id=1, source_target_pairs={{0,24},{1,97},{8,16},{9,105},{16,8},{17,113},{24,0},{25,121},{32,5... | collective-permute-start | bytes 393224 | tf_op jit(solution)/shard_map/ppermute | solution.py:492
  138.9 5.6 %collective-permute-start.24 = (bf16[64,512]{1,0:T(8,128)(2,1)S(1)}, bf16[64,512]{1,0:T(8,128)(2,1)S(1)}, u32[]{:S(2)}, u32[]{:S(2)}) collective-permute-start(bf16[64,512]{1,0:T(8,128)(2,1)S(1)} %slice.84), channel_id=1, source_target_pairs={{0,24},{1,97},{8,16},{9,105},{16,8},{17,113},{24,0},{25,121},{32,5... | collective-permute-start | bytes 196616 | tf_op jit(solution)/shard_map/ppermute | solution.py:492
  141.5 4.3 %collective-permute-start.21 = (bf16[64,512]{1,0:T(8,128)(2,1)S(1)}, bf16[64,512]{1,0:T(8,128)(2,1)S(1)}, u32[]{:S(2)}, u32[]{:S(2)}) collective-permute-start(bf16[64,512]{1,0:T(8,128)(2,1)S(1)} %slice.85), channel_id=1, source_target_pairs={{0,8},{1,33},{8,0},{9,41},{16,24},{17,49},{24,16},{25,57},{32,40},... | collective-permute-start | bytes 196616 | tf_op jit(solution)/shard_map/ppermute | solution.py:492
